TPU v7x, 256 devices: a whole 4x4x8 slice. The times are simulated.
256 devices in a mesh: wide: 16 (over y, x_hi, core), narrow: 16 (over z, x_lo).
Axes of the slice: x: 4 (x_hi: 2, x_lo: 2; x = x_hi * 2 + x_lo), y: 4, z: 8, core: 2. Of those that a mesh axis runs over, the one named last changes fastest.
Arguments:
- sequence_activity: bfloat16 [32, 4096, 256], P('narrow', 'wide'), may hold values from -6 to 6
- couple_activity: bfloat16 [512, 4096, 128], P('wide', 'narrow'), may hold values from -6 to 6
- sequence_valid_flags: int32 [32], replicated, may hold values 0 or 1
- position_valid_flags: int32 [4096], P('wide'), may hold values 0 or 1
- attend_scale_vector: float32 [256], replicated, may hold values from 0.1 to 1.9
- asking_matrix: bfloat16 [256, 256], replicated, may hold values from -10 to 10
- lookup_matrix: bfloat16 [256, 256], replicated, may hold values from -0.375 to 0.375
- content_matrix: bfloat16 [256, 256], replicated, may hold values from -0.375 to 0.375
- sigmoid_matrix: bfloat16 [256, 256], replicated, may hold values from -0.375 to 0.375
- attend_final_matrix: bfloat16 [256, 256], replicated, may hold values from -0.375 to 0.375
- couple_scale_vector: float32 [128], replicated, may hold values from 0.1 to 1.9
- headwise_additive_matrix: bfloat16 [128, 8], replicated, may hold values from -4 to 4
- product_scale_vector: float32 [256], replicated, may hold values from 0.1 to 1.9
- first_factor_matrix: bfloat16 [256, 32], replicated, may hold values from -0.375 to 0.375
- other_factor_matrix: bfloat16 [256, 32], replicated, may hold values from -0.375 to 0.375
- product_mapping_matrix: bfloat16 [1024, 128], replicated, may hold values from -0.1875 to 0.1875
Outputs:
- fresh_target_sequences: bfloat16 [32, 512, 256], P('narrow', 'wide')
- pair_strip_output: bfloat16 [512, 4096, 128], P('wide', 'narrow')
All inputs are finite; a program needn't handle non-finite values. No bound on the sum of `position_valid_flags` on one device may be relied on, other than what follows from the above.
Results may differ from a plain program's by a relative error of at most 0.012.
The roundings to bfloat16 on the way count: a program that leaves them out, or rounds other values in their place, can miss the bound.
Values may be sent and summed in bfloat16 or wider, within the bound.
No kernel may reach another device: no remote copies, remote signals or barrier semaphores. Data moves between devices by JAX's collectives and lax.ppermute only.
A program may use at most 128 MiB of HBM per device.

v0:
```python
import jax
import jax.numpy as jnp
from jax import lax
from jax.sharding import PartitionSpec as P

HEADS = 8
HEAD = 32
TARGET_STRIDE = 8


def standardize_features(values, gain):
    values = values.astype(jnp.float32)
    center = values - jnp.mean(values, axis=-1, keepdims=True)
    spread = jnp.mean(center * center, axis=-1, keepdims=True)
    return center * lax.rsqrt(spread + 1e-05) * gain


def local(
    sequence_activity,
    couple_activity,
    sequence_valid_flags,
    position_valid_flags,
    attend_scale_vector,
    asking_matrix,
    lookup_matrix,
    content_matrix,
    sigmoid_matrix,
    attend_final_matrix,
    couple_scale_vector,
    headwise_additive_matrix,
    product_scale_vector,
    first_factor_matrix,
    other_factor_matrix,
    product_mapping_matrix,
):
    device_sequences, device_positions, feature_width = sequence_activity.shape
    target_sequences = device_positions // TARGET_STRIDE
    cols_here = couple_activity.shape[1]
    width = first_factor_matrix.shape[1]
    standardized_sequences = standardize_features(sequence_activity, attend_scale_vector).astype(
        jnp.bfloat16
    )
    band_in = standardized_sequences.reshape(
        device_sequences, target_sequences, TARGET_STRIDE, feature_width
    )[:, :, 0]
    query = (
        jnp.dot(band_in, asking_matrix, preferred_element_type=jnp.float32) * HEAD ** (-0.5)
    ).astype(jnp.bfloat16)
    query = query.reshape(device_sequences, target_sequences, HEADS, HEAD)
    gate = jax.nn.sigmoid(jnp.dot(band_in, sigmoid_matrix, preferred_element_type=jnp.float32))
    pair_normed = standardize_features(couple_activity, couple_scale_vector).astype(jnp.bfloat16)
    local_bias = jnp.einsum(
        "rjc,ch->hrj", pair_normed, headwise_additive_matrix, preferred_element_type=jnp.float32
    ).astype(jnp.bfloat16)
    bias_full = lax.all_gather(local_bias, "narrow", axis=2, tiled=True)
    key_mask = position_valid_flags.astype(jnp.bfloat16)[None, :]
    keys = jnp.dot(
        standardized_sequences, lookup_matrix, preferred_element_type=jnp.float32
    ).astype(jnp.bfloat16)
    values = jnp.dot(
        standardized_sequences, content_matrix, preferred_element_type=jnp.float32
    ).astype(jnp.bfloat16)
    accumulate_keys = lax.all_gather(keys, "wide", axis=1, tiled=True)
    accumulate_values = lax.all_gather(values, "wide", axis=1, tiled=True)
    top = jnp.full((device_sequences, HEADS, target_sequences), -1e30, jnp.float32)
    count = accumulate_keys.shape[1]
    accumulate_keys = accumulate_keys.reshape(device_sequences, count, HEADS, HEAD)
    accumulate_values = accumulate_values.reshape(device_sequences, count, HEADS, HEAD)
    scores = jnp.einsum(
        "rqhd,rphd->rhqp", query, accumulate_keys, preferred_element_type=jnp.float32
    )
    bias_piece = bias_full.astype(jnp.float32)
    extra = (
        bias_piece
        + 1000000000.0
        * (lax.all_gather(key_mask, "wide", axis=1, tiled=True)[0].astype(jnp.float32) - 1.0)[
            None, None, :
        ]
    )
    scores = scores + extra[None]
    new_top = jnp.maximum(top, jnp.max(scores, axis=-1))
    expo = jnp.exp(scores - new_top[..., None])
    total = jnp.sum(expo, axis=-1)
    summed = jnp.einsum(
        "rhqp,rphd->rhqd",
        expo.astype(jnp.bfloat16),
        accumulate_values,
        preferred_element_type=jnp.float32,
    )
    state = (new_top, total, summed)
    top, total, summed = state
    attended = (
        (summed / total[..., None])
        .transpose(0, 2, 1, 3)
        .reshape(device_sequences, target_sequences, feature_width)
    )
    gate_applied = (gate * attended).astype(jnp.bfloat16)
    prior_band_slice = sequence_activity.reshape(
        device_sequences, target_sequences, TARGET_STRIDE, feature_width
    )[:, :, 0]
    fresh_target_sequences = (
        prior_band_slice.astype(jnp.float32)
        + jnp.dot(gate_applied, attend_final_matrix, preferred_element_type=jnp.float32)
    ).astype(jnp.bfloat16)
    refreshed_sequences = (
        sequence_activity.reshape(device_sequences, target_sequences, TARGET_STRIDE, feature_width)
        .at[:, :, 0]
        .set(fresh_target_sequences)
        .reshape(device_sequences, device_positions, feature_width)
    )
    normalized_second2 = standardize_features(refreshed_sequences, product_scale_vector).astype(
        jnp.bfloat16
    )
    row_live = lax.dynamic_slice_in_dim(
        sequence_valid_flags, lax.axis_index("narrow") * device_sequences, device_sequences
    ).astype(jnp.float32)
    live = row_live[:, None] * position_valid_flags.astype(jnp.float32)[None, :]
    left = (
        jnp.dot(normalized_second2, first_factor_matrix, preferred_element_type=jnp.float32)
        * live[..., None]
    ).astype(jnp.bfloat16)
    right = (
        jnp.dot(normalized_second2, other_factor_matrix, preferred_element_type=jnp.float32)
        * live[..., None]
    ).astype(jnp.bfloat16)
    left_band = left.reshape(device_sequences, target_sequences, TARGET_STRIDE, width)[:, :, 0]
    left_all, right_rows = (
        lax.all_gather(left_band, "narrow", axis=0, tiled=True),
        lax.all_gather(right, "narrow", axis=0, tiled=True),
    )
    right_every = lax.all_gather(right_rows, "wide", axis=1, tiled=True)
    right_cols = lax.dynamic_slice_in_dim(
        right_every, lax.axis_index("narrow") * cols_here, cols_here, 1
    )
    all_rows = left_all.shape[0]
    nvalid = jnp.sum(sequence_valid_flags.astype(jnp.float32))
    divisor = jnp.maximum(
        nvalid
        * position_valid_flags.reshape(target_sequences, TARGET_STRIDE)[:, 0].astype(jnp.float32),
        1.0,
    )
    blocks = target_sequences // 8
    left_blocks = left_all.reshape(all_rows, blocks, 8, width).transpose(1, 0, 2, 3)
    pair_blocks = couple_activity.reshape(blocks, 8, cols_here, couple_activity.shape[-1])
    divisor_blocks = divisor.reshape(blocks, 8)

    def outer_block(items):
        left_piece, pair_piece, divisor_piece = items
        outer = jnp.einsum(
            "sic,sjd->ijcd", left_piece, right_cols, preferred_element_type=jnp.float32
        ).astype(jnp.bfloat16)
        outer = outer.reshape(8 * cols_here, width * width)
        projected = jnp.dot(
            outer, product_mapping_matrix, preferred_element_type=jnp.float32
        ).reshape(8, cols_here, -1)
        return (pair_piece.astype(jnp.float32) + projected / divisor_piece[:, None, None]).astype(
            jnp.bfloat16
        )

    pair_strip_output = lax.map(outer_block, (left_blocks, pair_blocks, divisor_blocks)).reshape(
        target_sequences, cols_here, couple_activity.shape[-1]
    )
    return (fresh_target_sequences, pair_strip_output)


def solution(mesh):
    in_specs = (
        P("narrow", "wide", None),
        P("wide", "narrow", None),
        P(),
        P("wide"),
        P(),
        P(),
        P(),
        P(),
        P(),
        P(),
        P(),
        P(),
        P(),
        P(),
        P(),
        P(),
    )
    out_specs = (P("narrow", "wide", None), P("wide", "narrow", None))
    return jax.shard_map(local, mesh=mesh, in_specs=in_specs, out_specs=out_specs, check_vma=False)
```

profile of v0, /device:TPU:48, one launch (start us, length us, event | category | flops | bytes accessed | tf_op | source)
XLA Modules:
  0.0 393.7 jit_solution(15073106741071170809)
XLA Ops:
  8.4 2.2 convert_reduce_fusion
  10.6 3.6 fusion.12
  14.3 3.6 fusion.30
  21.3 20.1 %all-gather.2 = bf16[16,1,256]{2,1,0:T(2,128)(2,1)S(1)} all-gather(bf16[1,1,256]{2,1,0:T(2,128)(2,1)S(1)} %reshape.221), channel_id=2, replica_groups=mesh['wide'=16,'narrow'=16] {'wide'}, dimensions={0}, use_global_device_ids=true | all-gather | bytes 8704 | tf_op jit(solution)/shard_map/all_gather | solution.py:76
  41.6 59.9 %all-gather.10.cloned.1.call-done = bf16[8,32,4096]{2,0,1:T(8,128)(2,1)} async-done(((bf16[8,32,256]{2,0,1:T(8,128)(2,1)}), bf16[8,32,4096]{2,0,1:T(8,128)(2,1)}) %all-gather.10.cloned.1.call-update) | async-done | bytes 2097168 | tf_op jit(solution)/shard_map/all_gather | solution.py:55
  103.6 4.4 %copy.56 = f32[8,32,4096]{2,1,0:T(8,128)} copy(f32[8,32,4096]{2,0,1:T(8,128)S(1)} %convert_add_fusion) | data formatting | bytes 8388608 | tf_op jit(solution)/shard_map/add | solution.py:74
  108.0 56.5 %all-gather.8.cloned.1.call-done = bf16[2,4096,256]{2,1,0:T(8,128)(2,1)} async-done(((bf16[2,256,256]{2,1,0:T(8,128)(2,1)}), bf16[2,4096,256]{2,1,0:T(8,128)(2,1)}) %all-gather.8.cloned.1.call-update) | async-done | bytes 4194320 | tf_op jit(solution)/shard_map/all_gather | solution.py:63
  164.4 6.4 %copy.54 = bf16[2,4096,256]{1,2,0:T(8,128)(2,1)} copy(bf16[2,4096,256]{2,1,0:T(8,128)(2,1)} %all-gather.8.cloned.1.call-done) | data formatting | bytes 8388608 | tf_op jit(solution)/shard_map/all_gather | solution.py:63
  170.8 4.9 %add_reduce_fusion = (f32[2,8,32]{2,1,0:T(8,128)S(1)}, f32[2,8,32,4096]{3,2,1,0:T(8,128)S(1)}) fusion(f32[8,32,4096]{2,1,0:T(8,128)} %copy.56, bf16[2,4096,8,32]{1,3,2,0:T(8,128)(2,1)} %bitcast.116, bf16[2,32,8,32]{3,2,1,0:T(8,128)(2,1)S(1)} %reshape.199), kind=kOutput, calls=%fused_computation.13 | convolution fusion | flops 138411520 | bytes 16812032 | tf_op jit(solution)/shard_map/rqhd,rphd->rhqp/dot_general | solution.py:69
  175.7 3.2 copy-done.2
  180.6 45.4 %all-gather.12.cloned.1.call-done = bf16[2,4096,256]{2,1,0:T(8,128)(2,1)} async-done(((bf16[2,256,256]{2,1,0:T(8,128)(2,1)}), bf16[2,4096,256]{2,1,0:T(8,128)(2,1)}) %all-gather.12.cloned.1.call-update) | async-done | bytes 4194320 | tf_op jit(solution)/shard_map/all_gather | solution.py:64
  226.0 6.4 %copy.57 = bf16[2,4096,256]{1,2,0:T(8,128)(2,1)} copy(bf16[2,4096,256]{2,1,0:T(8,128)(2,1)} %all-gather.12.cloned.1.call-done) | data formatting | bytes 8388608 | tf_op jit(solution)/shard_map/all_gather | solution.py:64
  232.4 7.2 %fusion.27 = f32[2,32,8,32]{3,1,2,0:T(8,128)S(1)} fusion(bf16[2,4096,8,32]{1,3,2,0:T(8,128)(2,1)} %bitcast.115, f32[2,8,32,4096]{3,2,1,0:T(8,128)} %copy-done.2, f32[2,8,32]{2,1,0:T(8,128)S(1)} %broadcast_maximum_fusion, f32[8,32,4096]{2,1,0:T(8,128)} %copy.56, f32[2,32,8]{1,2,0:T(8,128)S(1)} %bitcast.123), kind=kOutput, calls=%fused_computation.32 | convolution fusion | flops 140525568 | bytes 16846848 | tf_op jit(solution)/shard_map/rhqp,rphd->rhqd/dot_general | solution.py:84
  243.0 35.7 %all_gather.26 = bf16[32,256,32]{1,2,0:T(8,128)(2,1)} all-gather(bf16[2,256,32]{1,2,0:T(8,128)(2,1)S(1)} %fusion.41), channel_id=1, replica_groups=mesh['wide'=16,'narrow'=16] {'narrow'}, dimensions={0}, use_global_device_ids=true | all-gather | bytes 557056 | tf_op jit(solution)/shard_map/all_gather | solution.py:129
  280.8 31.2 %all-gather.1 = bf16[32,32,1,32]{3,1,2,0:T(8,128)(2,1)S(1)} all-gather(bf16[2,32,1,32]{3,1,2,0:T(8,128)(2,1)S(1)} %copy.61), channel_id=3, replica_groups=mesh['wide'=16,'narrow'=16] {'narrow'}, dimensions={0}, use_global_device_ids=true | all-gather | bytes 69632 | tf_op jit(solution)/shard_map/all_gather | solution.py:128
  312.0 49.1 %all-gather.14.cloned.1.call-done = bf16[32,4096,32]{1,2,0:T(8,128)(2,1)} async-done(((bf16[32,256,32]{1,2,0:T(8,128)(2,1)}), bf16[32,4096,32]{1,2,0:T(8,128)(2,1)}) %all-gather.14.cloned.1.call-update) | async-done | bytes 8388624 | tf_op jit(solution)/shard_map/all_gather | solution.py:131
  362.5 24.7 %while.11 = (s32[]{:T(128)}, bf16[4,8,256,128]{3,2,1,0:T(8,128)(2,1)}, bf16[4,8,256,128]{3,2,1,0:T(8,128)(2,1)S(1)}, bf16[4,32,8,32]{3,2,0,1:T(8,128)(2,1)S(1)},...) while((s32[]{:T(128)}, ...), condition=%wide.region_10.11_spmd, body=%wide.region_9.0_spmd.sunk | while | flops 674234368 | bytes 18694844 | solution.py:160
  363.9 2.6 copy.83
  366.5 2.2 fusion.89
  370.0 2.6 copy.83
  372.7 2.2 fusion.89
  376.2 2.6 copy.83
  378.8 2.2 fusion.89
  382.4 2.6 copy.83
  (101 shorter events, 22.7 us)
Async XLA Ops:
  7.2 11.2 %copy-start = (bf16[256,256]{1,0:T(8,128)(2,1)S(1)}, bf16[256,256]{1,0:T(8,128)(2,1)}, u32[]{:S(2)}) copy-start(bf16[256,256]{1,0:T(8,128)(2,1)} %param.26) | copy-start | bytes 393220
  7.2 7.1 %copy-start.3 = (bf16[32,256,128]{2,1,0:T(8,128)(2,1)S(1)}, bf16[32,256,128]{2,1,0:T(8,128)(2,1)}, u32[]{:S(2)}) copy-start(bf16[32,256,128]{2,1,0:T(8,128)(2,1)} %param.21) | copy-start | bytes 6291460
  7.2 7.1 %copy-start.14 = (f32[128]{0:T(128)S(1)}, f32[128]{0:T(128)}, u32[]{:S(2)}) copy-start(f32[128]{0:T(128)} %param.30) | copy-start | bytes 1540
  7.2 7.1 %copy-start.12 = (bf16[128,8]{0,1:T(8,128)(2,1)S(1)}, bf16[128,8]{0,1:T(8,128)(2,1)}, u32[]{:S(2)}) copy-start(bf16[128,8]{0,1:T(8,128)(2,1)} %param.31) | copy-start | bytes 6148
  7.2 94.3 %all-gather.10.cloned.1.call-start = ((), (), s32[]{:S(2)}) async-start(), calls=%async_computation.1 | async-start | bytes 2228224 | tf_op jit(solution)/shard_map/all_gather | solution.py:55
  10.6 7.8 %copy-start.7 = (f32[256]{0:T(256)S(1)}, f32[256]{0:T(256)}, u32[]{:S(2)}) copy-start(f32[256]{0:T(256)} %param.24) | copy-start | bytes 3076
  10.6 8.9 %copy-start.9 = (bf16[256,256]{1,0:T(8,128)(2,1)S(1)}, bf16[256,256]{1,0:T(8,128)(2,1)}, u32[]{:S(2)}) copy-start(bf16[256,256]{1,0:T(8,128)(2,1)} %param.27) | copy-start | bytes 393220
  14.3 6.6 %copy-start.4 = (bf16[256,256]{1,0:T(8,128)(2,1)S(1)}, bf16[256,256]{1,0:T(8,128)(2,1)}, u32[]{:S(2)}) copy-start(bf16[256,256]{1,0:T(8,128)(2,1)} %param.25) | copy-start | bytes 393220
  14.3 6.9 %copy-start.6 = (s32[256]{0:T(256)S(1)}, s32[256]{0:T(256)}, u32[]{:S(2)}) copy-start(s32[256]{0:T(256)} %param.23) | copy-start | bytes 3076
  14.3 27.1 %copy-start.15 = (s32[32]{0:T(128)S(1)}, s32[32]{0:T(128)}, u32[]{:S(2)}) copy-start(s32[32]{0:T(128)} %param.22) | copy-start | bytes 388
  17.9 146.5 %all-gather.8.cloned.1.call-start = ((), (), s32[]{:S(2)}) async-start(), calls=%async_computation | async-start | bytes 4456448 | tf_op jit(solution)/shard_map/all_gather | solution.py:63
  19.5 206.5 %all-gather.12.cloned.1.call-start = ((), (), s32[]{:S(2)}) async-start(), calls=%async_computation.2 | async-start | bytes 4456448 | tf_op jit(solution)/shard_map/all_gather | solution.py:64
  20.6 340.5 %all-gather.14.cloned.1.call-start = ((), (), s32[]{:S(2)}) async-start(), calls=%async_computation.3 | async-start | bytes 8912896 | tf_op jit(solution)/shard_map/all_gather | solution.py:131
  170.8 8.1 %copy-start.1 = (f32[8,32,4096]{2,1,0:T(8,128)S(1)}, f32[8,32,4096]{2,1,0:T(8,128)}, u32[]{:S(2)}) copy-start(f32[8,32,4096]{2,1,0:T(8,128)} %copy.56) | copy-start | bytes 12582916
  175.7 3.2 copy-start.2
  232.4 10.3 %copy-start.10 = (bf16[256,32]{0,1:T(8,128)(2,1)S(1)}, bf16[256,32]{0,1:T(8,128)(2,1)}, u32[]{:S(2)}) copy-start(bf16[256,32]{0,1:T(8,128)(2,1)} %param.34) | copy-start | bytes 49156
  232.4 10.3 %copy-start.13 = (f32[256]{0:T(256)S(1)}, f32[256]{0:T(256)}, u32[]{:S(2)}) copy-start(f32[256]{0:T(256)} %param.32) | copy-start | bytes 3076
  239.6 40.7 %copy-start.11 = (bf16[256,32]{0,1:T(8,128)(2,1)S(1)}, bf16[256,32]{0,1:T(8,128)(2,1)}, u32[]{:S(2)}) copy-start(bf16[256,32]{0,1:T(8,128)(2,1)} %param.33) | copy-start | bytes 49156
  239.6 122.9 %copy-start.8 = (bf16[1024,128]{1,0:T(8,128)(2,1)S(1)}, bf16[1024,128]{1,0:T(8,128)(2,1)}, u32[]{:S(2)}) copy-start(bf16[1024,128]{1,0:T(8,128)(2,1)} %param.35) | copy-start | bytes 786436
  241.1 121.3 %copy-start.5 = (bf16[2,32,256]{2,1,0:T(8,128)(2,1)}, bf16[2,32,256]{2,1,0:T(8,128)(2,1)S(1)}, u32[]{:S(2)}) copy-start(bf16[2,32,256]{2,1,0:T(8,128)(2,1)S(1)} %fusion.39) | copy-start | bytes 98308
Sparse Core Ops, SparseCore 0:
  18.0 83.4 all-gather.9
  104.2 60.1 all-gather.7
  167.7 58.2 all-gather.11
  278.9 82.1 all-gather.13
where the time goes:
time: 398 us; the launch traced here: 394 us
  waiting for transfers between devices  211 us (53%)
  blocking collectives  87.1 us (22%)
  local copies, waits for them, and re-layouts  35.8 us (9%)
  matrix products  33.4 us (8%)
  between operations  14.2 us (4%)
  other arithmetic  12.1 us (3%)
    all_gather x1, waiting for transfers between devices, local(): bias_full = lax.all_gather(local_bias, 'narrow', axis=2, tiled=True)  59.9 us
    all_gather x1, waiting for transfers between devices, local(): accumulate_keys = lax.all_gather(keys, 'wide', axis=1, tiled=True)  56.5 us
    all_gather x1, waiting for transfers between devices, local(): right_every = lax.all_gather(right_rows, 'wide', axis=1, tiled=True)  49.1 us
    all_gather x1, waiting for transfers between devices, local(): accumulate_values = lax.all_gather(values, 'wide', axis=1, tiled=True)  45.4 us
    all_gather x1, blocking collectives, local(): lax.all_gather(right, 'narrow', axis=0, tiled=True)  35.7 us
    all_gather x1, blocking collectives, local(): lax.all_gather(left_band, 'narrow', axis=0, tiled=True)  31.2 us
    all_gather x1, blocking collectives, local(): lax.all_gather(key_mask, 'wide', axis=1, tiled=True)[0].astype(jnp.float32)  20.1 us
    convert_element_type x4, local copies, waits for them, and re-layouts, outer_block(): outer = jnp.einsum('sic,sjd->ijcd', left_piece, right_cols, preferred_ele...  10.4 us
  transfers between devices with their start and end apart: 4, of which 4 were waited for; matrix products, arithmetic and copies ran while one was open for 6% of the time, Pallas kernels for 0%

commit v1 on v0

v1 whole, which is shorter than its diff:
```python
import jax
import jax.numpy as jnp
from jax import lax
from jax.experimental import pallas as pl
from jax.experimental.pallas import tpu as pltpu
from jax.sharding import Mesh, PartitionSpec as P

EPS = 1e-05
BIG = 1000000000.0
F32 = jnp.float32
BF16 = jnp.bfloat16
VMEM = 48 * 1024 * 1024
ALL = ("q", "c", "z", "x")


def dot(a, b, dims):
    return lax.dot_general(a, b, (dims, ((), ())), preferred_element_type=F32)


NN = ((1,), (0,))
NT = ((1,), (1,))
TN = ((0,), (0,))
TT = ((0,), (1,))


def center_and_scale(values):
    center = values - jnp.mean(values, axis=-1, keepdims=True)
    spread = jnp.mean(center * center, axis=-1, keepdims=True)
    return center * lax.rsqrt(spread + EPS)


def front_kernel(
    pair_ref,
    seq_ref,
    live_ref,
    flags_ref,
    g1_ref,
    ask_ref,
    look_ref,
    cont_ref,
    sig_ref,
    gp_ref,
    head_ref,
    g2_ref,
    other_ref,
    msg_ref,
    gate_ref,
    right_ref,
    bias_scr,
    norm_scr,
):
    step = pl.program_id(0)
    rows = pair_ref.shape[0]

    pair = pair_ref[...].reshape(rows * 256, 128).astype(F32)
    pair = (center_and_scale(pair) * gp_ref[...]).astype(BF16)
    bias = dot(head_ref[...], pair, TT)
    for r in range(rows):
        for i in range(2):
            bias_scr[i, pl.ds(pl.multiple_of((step * rows + r) * 8, 8), 8), :] = bias[
                :, r * 256 + i * 128 : r * 256 + i * 128 + 128
            ]

    @pl.when(step == 0)
    def _():
        base = center_and_scale(seq_ref[...].astype(F32))
        normed = (base * g1_ref[...]).astype(BF16)
        keys = dot(look_ref[...], normed, TT).astype(BF16)
        values = dot(cont_ref[...], normed, TT).astype(BF16)
        for h in range(8):
            for s in range(2):
                cut = (slice(h * 32, h * 32 + 32), slice(s * 256, s * 256 + 256))
                msg_ref[h, 32 + s * 32 : 64 + s * 32, :] = keys[cut]
                msg_ref[h, 96 + s * 32 : 128 + s * 32, :] = values[cut]
        wide = normed.astype(F32)
        for i in range(2):
            norm_scr[i] = wide[:, i * 128 : (i + 1) * 128]
        band = jnp.concatenate(
            [norm_scr[i, pl.ds(0, 64, stride=8), :] for i in range(2)], axis=1
        ).astype(BF16)
        gate_ref[...] = jax.nn.sigmoid(dot(band, sig_ref[...], NN))
        query = (dot(band, ask_ref[...], NN) * 32 ** (-0.5)).astype(BF16).astype(F32)
        flags = flags_ref[...].astype(F32)
        row = lax.broadcasted_iota(jnp.int32, (16, 128), 0)
        mask = jnp.where(row == 0, flags[0:1], jnp.where(row == 1, flags[1:2], 0.0))
        for h in range(8):
            parts = [
                query[s * 32 + g * 16 : s * 32 + g * 16 + 16, h * 32 : h * 32 + 32]
                for g in range(2)
                for s in range(2)
            ]
            msg_ref[h, 160:176, :] = jnp.concatenate(parts + [mask], axis=1).astype(BF16)
        again = (base * g2_ref[...]).astype(BF16)
        right = dot(other_ref[...], again, TT)
        for s in range(2):
            right_ref[s] = (right[:, s * 256 : (s + 1) * 256] * live_ref[s : s + 1, :]).astype(BF16)

    @pl.when(step == pl.num_programs(0) - 1)
    def _():
        for h in range(8):
            for i in range(2):
                msg_ref[h, 0:32, i * 128 : i * 128 + 128] = bias_scr[
                    i, pl.ds(h, 32, stride=8), :
                ].astype(BF16)


def split3(value):
    high = value.astype(BF16).astype(F32)
    rest = value - high
    middle = rest.astype(BF16).astype(F32)
    return high, middle, rest - middle


def attend_kernel(
    place_ref, own_ref, swapped_ref, kva_ref, kvb_ref, bias_ref, x0_ref, x1_ref, out_ref, extra_scr
):
    c, x = place_ref[0], place_ref[1]
    lane = lax.broadcasted_iota(jnp.int32, (128, 128), 1)
    block, inner = lane // 32, lane % 32
    first_x = jnp.where(x == 0, x0_ref[...], x1_ref[...])
    second_x = jnp.where(x == 0, x1_ref[...], x0_ref[...])
    for q in range(8):
        out_ref[q, 0, 16:48, :] = first_x
        out_ref[q, 1, 16:48, :] = second_x
    mask = jnp.concatenate(
        [kva_ref[k, 128 + i : 129 + i, 128:256].astype(F32) for k in range(8) for i in range(2)], axis=1
    )
    penalty = BIG * (mask - 1.0)
    for g in range(2):
        for k in range(8):
            piece = bias_ref[k, :, g * 16 : g * 16 + 16, :].reshape(128, 256).astype(F32)
            extra_scr[g, :, k * 256 : (k + 1) * 256] = piece + penalty[:, k * 256 : (k + 1) * 256]
    own = own_ref[...].reshape(128, 128)
    swapped = swapped_ref[...].reshape(128, 128)
    for a in range(2):
        kv_ref = (kva_ref, kvb_ref)[a]
        half = c ^ a
        query = jnp.where(half == x, own, swapped).astype(F32)
        keys = jnp.concatenate([kv_ref[k, 0:64, :] for k in range(8)], axis=1)
        values = jnp.concatenate([kv_ref[k, 64:128, :] for k in range(8)], axis=1)
        keys = jnp.concatenate([keys, keys], axis=0)
        values = jnp.concatenate([values, values], axis=0)
        mixed = jnp.zeros((128, 128), F32)
        stats = jnp.zeros((128, 128), F32)
        for g in range(2):
            for s in range(2):
                here = block == g * 2 + s
                picked = jnp.where(here, query, 0.0).astype(BF16)
                scores = dot(picked, keys, NN) + extra_scr[g]
                top = jnp.max(scores, axis=1, keepdims=True)
                expo = jnp.exp(scores - top)
                total = jnp.sum(expo, axis=1, keepdims=True)
                part = dot(expo.astype(BF16), values, NT)
                mixed = jnp.where(here, part / total, mixed)
                for t, piece in enumerate(split3(top) + split3(total)):
                    stats = jnp.where(here & (inner == t), piece, stats)
        joined = jnp.concatenate([mixed, stats], axis=1).astype(BF16)
        for q in range(8):
            out_ref[q, half, 0:16, :] = joined[q * 16 : q * 16 + 16]


def refresh_kernel(
    parts_ref, gate_ref, prior_ref, final_ref, g2_ref, first_ref, other_ref, live_ref, fresh_ref, sides_ref
):
    rows = lax.broadcasted_iota(jnp.int32, (128, 128), 0)
    lanes = lax.broadcasted_iota(jnp.int32, (128, 128), 1)
    spread = [jnp.where(rows == (lanes // 32) * 32 + t, 1.0, 0.0).astype(BF16) for t in range(6)]
    tops, totals, mixes = [], [], []
    for x in range(2):
        mixes.append(
            jnp.concatenate([parts_ref[2 * h + x, 0:16, 0:128] for h in range(8)], axis=0).astype(F32)
        )
        stats = jnp.concatenate([parts_ref[2 * h + x, 0:16, 128:256] for h in range(8)], axis=0)
        wide = [dot(stats, spread[t], NN) for t in range(6)]
        tops.append(wide[0] + wide[1] + wide[2])
        totals.append(wide[3] + wide[4] + wide[5])
    top = jnp.maximum(tops[0], tops[1])
    weights = [totals[i] * jnp.exp(tops[i] - top) for i in range(2)]
    attended = (weights[0] * mixes[0] + weights[1] * mixes[1]) / (weights[0] + weights[1])
    lined = []
    for s in range(2):
        for g in range(2):
            cut = (g * 2 + s) * 32
            lined.append(
                jnp.concatenate(
                    [attended[h * 16 : h * 16 + 16, cut : cut + 32] for h in range(8)], axis=1
                )
            )
    attended = jnp.concatenate(lined, axis=0)
    gated = (gate_ref[...] * attended).astype(BF16)
    fresh = (prior_ref[...].astype(F32) + dot(gated, final_ref[...], NN)).astype(BF16)
    fresh_ref[...] = fresh
    again = (center_and_scale(fresh.astype(F32)) * g2_ref[...]).astype(BF16)
    left = dot(again, first_ref[...], NN) * live_ref[...]
    right = dot(again, other_ref[...], NN) * live_ref[...]
    sides_ref[...] = jnp.concatenate(
        [left[0:32], right[0:32], left[32:64], right[32:64]], axis=1
    ).astype(BF16)


def outer_kernel(divisor_ref, right_ref, left_ref, map_ref, pair_ref, out_ref, scr):
    step = pl.program_id(0)
    rows = pair_ref.shape[0]
    for r in range(0, rows, 2):
        mapped = dot(left_ref[r * 32 : (r + 2) * 32, :], map_ref[...], NN).astype(BF16)
        for d in range(32):
            for i in range(2):
                scr[d * 32 : d * 32 + 32, i * 128 : i * 128 + 128] = mapped[
                    i * 32 : i * 32 + 32, d * 128 : d * 128 + 128
                ]
        projected = dot(right_ref[...], scr[...], NN)
        for i in range(2):
            scale = 1.0 / divisor_ref[step * rows + r + i]
            out_ref[r + i] = (
                pair_ref[r + i].astype(F32) + projected[:, i * 128 : (i + 1) * 128] * scale
            ).astype(BF16)


def gather(value, axes, count):
    tiled = jnp.broadcast_to(value[None], (count,) + value.shape)
    return lax.all_to_all(tiled, axes, 0, 0, tiled=True)


def whole(shape):
    return pl.BlockSpec(shape, lambda *_: (0,) * len(shape))


def params():
    return pltpu.CompilerParams(vmem_limit_bytes=VMEM)


MIRROR = [(w * 16 + n, n * 16 + w) for w in range(16) for n in range(16)]
MIRROR_NEXT = [(w * 16 + n, n * 16 + (w ^ 1)) for w in range(16) for n in range(16)]
ACROSS = [(a * 2 + b, b * 2 + a) for a in range(2) for b in range(2)]
ACROSS_NEXT = [(a * 2 + b, (1 - b) * 2 + a) for a in range(2) for b in range(2)]
SWAP = [(0, 1), (1, 0)]


def local(
    sequence_activity,
    couple_activity,
    sequence_valid_flags,
    position_valid_flags,
    attend_scale_vector,
    asking_matrix,
    lookup_matrix,
    content_matrix,
    sigmoid_matrix,
    attend_final_matrix,
    couple_scale_vector,
    headwise_additive_matrix,
    product_scale_vector,
    first_factor_matrix,
    other_factor_matrix,
    product_mapping_matrix,
):
    c, z, x = lax.axis_index("c"), lax.axis_index("z"), lax.axis_index("x")
    row_live = lax.dynamic_slice_in_dim(sequence_valid_flags, (z * 2 + x) * 2, 2).astype(F32)
    positions = position_valid_flags.astype(F32)
    live = row_live[:, None] * positions[None, :]
    live_band = live.reshape(2, 32, 8)[:, :, 0].reshape(64, 1)
    prior = sequence_activity.reshape(64, 8, 256)[:, 0]
    g2 = product_scale_vector.reshape(1, 256)

    seq = sequence_activity.reshape(512, 256)
    message, gate, right = pl.pallas_call(
        front_kernel,
        grid=(4,),
        in_specs=[pl.BlockSpec((8, 256, 128), lambda i: (i, 0, 0))]
        + [
            whole(s)
            for s in (
                (512, 256),
                (2, 256),
                (2, 128),
                (1, 256),
                (256, 256),
                (256, 256),
                (256, 256),
                (256, 256),
                (1, 128),
                (128, 8),
                (1, 256),
                (256, 32),
            )
        ],
        out_specs=[whole((8, 176, 256)), whole((64, 256)), whole((2, 32, 256))],
        out_shape=[
            jax.ShapeDtypeStruct((8, 176, 256), BF16),
            jax.ShapeDtypeStruct((64, 256), F32),
            jax.ShapeDtypeStruct((2, 32, 256), BF16),
        ],
        scratch_shapes=[pltpu.VMEM((2, 256, 128), F32), pltpu.VMEM((2, 512, 128), F32)],
        compiler_params=params(),
    )(
        couple_activity,
        seq,
        live,
        position_valid_flags.reshape(2, 128),
        attend_scale_vector.reshape(1, 256),
        asking_matrix,
        lookup_matrix,
        content_matrix,
        sigmoid_matrix,
        couple_scale_vector.reshape(1, 128),
        headwise_additive_matrix,
        g2,
        other_factor_matrix,
    )

    heads = lax.all_to_all(message, "q", 0, 0, tiled=True)
    kv = heads[:, 32:176, :]
    own = heads[:, 160:176, 0:128]
    kva = lax.ppermute(kv, ("c", "x"), ACROSS)
    kvb = lax.ppermute(kv, ("c", "x"), ACROSS_NEXT)
    swapped = lax.ppermute(own, "x", SWAP)
    x0 = lax.ppermute(jnp.where(c == 0, right[0], right[1]), ALL, MIRROR)
    x1 = lax.ppermute(jnp.where(c == 0, right[1], right[0]), ALL, MIRROR_NEXT)
    bias = gather(heads[:, 0:32, :], "z", 8)

    parts = pl.pallas_call(
        attend_kernel,
        in_specs=[pl.BlockSpec(memory_space=pltpu.SMEM)] + [pl.BlockSpec(memory_space=pltpu.VMEM)] * 7,
        out_specs=pl.BlockSpec(memory_space=pltpu.VMEM),
        out_shape=jax.ShapeDtypeStruct((8, 2, 48, 256), BF16),
        scratch_shapes=[pltpu.VMEM((2, 128, 2048), F32)],
        compiler_params=params(),
    )(jnp.stack([c, x]).astype(jnp.int32), own, swapped, kva, kvb, bias, x0, x1)

    parts = lax.all_to_all(parts.reshape(16, 48, 256), ("q", "x"), 0, 0, tiled=True)
    mine = parts[:, 16:48, :]
    theirs = lax.ppermute(mine, "c", SWAP)

    fresh, sides = pl.pallas_call(
        refresh_kernel,
        in_specs=[pl.BlockSpec(memory_space=pltpu.VMEM)] * 8,
        out_specs=[pl.BlockSpec(memory_space=pltpu.VMEM)] * 2,
        out_shape=[jax.ShapeDtypeStruct((64, 256), BF16), jax.ShapeDtypeStruct((32, 128), BF16)],
        compiler_params=params(),
    )(parts, gate, prior, attend_final_matrix, g2, first_factor_matrix, other_factor_matrix, live_band)

    sides = gather(sides, ("z", "x"), 16).reshape(16, 32, 2, 2, 32)
    left = sides[:, :, :, 0].transpose(1, 0, 2, 3).reshape(1024, 32)
    right_band = lax.ppermute(sides[:, :, :, 1], ALL, MIRROR)
    right_band = right_band.transpose(1, 3, 0, 2).reshape(32, 1, 1024)
    even, odd = jnp.where(c == 0, mine, theirs), jnp.where(c == 0, theirs, mine)
    factors = jnp.stack([even.reshape(8, 2, 32, 256), odd.reshape(8, 2, 32, 256)], axis=1)
    factors = factors.transpose(4, 3, 0, 1, 2).reshape(32, 8, 1024)
    slot = lax.broadcasted_iota(jnp.int32, (1, 8, 1), 1)
    factors = jnp.where(slot == 0, right_band, factors).reshape(256, 1024)

    nvalid = jnp.sum(sequence_valid_flags.astype(F32))
    divisor = jnp.maximum(nvalid * positions.reshape(32, 8)[:, 0], 1.0)
    mapping = product_mapping_matrix.reshape(32, 4096)
    pair_out = pl.pallas_call(
        outer_kernel,
        grid=(4,),
        in_specs=[
            pl.BlockSpec(memory_space=pltpu.SMEM),
            whole((256, 1024)),
            pl.BlockSpec((256, 32), lambda i: (i, 0)),
            whole((32, 4096)),
            pl.BlockSpec((8, 256, 128), lambda i: (i, 0, 0)),
        ],
        out_specs=pl.BlockSpec((8, 256, 128), lambda i: (i, 0, 0)),
        out_shape=jax.ShapeDtypeStruct((32, 256, 128), BF16),
        scratch_shapes=[pltpu.VMEM((1024, 256), BF16)],
        compiler_params=params(),
    )(divisor, factors, left, mapping, couple_activity)
    return fresh.reshape(2, 32, 256), pair_out


def solution(mesh):
    mesh = Mesh(mesh.devices.reshape(8, 2, 8, 2), ALL)
    wide, narrow = ("q", "c"), ("z", "x")
    in_specs = (P(narrow, wide, None), P(wide, narrow, None), P(), P(wide)) + (P(),) * 12
    out_specs = (P(narrow, wide, None), P(wide, narrow, None))
    return jax.shard_map(local, mesh=mesh, in_specs=in_specs, out_specs=out_specs, check_vma=False)
```

time: 398 us -> 154 us (0.39)
  the two profiles are of different devices: /device:TPU:48 before, /device:TPU:68 now
where the time goes in v1:
time: 154 us; the launch traced here: 153 us
  waiting for transfers between devices  52.2 us (34%)
  starting transfers between devices  37.8 us (25%)
  local copies, waits for them, and re-layouts  20.7 us (13%)
  Pallas kernels  19.1 us (12%)
  blocking collectives  18.3 us (12%)
  other arithmetic  4.35 us (3%)
    ppermute x1, waiting for transfers between devices, local(): right_band = lax.ppermute(sides[:, :, :, 1], ALL, MIRROR)  26.6 us
    all_to_all x1, blocking collectives, local(): heads = lax.all_to_all(message, 'q', 0, 0, tiled=True)  18.3 us
    all_to_all x2, starting transfers between devices, gather(): return lax.all_to_all(tiled, axes, 0, 0, tiled=True)  14.9 us
    ppermute x1, waiting for transfers between devices, local(): x0 = lax.ppermute(jnp.where(c == 0, right[0], right[1]), ALL, MIRROR)  11.7 us
    unnamed x37, local copies, waits for them, and re-layouts  10.7 us
    pallas_call x1, Pallas kernels, local(): pl.pallas_call(outer_kernel, grid=(4,), in_specs=[pl.BlockSpec(memory_spa...  8.58 us
    all_to_all x1, starting transfers between devices, local(): lax.all_to_all(parts.reshape(16, 48, 256), ('q', 'x'), 0, 0, tiled=True)  7.66 us
    all_to_all x2, waiting for transfers between devices, gather(): return lax.all_to_all(tiled, axes, 0, 0, tiled=True)  7.12 us
  transfers between devices with their start and end apart: 10, of which 5 were waited for; matrix products, arithmetic and copies ran while one was open for 6% of the time, Pallas kernels for 0%

profile of v1, /device:TPU:68, one launch (start us, length us, event | category | flops | bytes accessed | tf_op | source)
XLA Modules:
  0.0 153.3 jit_solution(16430378806862785056)
XLA Ops:
  3.8 1.6 %copy-done = bf16[32,256,128]{2,1,0:T(8,128)(2,1)S(1)} copy-done((bf16[32,256,128]{2,1,0:T(8,128)(2,1)S(1)}, bf16[32,256,128]{2,1,0:T(8,128)(2,1)}, u32[]{:S(2)}) %copy-start) | copy-done | bytes 2097176
  12.6 3.9 %shard_map.167 = (bf16[8,176,256]{2,1,0:T(8,128)(2,1)S(1)}, f32[64,256]{1,0:T(8,128)S(1)}, bf16[2,32,256]{2,1,0:T(8,128)(2,1)S(1)}) custom-call(bf16[32,256,128]{2,1,0:T(8,128)(2,1)S(1)} %copy-done, bf16[512,256]{1,0:T(8,128)(2,1)S(1)} %bitcast.40, f32[2,256]{1,0:T(2,128)S(1)} %broadcast_multiply_fusion.live_ref, s32[2,128]{1,0:T(2,128)S(1)} %bitcast.44, ...), custom_call_target="tpu_custom_call" | custom-call | tf_op jit(solution)/shard_map/pallas_call | solution.py:266
  16.5 18.3 %all_to_all.20 = bf16[8,176,256]{2,1,0:T(8,128)(2,1)S(1)} all-to-all(bf16[8,176,256]{2,1,0:T(8,128)(2,1)S(1)} %get-tuple-element.7), channel_id=1, replica_groups=mesh['q'=8,'c'=2,'z'=8,'x'=2] {'q'}, dimensions={0} | all-to-all | bytes 1441792 | tf_op jit(solution)/shard_map/all_to_all | solution.py:311
  34.8 1.1 broadcast_in_dim.38
  35.9 8.2 %all-to-all-start.1 = ((bf16[8,8,32,256]{3,2,1,0:T(8,128)(2,1)}), bf16[8,8,32,256]{3,2,1,0:T(8,128)(2,1)S(1)}, u32[]{:S(2)}, u32[]{:S(2)}) async-start(bf16[8,8,32,256]{3,2,1,0:T(8,128)(2,1)} %broadcast_in_dim.38), calls=%async_computation.1 | async-start | bytes 2097152 | tf_op jit(solution)/shard_map/all_to_all | solution.py:221
  45.0 1.8 %collective-permute-start.1 = (bf16[8,144,256]{2,1,0:T(8,128)(2,1)}, bf16[8,144,256]{2,1,0:T(8,128)(2,1)S(1)}, u32[]{:S(2)}, u32[]{:S(2)}) collective-permute-start(bf16[8,144,256]{2,1,0:T(8,128)(2,1)} %slice.47), channel_id=1, source_target_pairs={{0,0},{1,16},{16,1},{17,17},{2,2},{3,18},{18,3},{19,19},{4,4},{5,2... | collective-permute-start | bytes 1769480 | tf_op jit(solution)/shard_map/ppermute | solution.py:314
  46.8 1.6 %collective-permute-start.2 = (bf16[8,144,256]{2,1,0:T(8,128)(2,1)}, bf16[8,144,256]{2,1,0:T(8,128)(2,1)S(1)}, u32[]{:S(2)}, u32[]{:S(2)}) collective-permute-start(bf16[8,144,256]{2,1,0:T(8,128)(2,1)} %slice.47), channel_id=1, source_target_pairs={{0,16},{1,0},{16,17},{17,1},{2,18},{3,2},{18,19},{19,3},{4,20},{5,... | collective-permute-start | bytes 1769480 | tf_op jit(solution)/shard_map/ppermute | solution.py:315
  49.0 3.7 %collective-permute-start.3 = (bf16[32,256]{1,0:T(8,128)(2,1)}, bf16[32,256]{1,0:T(8,128)(2,1)S(1)}, u32[]{:S(2)}, u32[]{:S(2)}) collective-permute-start(bf16[32,256]{1,0:T(8,128)(2,1)} %get-tuple-element.17), channel_id=1, source_target_pairs={{0,0},{1,16},{2,32},{3,48},{4,64},{5,80},{6,96},{7,112},{8,128},{9... | collective-permute-start | bytes 49160 | tf_op jit(solution)/shard_map/ppermute | solution.py:317
  52.8 1.7 %collective-permute-start.4 = (bf16[32,256]{1,0:T(8,128)(2,1)}, bf16[32,256]{1,0:T(8,128)(2,1)S(1)}, u32[]{:S(2)}, u32[]{:S(2)}) collective-permute-start(bf16[32,256]{1,0:T(8,128)(2,1)} %get-tuple-element.16), channel_id=1, source_target_pairs={{0,1},{1,17},{2,33},{3,49},{4,65},{5,81},{6,97},{7,113},{8,129},{9... | collective-permute-start | bytes 49160 | tf_op jit(solution)/shard_map/ppermute | solution.py:318
  55.1 1.6 %collective-permute-start = (bf16[8,16,128]{2,1,0:T(8,128)(2,1)S(1)}, bf16[8,16,128]{2,1,0:T(8,128)(2,1)S(1)}, u32[]{:S(2)}, u32[]{:S(2)}) collective-permute-start(bf16[8,16,128]{2,1,0:T(8,128)(2,1)S(1)} %slice.46.own_ref), channel_id=1, source_target_pairs={{0,1},{1,0},{2,3},{3,2},{4,5},{5,4},{6,7},{7,6},{8,9},{9,8},{10,11... | collective-permute-start | bytes 98312 | tf_op jit(solution)/shard_map/ppermute | solution.py:316
  56.8 1.0 slice.49
  58.0 11.7 %collective-permute-done.3.x0_ref = bf16[32,256]{1,0:T(8,128)(2,1)S(1)} collective-permute-done((bf16[32,256]{1,0:T(8,128)(2,1)}, bf16[32,256]{1,0:T(8,128)(2,1)S(1)}, u32[]{:S(2)}, u32[]{:S(2)}) %collective-permute-start.3) | collective-permute-done | bytes 16416 | tf_op jit(solution)/shard_map/ppermute | solution.py:317
  69.9 5.2 %shard_map.168 = bf16[8,2,48,256]{3,2,1,0:T(8,128)(2,1)} custom-call(s32[2]{0:T(128)S(1)} %pad_add_fusion.place_ref, bf16[8,16,128]{2,1,0:T(8,128)(2,1)S(1)} %slice.46.own_ref, bf16[8,16,128]{2,1,0:T(8,128)(2,1)S(1)} %collective-permute-done.swapped_ref, bf16[8,144,256]{2,1,0:T(8,128)(2,1)S(1)} %collective-permute-done.1.kva_ref, ...), custom_call_target="tpu_custom_call" | custom-call | tf_op jit(solution)/shard_map/pallas_call | solution.py:321
  75.2 7.7 %all-to-all-start.2 = ((bf16[16,48,256]{2,1,0:T(8,128)(2,1)}), bf16[16,48,256]{2,1,0:T(8,128)(2,1)S(1)}, u32[]{:S(2)}, u32[]{:S(2)}) async-start(bf16[16,48,256]{2,1,0:T(8,128)(2,1)} %bitcast.9), calls=%async_computation.2 | async-start | bytes 786432 | tf_op jit(solution)/shard_map/all_to_all | solution.py:330
  83.8 6.6 %all-to-all-done.2.parts_ref = bf16[16,48,256]{2,1,0:T(8,128)(2,1)S(1)} async-done(((bf16[16,48,256]{2,1,0:T(8,128)(2,1)}), bf16[16,48,256]{2,1,0:T(8,128)(2,1)S(1)}, u32[]{:S(2)}, u32[]{:S(2)}) %all-to-all-start.2) | async-done | bytes 393248 | tf_op jit(solution)/shard_map/all_to_all | solution.py:330
  90.3 1.5 shard_map.169
  92.5 6.6 %all-to-all-start.3 = ((bf16[16,32,128]{2,1,0:T(8,128)(2,1)}), bf16[16,32,128]{2,1,0:T(8,128)(2,1)S(1)}, u32[]{:S(2)}, u32[]{:S(2)}) async-start(bf16[16,32,128]{2,1,0:T(8,128)(2,1)} %broadcast_in_dim.42), calls=%async_computation.3 | async-start | bytes 262144 | tf_op jit(solution)/shard_map/all_to_all | solution.py:221
  99.5 7.1 %all-to-all-done.3 = bf16[16,32,128]{2,1,0:T(8,128)(2,1)S(1)} async-done(((bf16[16,32,128]{2,1,0:T(8,128)(2,1)}), bf16[16,32,128]{2,1,0:T(8,128)(2,1)S(1)}, u32[]{:S(2)}, u32[]{:S(2)}) %all-to-all-start.3) | async-done | bytes 131104 | tf_op jit(solution)/shard_map/all_to_all | solution.py:221
  106.8 1.1 fusion.2
  108.0 4.7 %collective-permute-start.5 = (bf16[16,32,2,32]{3,1,2,0:T(8,128)(2,1)S(1)}, bf16[16,32,2,32]{3,1,2,0:T(8,128)(2,1)}, u32[]{:S(2)}, u32[]{:S(2)}) collective-permute-start(bf16[16,32,2,32]{3,1,2,0:T(8,128)(2,1)S(1)} %bitcast.51), channel_id=1, source_target_pairs={{0,0},{1,16},{2,32},{3,48},{4,64},{5,80},{6,96},{7,112},{8,128},{9... | collective-permute-start | bytes 196616 | tf_op jit(solution)/shard_map/ppermute | solution.py:344
  115.3 1.2 copy.50
  116.5 26.6 %collective-permute-done.5 = bf16[16,32,2,32]{3,1,2,0:T(8,128)(2,1)} collective-permute-done((bf16[16,32,2,32]{3,1,2,0:T(8,128)(2,1)S(1)}, bf16[16,32,2,32]{3,1,2,0:T(8,128)(2,1)}, u32[]{:S(2)}, u32[]{:S(2)}) %collective-permute-start.5) | collective-permute-done | bytes 65568 | tf_op jit(solution)/shard_map/ppermute | solution.py:344
  143.1 1.3 copy.46
  144.7 8.6 %shard_map.170 = bf16[32,256,128]{2,1,0:T(8,128)(2,1)} custom-call(f32[32]{0:T(128)S(1)} %get-tuple-element.18.divisor_ref, bf16[256,1024]{1,0:T(8,128)(2,1)S(1)} %bitcast_select_fusion.right_ref, bf16[1024,32]{1,0:T(8,128)(2,1)S(1)} %bitcast.38, bf16[32,4096]{1,0:T(8,128)(2,1)S(1)} %reshape.84.map_ref, bf16[32,256,128]{2,1,0:T(8,128)(2,1)S(1)} %copy-done.1), custom_call_target="tpu_custom_call" | custom-call | tf_op jit(solution)/shard_map/pallas_call | solution.py:355
  (73 shorter events, 18.0 us)
Async XLA Ops:
  3.8 1.6 %copy-start = (bf16[32,256,128]{2,1,0:T(8,128)(2,1)S(1)}, bf16[32,256,128]{2,1,0:T(8,128)(2,1)}, u32[]{:S(2)}) copy-start(bf16[32,256,128]{2,1,0:T(8,128)(2,1)} %pair_ref.3) | copy-start | bytes 6291460
  5.4 0.9 copy-start.2
  6.3 0.9 copy-start.3
  7.2 0.9 copy-start.4
  8.1 0.9 copy-start.5
  9.0 0.9 copy-start.6
  9.9 0.7 copy-start.8
  10.6 0.7 copy-start.10
  34.8 19.7 %copy-start.15 = (s32[32]{0:T(128)S(1)}, s32[32]{0:T(128)}, u32[]{:S(2)}) copy-start(s32[32]{0:T(128)} %param.18) | copy-start | bytes 388
  35.9 22.0 %copy-start.14 = (bf16[256,32]{0,1:T(8,128)(2,1)S(1)}, bf16[256,32]{0,1:T(8,128)(2,1)}, u32[]{:S(2)}) copy-start(bf16[256,32]{0,1:T(8,128)(2,1)} %param.29) | copy-start | bytes 49156
  35.9 34.0 %all-to-all-start.1 = ((bf16[8,8,32,256]{3,2,1,0:T(8,128)(2,1)}), bf16[8,8,32,256]{3,2,1,0:T(8,128)(2,1)S(1)}, u32[]{:S(2)}, u32[]{:S(2)}) async-start(bf16[8,8,32,256]{3,2,1,0:T(8,128)(2,1)} %broadcast_in_dim.38), calls=%async_computation.1 | async-start | bytes 2097152 | tf_op jit(solution)/shard_map/all_to_all | solution.py:221
  45.0 45.3 %copy-start.7 = (bf16[256,256]{1,0:T(8,128)(2,1)S(1)}, bf16[256,256]{1,0:T(8,128)(2,1)}, u32[]{:S(2)}) copy-start(bf16[256,256]{1,0:T(8,128)(2,1)} %final_ref.1) | copy-start | bytes 393220
  45.0 45.3 %copy-start.9 = (f32[256]{0:T(256)S(1)}, f32[256]{0:T(256)}, u32[]{:S(2)}) copy-start(f32[256]{0:T(256)} %param.28) | copy-start | bytes 3076
  45.0 24.9 %collective-permute-start.1 = (bf16[8,144,256]{2,1,0:T(8,128)(2,1)}, bf16[8,144,256]{2,1,0:T(8,128)(2,1)S(1)}, u32[]{:S(2)}, u32[]{:S(2)}) collective-permute-start(bf16[8,144,256]{2,1,0:T(8,128)(2,1)} %slice.47), channel_id=1, source_target_pairs={{0,0},{1,16},{16,1},{17,17},{2,2},{3,18},{18,3},{19,19},{4,4},{5,2... | collective-permute-start | bytes 1769480 | tf_op jit(solution)/shard_map/ppermute | solution.py:314
  46.8 23.1 %collective-permute-start.2 = (bf16[8,144,256]{2,1,0:T(8,128)(2,1)}, bf16[8,144,256]{2,1,0:T(8,128)(2,1)S(1)}, u32[]{:S(2)}, u32[]{:S(2)}) collective-permute-start(bf16[8,144,256]{2,1,0:T(8,128)(2,1)} %slice.47), channel_id=1, source_target_pairs={{0,16},{1,0},{16,17},{17,1},{2,18},{3,2},{18,19},{19,3},{4,20},{5,... | collective-permute-start | bytes 1769480 | tf_op jit(solution)/shard_map/ppermute | solution.py:315
  49.0 20.6 %collective-permute-start.3 = (bf16[32,256]{1,0:T(8,128)(2,1)}, bf16[32,256]{1,0:T(8,128)(2,1)S(1)}, u32[]{:S(2)}, u32[]{:S(2)}) collective-permute-start(bf16[32,256]{1,0:T(8,128)(2,1)} %get-tuple-element.17), channel_id=1, source_target_pairs={{0,0},{1,16},{2,32},{3,48},{4,64},{5,80},{6,96},{7,112},{8,128},{9... | collective-permute-start | bytes 49160 | tf_op jit(solution)/shard_map/ppermute | solution.py:317
  52.8 17.1 %collective-permute-start.4 = (bf16[32,256]{1,0:T(8,128)(2,1)}, bf16[32,256]{1,0:T(8,128)(2,1)S(1)}, u32[]{:S(2)}, u32[]{:S(2)}) collective-permute-start(bf16[32,256]{1,0:T(8,128)(2,1)} %get-tuple-element.16), channel_id=1, source_target_pairs={{0,1},{1,17},{2,33},{3,49},{4,65},{5,81},{6,97},{7,113},{8,129},{9... | collective-permute-start | bytes 49160 | tf_op jit(solution)/shard_map/ppermute | solution.py:318
  55.1 14.8 %collective-permute-start = (bf16[8,16,128]{2,1,0:T(8,128)(2,1)S(1)}, bf16[8,16,128]{2,1,0:T(8,128)(2,1)S(1)}, u32[]{:S(2)}, u32[]{:S(2)}) collective-permute-start(bf16[8,16,128]{2,1,0:T(8,128)(2,1)S(1)} %slice.46.own_ref), channel_id=1, source_target_pairs={{0,1},{1,0},{2,3},{3,2},{4,5},{5,4},{6,7},{7,6},{8,9},{9,8},{10,11... | collective-permute-start | bytes 98312 | tf_op jit(solution)/shard_map/ppermute | solution.py:316
  58.0 41.2 %copy-start.13 = (bf16[1024,128]{1,0:T(8,128)(2,1)S(1)}, bf16[1024,128]{1,0:T(8,128)(2,1)}, u32[]{:S(2)}) copy-start(bf16[1024,128]{1,0:T(8,128)(2,1)} %param.31) | copy-start | bytes 786436
  75.2 15.2 %all-to-all-start.2 = ((bf16[16,48,256]{2,1,0:T(8,128)(2,1)}), bf16[16,48,256]{2,1,0:T(8,128)(2,1)S(1)}, u32[]{:S(2)}, u32[]{:S(2)}) async-start(bf16[16,48,256]{2,1,0:T(8,128)(2,1)} %bitcast.9), calls=%async_computation.2 | async-start | bytes 786432 | tf_op jit(solution)/shard_map/all_to_all | solution.py:330
  92.5 14.1 %all-to-all-start.3 = ((bf16[16,32,128]{2,1,0:T(8,128)(2,1)}), bf16[16,32,128]{2,1,0:T(8,128)(2,1)S(1)}, u32[]{:S(2)}, u32[]{:S(2)}) async-start(bf16[16,32,128]{2,1,0:T(8,128)(2,1)} %broadcast_in_dim.42), calls=%async_computation.3 | async-start | bytes 262144 | tf_op jit(solution)/shard_map/all_to_all | solution.py:221
  99.4 13.6 %collective-permute-start.6 = (bf16[16,32,256]{2,1,0:T(8,128)(2,1)S(1)}, bf16[16,32,256]{2,1,0:T(8,128)(2,1)S(1)}, u32[]{:S(2)}, u32[]{:S(2)}) collective-permute-start(bf16[16,32,256]{2,1,0:T(8,128)(2,1)S(1)} %slice.53), channel_id=1, source_target_pairs={{0,16},{16,0},{1,17},{17,1},{2,18},{18,2},{3,19},{19,3},{4,20},{20... | collective-permute-start | bytes 786440 | tf_op jit(solution)/shard_map/ppermute | solution.py:332
  108.0 35.1 %collective-permute-start.5 = (bf16[16,32,2,32]{3,1,2,0:T(8,128)(2,1)S(1)}, bf16[16,32,2,32]{3,1,2,0:T(8,128)(2,1)}, u32[]{:S(2)}, u32[]{:S(2)}) collective-permute-start(bf16[16,32,2,32]{3,1,2,0:T(8,128)(2,1)S(1)} %bitcast.51), channel_id=1, source_target_pairs={{0,0},{1,16},{2,32},{3,48},{4,64},{5,80},{6,96},{7,112},{8,128},{9... | collective-permute-start | bytes 196616 | tf_op jit(solution)/shard_map/ppermute | solution.py:344
  114.3 30.4 %copy-start.1 = (bf16[32,256,128]{2,1,0:T(8,128)(2,1)S(1)}, bf16[32,256,128]{2,1,0:T(8,128)(2,1)}, u32[]{:S(2)}) copy-start(bf16[32,256,128]{2,1,0:T(8,128)(2,1)} %pair_ref.3) | copy-start | bytes 6291460
  (2 other events, 1.3 us)

commit v2 on v1

--- a/solution.py
+++ b/solution.py
@@ -9,7 +9,8 @@
 BIG = 1000000000.0
 F32 = jnp.float32
 BF16 = jnp.bfloat16
-VMEM = 48 * 1024 * 1024
+VMEM = 40 * 1024 * 1024
+FULL = 60 * 1024 * 1024
 ALL = ("q", "c", "z", "x")
 
 
@@ -29,10 +30,16 @@
     return center * lax.rsqrt(spread + EPS)
 
 
+def row_of(flags, count):
+    lane = lax.broadcasted_iota(jnp.int32, (count, 256), 1)
+    row = lax.broadcasted_iota(jnp.int32, (count, 256), 0)
+    return jnp.sum(jnp.where(lane == row * 8, flags, 0.0), axis=1, keepdims=True)
+
+
 def front_kernel(
+    live_ref,
     pair_ref,
     seq_ref,
-    live_ref,
     flags_ref,
     g1_ref,
     ask_ref,
@@ -45,16 +52,18 @@
     other_ref,
     msg_ref,
     gate_ref,
+    prior_ref,
     right_ref,
     bias_scr,
     norm_scr,
 ):
     step = pl.program_id(0)
     rows = pair_ref.shape[0]
+    first_row = (lax.axis_index("z") * 2 + lax.axis_index("x")) * 2
 
     pair = pair_ref[...].reshape(rows * 256, 128).astype(F32)
     pair = (center_and_scale(pair) * gp_ref[...]).astype(BF16)
-    bias = dot(head_ref[...], pair, TT)
+    bias = dot(head_ref[...], pair, NT)
     for r in range(rows):
         for i in range(2):
             bias_scr[i, pl.ds(pl.multiple_of((step * rows + r) * 8, 8), 8), :] = bias[
@@ -63,7 +72,8 @@
 
     @pl.when(step == 0)
     def _():
-        base = center_and_scale(seq_ref[...].astype(F32))
+        raw = seq_ref[...].astype(F32)
+        base = center_and_scale(raw)
         normed = (base * g1_ref[...]).astype(BF16)
         keys = dot(look_ref[...], normed, TT).astype(BF16)
         values = dot(cont_ref[...], normed, TT).astype(BF16)
@@ -75,9 +85,10 @@
         wide = normed.astype(F32)
         for i in range(2):
             norm_scr[i] = wide[:, i * 128 : (i + 1) * 128]
-        band = jnp.concatenate(
-            [norm_scr[i, pl.ds(0, 64, stride=8), :] for i in range(2)], axis=1
-        ).astype(BF16)
+            norm_scr[2 + i] = raw[:, i * 128 : (i + 1) * 128]
+        cuts = [norm_scr[i, pl.ds(0, 64, stride=8), :] for i in range(4)]
+        band = jnp.concatenate(cuts[:2], axis=1).astype(BF16)
+        prior_ref[...] = jnp.concatenate(cuts[2:], axis=1)
         gate_ref[...] = jax.nn.sigmoid(dot(band, sig_ref[...], NN))
         query = (dot(band, ask_ref[...], NN) * 32 ** (-0.5)).astype(BF16).astype(F32)
         flags = flags_ref[...].astype(F32)
@@ -91,9 +102,11 @@
             ]
             msg_ref[h, 160:176, :] = jnp.concatenate(parts + [mask], axis=1).astype(BF16)
         again = (base * g2_ref[...]).astype(BF16)
-        right = dot(other_ref[...], again, TT)
+        right = dot(other_ref[...], again, NT)
+        flags = jnp.concatenate([flags[0:1], flags[1:2]], axis=1)
         for s in range(2):
-            right_ref[s] = (right[:, s * 256 : (s + 1) * 256] * live_ref[s : s + 1, :]).astype(BF16)
+            live = live_ref[first_row + s].astype(F32) * flags
+            right_ref[s] = (right[:, s * 256 : (s + 1) * 256] * live).astype(BF16)
 
     @pl.when(step == pl.num_programs(0) - 1)
     def _():
@@ -112,9 +125,9 @@
 
 
 def attend_kernel(
-    place_ref, own_ref, swapped_ref, kva_ref, kvb_ref, bias_ref, x0_ref, x1_ref, out_ref, extra_scr
+    own_ref, swapped_ref, kva_ref, kvb_ref, bias_ref, x0_ref, x1_ref, out_ref, extra_scr
 ):
-    c, x = place_ref[0], place_ref[1]
+    c, x = lax.axis_index("c"), lax.axis_index("x")
     lane = lax.broadcasted_iota(jnp.int32, (128, 128), 1)
     block, inner = lane // 32, lane % 32
     first_x = jnp.where(x == 0, x0_ref[...], x1_ref[...])
@@ -160,8 +173,22 @@
 
 
 def refresh_kernel(
-    parts_ref, gate_ref, prior_ref, final_ref, g2_ref, first_ref, other_ref, live_ref, fresh_ref, sides_ref
+    live_ref,
+    parts_ref,
+    gate_ref,
+    prior_ref,
+    flags_ref,
+    final_ref,
+    g2_ref,
+    first_ref,
+    other_ref,
+    fresh_ref,
+    sides_ref,
 ):
+    first_row = (lax.axis_index("z") * 2 + lax.axis_index("x")) * 2
+    flags = flags_ref[...].astype(F32)
+    band = row_of(jnp.concatenate([flags[0:1], flags[1:2]], axis=1), 32)
+    live = jnp.concatenate([band * live_ref[first_row + s].astype(F32) for s in range(2)], axis=0)
     rows = lax.broadcasted_iota(jnp.int32, (128, 128), 0)
     lanes = lax.broadcasted_iota(jnp.int32, (128, 128), 1)
     spread = [jnp.where(rows == (lanes // 32) * 32 + t, 1.0, 0.0).astype(BF16) for t in range(6)]
@@ -188,29 +215,86 @@
             )
     attended = jnp.concatenate(lined, axis=0)
     gated = (gate_ref[...] * attended).astype(BF16)
-    fresh = (prior_ref[...].astype(F32) + dot(gated, final_ref[...], NN)).astype(BF16)
+    fresh = (prior_ref[...] + dot(gated, final_ref[...], NN)).astype(BF16)
     fresh_ref[...] = fresh
     again = (center_and_scale(fresh.astype(F32)) * g2_ref[...]).astype(BF16)
-    left = dot(again, first_ref[...], NN) * live_ref[...]
-    right = dot(again, other_ref[...], NN) * live_ref[...]
-    sides_ref[...] = jnp.concatenate(
-        [left[0:32], right[0:32], left[32:64], right[32:64]], axis=1
-    ).astype(BF16)
-
-
-def outer_kernel(divisor_ref, right_ref, left_ref, map_ref, pair_ref, out_ref, scr):
+    for i, factor in enumerate((first_ref, other_ref)):
+        side = dot(again, factor[...], NT) * live
+        parts = [side[s * 32 + g * 16 : s * 32 + g * 16 + 16] for g in range(2) for s in range(2)]
+        sides_ref[i * 16 : i * 16 + 16, :] = jnp.concatenate(parts, axis=1).astype(BF16)
+
+
+def pack_kernel(mine_ref, theirs_ref, map_ref, factors_ref, mapping_ref, scr):
+    swapped = lax.axis_index("c") == 1
+    rows = []
+    for q in range(8):
+        for c in range(2):
+            for x in range(2):
+                mine = mine_ref[2 * q + x, 16:48, :].astype(F32)
+                theirs = theirs_ref[2 * q + x].astype(F32)
+                rows.append(jnp.where(swapped == (c == 1), mine, theirs))
+    for i in range(8):
+        factors_ref[:, i * 128 : (i + 1) * 128] = jnp.concatenate(
+            rows[i * 4 : i * 4 + 4], axis=0
+        ).T.astype(BF16)
+    scr[...] = map_ref[...].astype(F32)
+    for d in range(32):
+        piece = scr[pl.ds(d, 32, stride=32), :].astype(BF16)
+        for k in range(4):
+            mapping_ref[k * 32 : k * 32 + 32, d * 128 : (d + 1) * 128] = piece
+
+
+def map_kernel(sides_ref, mapping_ref, out_ref, side_scr, scr):
+    step = pl.program_id(0)
+
+    @pl.when(step == 0)
+    def _():
+        for n in range(16):
+            side_scr[n * 16 : n * 16 + 16, :] = sides_ref[n, 0:16, :].astype(F32)
+
+    block = lax.broadcasted_iota(jnp.int32, (16, 128), 1) // 32
+    group = step // 2
+    lefts = []
+    for r in range(8):
+        lined = side_scr[pl.ds((step % 2) * 8 + r, 16, stride=16), :]
+        for s in range(2):
+            lefts.append(jnp.where(block == group * 2 + s, lined, 0.0))
+    left = jnp.concatenate(lefts, axis=0).astype(BF16)
+    for d in range(0, 32, 2):
+        mapped = dot(left, mapping_ref[:, d * 128 : (d + 2) * 128], NN)
+        for e in range(2):
+            for r in range(8):
+                for s in range(2):
+                    scr[r, pl.ds(s * 32 + d + e, 16, stride=64), :] = mapped[
+                        r * 32 + s * 16 : r * 32 + s * 16 + 16, e * 128 : e * 128 + 128
+                    ]
+    for r in range(8):
+        out_ref[r // 2, :, (r % 2) * 128 : (r % 2) * 128 + 128] = scr[r].astype(BF16)
+
+
+def outer_kernel(live_ref, flags_ref, factors_ref, band_ref, mapped_ref, pair_ref, out_ref, scr, full_scr):
     step = pl.program_id(0)
     rows = pair_ref.shape[0]
+
+    @pl.when(step == 0)
+    def _():
+        for i in range(8):
+            scr[...] = factors_ref[:, i * 128 : (i + 1) * 128].astype(F32)
+            pair = [band_ref[2 * i + n].astype(F32) for n in range(2)]
+            band = jnp.concatenate(
+                [jnp.concatenate([p[:, g * 64 : g * 64 + 64] for p in pair], axis=1) for g in range(2)], axis=0
+            )
+            scr[pl.ds(0, 32, stride=8), :] = band
+            full_scr[:, i * 128 : (i + 1) * 128] = scr[...].astype(BF16)
+
+    nvalid = jnp.int32(0)
+    for s in range(32):
+        nvalid += live_ref[s]
     for r in range(0, rows, 2):
-        mapped = dot(left_ref[r * 32 : (r + 2) * 32, :], map_ref[...], NN).astype(BF16)
-        for d in range(32):
-            for i in range(2):
-                scr[d * 32 : d * 32 + 32, i * 128 : i * 128 + 128] = mapped[
-                    i * 32 : i * 32 + 32, d * 128 : d * 128 + 128
-                ]
-        projected = dot(right_ref[...], scr[...], NN)
+        projected = dot(full_scr[...], mapped_ref[r // 2], NN)
         for i in range(2):
-            scale = 1.0 / divisor_ref[step * rows + r + i]
+            flag = flags_ref[(step * rows + r + i) * 8]
+            scale = 1.0 / jnp.maximum((nvalid * flag).astype(F32), 1.0)
             out_ref[r + i] = (
                 pair_ref[r + i].astype(F32) + projected[:, i * 128 : (i + 1) * 128] * scale
             ).astype(BF16)
@@ -223,6 +307,10 @@
 
 def whole(shape):
     return pl.BlockSpec(shape, lambda *_: (0,) * len(shape))
+
+
+SCALARS = pl.BlockSpec(memory_space=pltpu.SMEM)
+ARRAY = pl.BlockSpec(memory_space=pltpu.VMEM)
 
 
 def params():
@@ -254,24 +342,19 @@
     other_factor_matrix,
     product_mapping_matrix,
 ):
-    c, z, x = lax.axis_index("c"), lax.axis_index("z"), lax.axis_index("x")
-    row_live = lax.dynamic_slice_in_dim(sequence_valid_flags, (z * 2 + x) * 2, 2).astype(F32)
-    positions = position_valid_flags.astype(F32)
-    live = row_live[:, None] * positions[None, :]
-    live_band = live.reshape(2, 32, 8)[:, :, 0].reshape(64, 1)
-    prior = sequence_activity.reshape(64, 8, 256)[:, 0]
+    c = lax.axis_index("c")
     g2 = product_scale_vector.reshape(1, 256)
-
-    seq = sequence_activity.reshape(512, 256)
-    message, gate, right = pl.pallas_call(
+    flags = position_valid_flags.reshape(2, 128)
+    first, other = first_factor_matrix.T, other_factor_matrix.T
+
+    message, gate, prior, right = pl.pallas_call(
         front_kernel,
         grid=(4,),
-        in_specs=[pl.BlockSpec((8, 256, 128), lambda i: (i, 0, 0))]
+        in_specs=[SCALARS, pl.BlockSpec((8, 256, 128), lambda i: (i, 0, 0))]
         + [
             whole(s)
             for s in (
                 (512, 256),
-                (2, 256),
                 (2, 128),
                 (1, 256),
                 (256, 256),
@@ -279,33 +362,34 @@
                 (256, 256),
                 (256, 256),
                 (1, 128),
-                (128, 8),
+                (8, 128),
                 (1, 256),
-                (256, 32),
+                (32, 256),
             )
         ],
-        out_specs=[whole((8, 176, 256)), whole((64, 256)), whole((2, 32, 256))],
+        out_specs=[whole((8, 176, 256)), whole((64, 256)), whole((64, 256)), whole((2, 32, 256))],
         out_shape=[
             jax.ShapeDtypeStruct((8, 176, 256), BF16),
             jax.ShapeDtypeStruct((64, 256), F32),
+            jax.ShapeDtypeStruct((64, 256), F32),
             jax.ShapeDtypeStruct((2, 32, 256), BF16),
         ],
-        scratch_shapes=[pltpu.VMEM((2, 256, 128), F32), pltpu.VMEM((2, 512, 128), F32)],
-        compiler_params=params(),
+        scratch_shapes=[pltpu.VMEM((2, 256, 128), F32), pltpu.VMEM((4, 512, 128), F32)],
+        compiler_params=pltpu.CompilerParams(vmem_limit_bytes=FULL),
     )(
+        sequence_valid_flags,
         couple_activity,
-        seq,
-        live,
-        position_valid_flags.reshape(2, 128),
+        sequence_activity.reshape(512, 256),
+        flags,
         attend_scale_vector.reshape(1, 256),
         asking_matrix,
         lookup_matrix,
         content_matrix,
         sigmoid_matrix,
         couple_scale_vector.reshape(1, 128),
-        headwise_additive_matrix,
+        headwise_additive_matrix.T,
         g2,
-        other_factor_matrix,
+        other,
     )
 
     heads = lax.all_to_all(message, "q", 0, 0, tiled=True)
@@ -320,53 +404,62 @@
 
     parts = pl.pallas_call(
         attend_kernel,
-        in_specs=[pl.BlockSpec(memory_space=pltpu.SMEM)] + [pl.BlockSpec(memory_space=pltpu.VMEM)] * 7,
-        out_specs=pl.BlockSpec(memory_space=pltpu.VMEM),
+        in_specs=[ARRAY] * 7,
+        out_specs=ARRAY,
         out_shape=jax.ShapeDtypeStruct((8, 2, 48, 256), BF16),
         scratch_shapes=[pltpu.VMEM((2, 128, 2048), F32)],
         compiler_params=params(),
-    )(jnp.stack([c, x]).astype(jnp.int32), own, swapped, kva, kvb, bias, x0, x1)
+    )(own, swapped, kva, kvb, bias, x0, x1)
 
     parts = lax.all_to_all(parts.reshape(16, 48, 256), ("q", "x"), 0, 0, tiled=True)
-    mine = parts[:, 16:48, :]
-    theirs = lax.ppermute(mine, "c", SWAP)
+    theirs = lax.ppermute(parts[:, 16:48, :], "c", SWAP)
 
     fresh, sides = pl.pallas_call(
         refresh_kernel,
-        in_specs=[pl.BlockSpec(memory_space=pltpu.VMEM)] * 8,
-        out_specs=[pl.BlockSpec(memory_space=pltpu.VMEM)] * 2,
+        in_specs=[SCALARS] + [ARRAY] * 8,
+        out_specs=[ARRAY] * 2,
         out_shape=[jax.ShapeDtypeStruct((64, 256), BF16), jax.ShapeDtypeStruct((32, 128), BF16)],
         compiler_params=params(),
-    )(parts, gate, prior, attend_final_matrix, g2, first_factor_matrix, other_factor_matrix, live_band)
-
-    sides = gather(sides, ("z", "x"), 16).reshape(16, 32, 2, 2, 32)
-    left = sides[:, :, :, 0].transpose(1, 0, 2, 3).reshape(1024, 32)
-    right_band = lax.ppermute(sides[:, :, :, 1], ALL, MIRROR)
-    right_band = right_band.transpose(1, 3, 0, 2).reshape(32, 1, 1024)
-    even, odd = jnp.where(c == 0, mine, theirs), jnp.where(c == 0, theirs, mine)
-    factors = jnp.stack([even.reshape(8, 2, 32, 256), odd.reshape(8, 2, 32, 256)], axis=1)
-    factors = factors.transpose(4, 3, 0, 1, 2).reshape(32, 8, 1024)
-    slot = lax.broadcasted_iota(jnp.int32, (1, 8, 1), 1)
-    factors = jnp.where(slot == 0, right_band, factors).reshape(256, 1024)
-
-    nvalid = jnp.sum(sequence_valid_flags.astype(F32))
-    divisor = jnp.maximum(nvalid * positions.reshape(32, 8)[:, 0], 1.0)
-    mapping = product_mapping_matrix.reshape(32, 4096)
+    )(sequence_valid_flags, parts, gate, prior, flags, attend_final_matrix, g2, first, other)
+
+    sides = gather(sides, ("z", "x"), 16)
+    band = lax.ppermute(sides[:, 16:32, :], ALL, MIRROR)
+
+    factors, mapping = pl.pallas_call(
+        pack_kernel,
+        in_specs=[ARRAY] * 3,
+        out_specs=[ARRAY] * 2,
+        out_shape=[jax.ShapeDtypeStruct((256, 1024), BF16), jax.ShapeDtypeStruct((128, 4096), BF16)],
+        scratch_shapes=[pltpu.VMEM((1024, 128), F32)],
+        cost_estimate=pl.CostEstimate(flops=0, bytes_accessed=12 << 20, transcendentals=0),
+        compiler_params=params(),
+    )(parts, theirs, product_mapping_matrix)
+    mapped = pl.pallas_call(
+        map_kernel,
+        grid=(4,),
+        in_specs=[whole((16, 32, 128)), whole((128, 4096))],
+        out_specs=pl.BlockSpec((4, 1024, 256), lambda i: (i, 0, 0)),
+        out_shape=jax.ShapeDtypeStruct((16, 1024, 256), BF16),
+        scratch_shapes=[pltpu.VMEM((256, 128), F32), pltpu.VMEM((8, 1024, 128), F32)],
+        cost_estimate=pl.CostEstimate(flops=4 << 30, bytes_accessed=20 << 20, transcendentals=0),
+        compiler_params=params(),
+    )(sides, mapping)
     pair_out = pl.pallas_call(
         outer_kernel,
         grid=(4,),
         in_specs=[
-            pl.BlockSpec(memory_space=pltpu.SMEM),
+            SCALARS,
+            SCALARS,
             whole((256, 1024)),
-            pl.BlockSpec((256, 32), lambda i: (i, 0)),
-            whole((32, 4096)),
+            whole((16, 16, 128)),
+            pl.BlockSpec((4, 1024, 256), lambda i: (i, 0, 0)),
             pl.BlockSpec((8, 256, 128), lambda i: (i, 0, 0)),
         ],
         out_specs=pl.BlockSpec((8, 256, 128), lambda i: (i, 0, 0)),
         out_shape=jax.ShapeDtypeStruct((32, 256, 128), BF16),
-        scratch_shapes=[pltpu.VMEM((1024, 256), BF16)],
+        scratch_shapes=[pltpu.VMEM((256, 128), F32), pltpu.VMEM((256, 1024), BF16)],
         compiler_params=params(),
-    )(divisor, factors, left, mapping, couple_activity)
+    )(sequence_valid_flags, position_valid_flags, factors, band, mapped, couple_activity)
     return fresh.reshape(2, 32, 256), pair_out
 
 

time: 154 us -> 124 us (0.81)
  the two profiles are of different devices: /device:TPU:68 before, /device:TPU:1 now
where the time goes in v2:
time: 124 us; the launch traced here: 123 us
  blocking collectives  49.1 us (40%)
  Pallas kernels  30.7 us (25%)
  starting transfers between devices  24.2 us (20%)
  waiting for transfers between devices  16.3 us (13%)
  local copies, waits for them, and re-layouts  2.08 us (2%)
    all_to_all x1, blocking collectives, local(): heads = lax.all_to_all(message, 'q', 0, 0, tiled=True)  20 us
    all_to_all x1, blocking collectives, local(): lax.all_to_all(parts.reshape(16, 48, 256), ('q', 'x'), 0, 0, tiled=True)  17.5 us
    pallas_call x1, Pallas kernels, local(): pl.pallas_call(map_kernel, grid=(4,), in_specs=[whole((16, 32, 128)), who...  13 us
    all_to_all x1, blocking collectives, gather(): return lax.all_to_all(tiled, axes, 0, 0, tiled=True)  11.7 us
    ppermute x1, waiting for transfers between devices, local(): x0 = lax.ppermute(jnp.where(c == 0, right[0], right[1]), ALL, MIRROR)  9.59 us
    all_to_all x1, starting transfers between devices, gather(): return lax.all_to_all(tiled, axes, 0, 0, tiled=True)  8.18 us
    all_to_all x1, waiting for transfers between devices, gather(): return lax.all_to_all(tiled, axes, 0, 0, tiled=True)  6.7 us
    pallas_call x1, Pallas kernels, local(): pl.pallas_call(front_kernel, grid=(4,), in_specs=[SCALARS, pl.BlockSpec((...  6.42 us
  transfers between devices with their start and end apart: 8, of which 2 were waited for; matrix products, arithmetic and copies ran while one was open for 1% of the time, Pallas kernels for 13%

profile of v2, /device:TPU:1, one launch (start us, length us, event | category | flops | bytes accessed | tf_op | source)
XLA Modules:
  0.0 123.3 jit_solution(17698017272247078970)
XLA Ops:
  0.6 6.4 %shard_map.167 = (bf16[8,176,256]{2,1,0:T(8,128)(2,1)}, f32[64,256]{1,0:T(8,128)}, f32[64,256]{1,0:T(8,128)}, bf16[2,32,256]{2,1,0:T(8,128)(2,1)}) custom-call(s32[32]{0:T(128)} %live_ref.5, bf16[32,256,128]{2,1,0:T(8,128)(2,1)} %pair_ref.3, bf16[512,256]{1,0:T(8,128)(2,1)} %bitcast.22, s32[2,128]{1,0:T(2,128)} %bitcast.18, f32[1,256]{1,0:T(1,128)} %bitcast.24, ...), custom_call_target="tpu_custom_call" | custom-call | tf_op jit(solution)/shard_map/pallas_call | solution.py:350
  7.1 20.0 %all_to_all.20 = bf16[8,176,256]{2,1,0:T(8,128)(2,1)S(1)} all-to-all(bf16[8,176,256]{2,1,0:T(8,128)(2,1)} %get-tuple-element.10), channel_id=1, replica_groups=mesh['q'=8,'c'=2,'z'=8,'x'=2] {'q'}, dimensions={0} | all-to-all | bytes 1441792 | tf_op jit(solution)/shard_map/all_to_all | solution.py:395
  27.0 0.0 copy-start.10
  27.1 1.1 broadcast_in_dim.4
  28.2 8.2 %all-to-all-start.1 = ((bf16[8,8,32,256]{3,2,1,0:T(8,128)(2,1)}), bf16[8,8,32,256]{3,2,1,0:T(8,128)(2,1)S(1)}, u32[]{:S(2)}, u32[]{:S(2)}) async-start(bf16[8,8,32,256]{3,2,1,0:T(8,128)(2,1)} %broadcast_in_dim.4), calls=%async_computation.1 | async-start | bytes 2097152 | tf_op jit(solution)/shard_map/all_to_all | solution.py:305
  36.3 0.9 slice.31
  37.2 0.0 copy-start.7
  37.2 0.0 copy-start.8
  37.3 0.4 collective-permute-start.2
  37.7 5.7 %collective-permute-start.1 = (bf16[8,144,256]{2,1,0:T(8,128)(2,1)}, bf16[8,144,256]{2,1,0:T(8,128)(2,1)S(1)}, u32[]{:S(2)}, u32[]{:S(2)}) collective-permute-start(bf16[8,144,256]{2,1,0:T(8,128)(2,1)} %slice.31), channel_id=1, source_target_pairs={{0,0},{1,16},{16,1},{17,17},{2,2},{3,18},{18,3},{19,19},{4,4},{5,2... | collective-permute-start | bytes 1769480 | tf_op jit(solution)/shard_map/ppermute | solution.py:398
  43.4 0.1 collective-permute-start
  43.5 0.5 collective-permute-start.4
  44.0 3.5 %collective-permute-start.3 = (bf16[32,256]{1,0:T(8,128)(2,1)S(1)}, bf16[32,256]{1,0:T(8,128)(2,1)S(1)}, u32[]{:S(2)}, u32[]{:S(2)}) collective-permute-start(bf16[32,256]{1,0:T(8,128)(2,1)S(1)} %get-tuple-element.19), channel_id=1, source_target_pairs={{0,0},{1,16},{2,32},{3,48},{4,64},{5,80},{6,96},{7,112},{8,128},{9... | collective-permute-start | bytes 49160 | tf_op jit(solution)/shard_map/ppermute | solution.py:401
  47.5 9.6 %collective-permute-done.3.x0_ref = bf16[32,256]{1,0:T(8,128)(2,1)S(1)} collective-permute-done((bf16[32,256]{1,0:T(8,128)(2,1)S(1)}, bf16[32,256]{1,0:T(8,128)(2,1)S(1)}, u32[]{:S(2)}, u32[]{:S(2)}) %collective-permute-start.3) | collective-permute-done | bytes 16416 | tf_op jit(solution)/shard_map/ppermute | solution.py:401
  57.1 6.7 %all-to-all-done.1.bias_ref = bf16[8,8,32,256]{3,2,1,0:T(8,128)(2,1)S(1)} async-done(((bf16[8,8,32,256]{3,2,1,0:T(8,128)(2,1)}), bf16[8,8,32,256]{3,2,1,0:T(8,128)(2,1)S(1)}, u32[]{:S(2)}, u32[]{:S(2)}) %all-to-all-start.1) | async-done | bytes 1048608 | tf_op jit(solution)/shard_map/all_to_all | solution.py:305
  63.8 3.8 %shard_map.168 = bf16[8,2,48,256]{3,2,1,0:T(8,128)(2,1)S(1)} custom-call(bf16[8,16,128]{2,1,0:T(8,128)(2,1)S(1)} %slice.30.own_ref, bf16[8,16,128]{2,1,0:T(8,128)(2,1)S(1)} %collective-permute-done.swapped_ref, bf16[8,144,256]{2,1,0:T(8,128)(2,1)S(1)} %collective-permute-done.1.kva_ref, bf16[8,144,256]{2,1,0:T(8,128)(2,1)S(1)} %collective-permute-done.2.kvb_ref, ...), custom_call_target="tpu_custom_call" | custom-call | tf_op jit(solution)/shard_map/pallas_call | solution.py:405
  67.6 17.5 %all_to_all.21.parts_ref.mine_ref = bf16[16,48,256]{2,1,0:T(8,128)(2,1)S(1)} all-to-all(bf16[16,48,256]{2,1,0:T(8,128)(2,1)S(1)} %bitcast.14), channel_id=1, replica_groups=mesh['q'=8,'c'=2,'z'=8,'x'=2] {'q','x'}, dimensions={0} | all-to-all | bytes 786432 | tf_op jit(solution)/shard_map/all_to_all | solution.py:414
  85.1 2.0 %collective-permute-start.5 = (bf16[16,32,256]{2,1,0:T(8,128)(2,1)S(1)}, bf16[16,32,256]{2,1,0:T(8,128)(2,1)S(1)}, u32[]{:S(2)}, u32[]{:S(2)}) collective-permute-start(bf16[16,32,256]{2,1,0:T(8,128)(2,1)S(1)} %slice.33), channel_id=1, source_target_pairs={{0,16},{16,0},{1,17},{17,1},{2,18},{18,2},{3,19},{19,3},{4,20},{20... | collective-permute-start | bytes 786440 | tf_op jit(solution)/shard_map/ppermute | solution.py:415
  87.2 2.0 %shard_map.169 = (bf16[64,256]{1,0:T(8,128)(2,1)}, bf16[32,128]{1,0:T(8,128)(2,1)S(1)}) custom-call(s32[32]{0:T(128)S(1)} %copy-done.8, bf16[16,48,256]{2,1,0:T(8,128)(2,1)S(1)} %all_to_all.21.parts_ref.mine_ref, f32[64,256]{1,0:T(8,128)S(1)} %copy-done.4, f32[64,256]{1,0:T(8,128)S(1)} %copy-done.5, s32[2,128]{1,0:T(2,128)S(1)} %bitcast.19, ...), custom_call_target="tpu_custom_call" | custom-call | tf_op jit(solution)/shard_map/pallas_call | solution.py:417
  89.3 11.7 %all_to_all.22.sides_ref = bf16[16,32,128]{2,1,0:T(8,128)(2,1)S(1)} all-to-all(bf16[16,32,128]{2,1,0:T(8,128)(2,1)S(1)} %broadcast_in_dim.5), channel_id=1, replica_groups=mesh['q'=8,'c'=2,'z'=8,'x'=2] {'z','x'}, dimensions={0} | all-to-all | bytes 262144 | tf_op jit(solution)/shard_map/all_to_all | solution.py:305
  100.9 3.9 %collective-permute-start.6 = (bf16[16,16,128]{2,1,0:T(8,128)(2,1)S(1)}, bf16[16,16,128]{2,1,0:T(8,128)(2,1)S(1)}, u32[]{:S(2)}, u32[]{:S(2)}) collective-permute-start(bf16[16,16,128]{2,1,0:T(8,128)(2,1)S(1)} %slice.34), channel_id=1, source_target_pairs={{0,0},{1,16},{2,32},{3,48},{4,64},{5,80},{6,96},{7,112},{8,128},{9... | collective-permute-start | bytes 196616 | tf_op jit(solution)/shard_map/ppermute | solution.py:426
  104.8 0.7 shard_map.170
  105.5 13.0 %shard_map.171.mapped_ref = bf16[16,1024,256]{2,1,0:T(8,128)(2,1)S(1)} custom-call(bf16[16,32,128]{2,1,0:T(8,128)(2,1)S(1)} %all_to_all.22.sides_ref, bf16[128,4096]{1,0:T(8,128)(2,1)S(1)} %get-tuple-element.17.mapping_ref), custom_call_target="tpu_custom_call" | custom-call | flops 4294967296 | bytes 20971520 | tf_op jit(solution)/shard_map/pallas_call | solution.py:437
  118.6 4.8 %shard_map.172 = bf16[32,256,128]{2,1,0:T(8,128)(2,1)} custom-call(s32[32]{0:T(128)S(1)} %copy-done.8, s32[256]{0:T(256)S(1)} %copy-done.7, bf16[256,1024]{1,0:T(8,128)(2,1)S(1)} %get-tuple-element.15.factors_ref, bf16[16,16,128]{2,1,0:T(8,128)(2,1)S(1)} %collective-permute-done.6.band_ref, bf16[16,1024,256]{2,1,0:T(8,128)(2,1)S(1)} %shard_map.171.mapped_ref, ...), custom_call_target="tpu_custom_call" | custom-call | tf_op jit(solution)/shard_map/pallas_call | solution.py:447
  (31 shorter events, 0.1 us)
Async XLA Ops:
  27.0 16.4 %copy-start.10 = (bf16[2,32,256]{2,1,0:T(8,128)(2,1)S(1)}, bf16[2,32,256]{2,1,0:T(8,128)(2,1)}, u32[]{:S(2)}) copy-start(bf16[2,32,256]{2,1,0:T(8,128)(2,1)} %get-tuple-element.11) | copy-start | bytes 98308
  28.2 35.6 %all-to-all-start.1 = ((bf16[8,8,32,256]{3,2,1,0:T(8,128)(2,1)}), bf16[8,8,32,256]{3,2,1,0:T(8,128)(2,1)S(1)}, u32[]{:S(2)}, u32[]{:S(2)}) async-start(bf16[8,8,32,256]{3,2,1,0:T(8,128)(2,1)} %broadcast_in_dim.4), calls=%async_computation.1 | async-start | bytes 2097152 | tf_op jit(solution)/shard_map/all_to_all | solution.py:305
  37.2 50.0 %copy-start.2 = (bf16[256,256]{1,0:T(8,128)(2,1)S(1)}, bf16[256,256]{1,0:T(8,128)(2,1)}, u32[]{:S(2)}) copy-start(bf16[256,256]{1,0:T(8,128)(2,1)} %final_ref.1) | copy-start | bytes 393220
  37.2 50.0 %copy-start.3 = (bf16[256,32]{0,1:T(8,128)(2,1)S(1)}, bf16[256,32]{0,1:T(8,128)(2,1)}, u32[]{:S(2)}) copy-start(bf16[256,32]{0,1:T(8,128)(2,1)} %param.30) | copy-start | bytes 49156
  37.2 50.0 %copy-start.4 = (f32[64,256]{1,0:T(8,128)S(1)}, f32[64,256]{1,0:T(8,128)}, u32[]{:S(2)}) copy-start(f32[64,256]{1,0:T(8,128)} %get-tuple-element.12.gate_ref) | copy-start | bytes 196612
  37.2 50.0 %copy-start.5 = (f32[64,256]{1,0:T(8,128)S(1)}, f32[64,256]{1,0:T(8,128)}, u32[]{:S(2)}) copy-start(f32[64,256]{1,0:T(8,128)} %get-tuple-element.13.prior_ref) | copy-start | bytes 196612
  37.2 50.0 %copy-start.6 = (bf16[256,32]{0,1:T(8,128)(2,1)S(1)}, bf16[256,32]{0,1:T(8,128)(2,1)}, u32[]{:S(2)}) copy-start(bf16[256,32]{0,1:T(8,128)(2,1)} %param.29) | copy-start | bytes 49156
  37.2 50.0 %copy-start.7 = (s32[256]{0:T(256)S(1)}, s32[256]{0:T(256)}, u32[]{:S(2)}) copy-start(s32[256]{0:T(256)} %flags_ref.1) | copy-start | bytes 3076
  37.2 50.0 %copy-start.8 = (s32[32]{0:T(128)S(1)}, s32[32]{0:T(128)}, u32[]{:S(2)}) copy-start(s32[32]{0:T(128)} %live_ref.5) | copy-start | bytes 388
  37.3 50.0 %copy-start.9 = (f32[256]{0:T(256)S(1)}, f32[256]{0:T(256)}, u32[]{:S(2)}) copy-start(f32[256]{0:T(256)} %param.28) | copy-start | bytes 3076
  37.3 19.8 %collective-permute-start.2 = (bf16[8,144,256]{2,1,0:T(8,128)(2,1)}, bf16[8,144,256]{2,1,0:T(8,128)(2,1)S(1)}, u32[]{:S(2)}, u32[]{:S(2)}) collective-permute-start(bf16[8,144,256]{2,1,0:T(8,128)(2,1)} %slice.31), channel_id=1, source_target_pairs={{0,16},{1,0},{16,17},{17,1},{2,18},{3,2},{18,19},{19,3},{4,20},{5,... | collective-permute-start | bytes 1769480 | tf_op jit(solution)/shard_map/ppermute | solution.py:399
  37.7 19.4 %collective-permute-start.1 = (bf16[8,144,256]{2,1,0:T(8,128)(2,1)}, bf16[8,144,256]{2,1,0:T(8,128)(2,1)S(1)}, u32[]{:S(2)}, u32[]{:S(2)}) collective-permute-start(bf16[8,144,256]{2,1,0:T(8,128)(2,1)} %slice.31), channel_id=1, source_target_pairs={{0,0},{1,16},{16,1},{17,17},{2,2},{3,18},{18,3},{19,19},{4,4},{5,2... | collective-permute-start | bytes 1769480 | tf_op jit(solution)/shard_map/ppermute | solution.py:398
  43.4 13.7 %collective-permute-start = (bf16[8,16,128]{2,1,0:T(8,128)(2,1)S(1)}, bf16[8,16,128]{2,1,0:T(8,128)(2,1)S(1)}, u32[]{:S(2)}, u32[]{:S(2)}) collective-permute-start(bf16[8,16,128]{2,1,0:T(8,128)(2,1)S(1)} %slice.30.own_ref), channel_id=1, source_target_pairs={{0,1},{1,0},{2,3},{3,2},{4,5},{5,4},{6,7},{7,6},{8,9},{9,8},{10,11... | collective-permute-start | bytes 98312 | tf_op jit(solution)/shard_map/ppermute | solution.py:400
  43.5 4.0 %collective-permute-start.4 = (bf16[32,256]{1,0:T(8,128)(2,1)S(1)}, bf16[32,256]{1,0:T(8,128)(2,1)S(1)}, u32[]{:S(2)}, u32[]{:S(2)}) collective-permute-start(bf16[32,256]{1,0:T(8,128)(2,1)S(1)} %get-tuple-element.18), channel_id=1, source_target_pairs={{0,1},{1,17},{2,33},{3,49},{4,65},{5,81},{6,97},{7,113},{8,129},{9... | collective-permute-start | bytes 49160 | tf_op jit(solution)/shard_map/ppermute | solution.py:402
  44.0 60.9 %copy-start.1 = (bf16[1024,128]{1,0:T(8,128)(2,1)S(1)}, bf16[1024,128]{1,0:T(8,128)(2,1)}, u32[]{:S(2)}) copy-start(bf16[1024,128]{1,0:T(8,128)(2,1)} %map_ref.1) | copy-start | bytes 786436
  44.0 13.1 %collective-permute-start.3 = (bf16[32,256]{1,0:T(8,128)(2,1)S(1)}, bf16[32,256]{1,0:T(8,128)(2,1)S(1)}, u32[]{:S(2)}, u32[]{:S(2)}) collective-permute-start(bf16[32,256]{1,0:T(8,128)(2,1)S(1)} %get-tuple-element.19), channel_id=1, source_target_pairs={{0,0},{1,16},{2,32},{3,48},{4,64},{5,80},{6,96},{7,112},{8,128},{9... | collective-permute-start | bytes 49160 | tf_op jit(solution)/shard_map/ppermute | solution.py:401
  85.1 19.7 %collective-permute-start.5 = (bf16[16,32,256]{2,1,0:T(8,128)(2,1)S(1)}, bf16[16,32,256]{2,1,0:T(8,128)(2,1)S(1)}, u32[]{:S(2)}, u32[]{:S(2)}) collective-permute-start(bf16[16,32,256]{2,1,0:T(8,128)(2,1)S(1)} %slice.33), channel_id=1, source_target_pairs={{0,16},{16,0},{1,17},{17,1},{2,18},{18,2},{3,19},{19,3},{4,20},{20... | collective-permute-start | bytes 786440 | tf_op jit(solution)/shard_map/ppermute | solution.py:415
  100.9 17.6 %collective-permute-start.6 = (bf16[16,16,128]{2,1,0:T(8,128)(2,1)S(1)}, bf16[16,16,128]{2,1,0:T(8,128)(2,1)S(1)}, u32[]{:S(2)}, u32[]{:S(2)}) collective-permute-start(bf16[16,16,128]{2,1,0:T(8,128)(2,1)S(1)} %slice.34), channel_id=1, source_target_pairs={{0,0},{1,16},{2,32},{3,48},{4,64},{5,80},{6,96},{7,112},{8,128},{9... | collective-permute-start | bytes 196616 | tf_op jit(solution)/shard_map/ppermute | solution.py:426
  105.5 13.0 %copy-start = (bf16[32,256,128]{2,1,0:T(8,128)(2,1)S(1)}, bf16[32,256,128]{2,1,0:T(8,128)(2,1)}, u32[]{:S(2)}) copy-start(bf16[32,256,128]{2,1,0:T(8,128)(2,1)} %pair_ref.3) | copy-start | bytes 6291460

commit v3 on v2

--- a/solution.py
+++ b/solution.py
@@ -124,37 +124,27 @@
     return high, middle, rest - middle
 
 
-def attend_kernel(
-    own_ref, swapped_ref, kva_ref, kvb_ref, bias_ref, x0_ref, x1_ref, out_ref, extra_scr
-):
-    c, x = lax.axis_index("c"), lax.axis_index("x")
-    lane = lax.broadcasted_iota(jnp.int32, (128, 128), 1)
-    block, inner = lane // 32, lane % 32
-    first_x = jnp.where(x == 0, x0_ref[...], x1_ref[...])
-    second_x = jnp.where(x == 0, x1_ref[...], x0_ref[...])
-    for q in range(8):
-        out_ref[q, 0, 16:48, :] = first_x
-        out_ref[q, 1, 16:48, :] = second_x
-    mask = jnp.concatenate(
-        [kva_ref[k, 128 + i : 129 + i, 128:256].astype(F32) for k in range(8) for i in range(2)], axis=1
-    )
-    penalty = BIG * (mask - 1.0)
-    for g in range(2):
-        for k in range(8):
-            piece = bias_ref[k, :, g * 16 : g * 16 + 16, :].reshape(128, 256).astype(F32)
-            extra_scr[g, :, k * 256 : (k + 1) * 256] = piece + penalty[:, k * 256 : (k + 1) * 256]
+def attend_blocks(own_ref, swapped_ref, kva_ref, kvb_ref, blocks, extra_scr):
+    c, x, z = lax.axis_index("c"), lax.axis_index("x"), lax.axis_index("z")
+    places = [lax.rem(z + offset + 8, 8) for offset, _ in blocks]
+    block = lax.broadcasted_iota(jnp.int32, (128, 128), 1) // 32
+    for k, (place, (_, bias_ref)) in enumerate(zip(places, blocks)):
+        mask = jnp.concatenate(
+            [kva_ref[place, 128 + i : 129 + i, 128:256].astype(F32) for i in range(2)], axis=1
+        )
+        for g in range(2):
+            piece = bias_ref[:, g * 16 : g * 16 + 16, :].reshape(128, 256).astype(F32)
+            extra_scr[g, :, k * 256 : (k + 1) * 256] = piece + BIG * (mask - 1.0)
     own = own_ref[...].reshape(128, 128)
     swapped = swapped_ref[...].reshape(128, 128)
-    for a in range(2):
-        kv_ref = (kva_ref, kvb_ref)[a]
-        half = c ^ a
-        query = jnp.where(half == x, own, swapped).astype(F32)
-        keys = jnp.concatenate([kv_ref[k, 0:64, :] for k in range(8)], axis=1)
-        values = jnp.concatenate([kv_ref[k, 64:128, :] for k in range(8)], axis=1)
+    states = []
+    for a, kv_ref in enumerate((kva_ref, kvb_ref)):
+        query = jnp.where((c ^ a) == x, own, swapped).astype(F32)
+        keys = jnp.concatenate([kv_ref[place, 0:64, :] for place in places], axis=1)
+        values = jnp.concatenate([kv_ref[place, 64:128, :] for place in places], axis=1)
         keys = jnp.concatenate([keys, keys], axis=0)
         values = jnp.concatenate([values, values], axis=0)
-        mixed = jnp.zeros((128, 128), F32)
-        stats = jnp.zeros((128, 128), F32)
+        state = [jnp.zeros((128, 128), F32)] * 3
         for g in range(2):
             for s in range(2):
                 here = block == g * 2 + s
@@ -163,13 +153,43 @@
                 top = jnp.max(scores, axis=1, keepdims=True)
                 expo = jnp.exp(scores - top)
                 total = jnp.sum(expo, axis=1, keepdims=True)
-                part = dot(expo.astype(BF16), values, NT)
-                mixed = jnp.where(here, part / total, mixed)
-                for t, piece in enumerate(split3(top) + split3(total)):
-                    stats = jnp.where(here & (inner == t), piece, stats)
+                mixed = dot(expo.astype(BF16), values, NT)
+                state = [jnp.where(here, new, old) for new, old in zip((mixed, top, total), state)]
+        states.append(state)
+    return states
+
+
+def attend_kernel(own_ref, swapped_ref, kva_ref, kvb_ref, *refs):
+    *bias_refs, out_ref, extra_scr = refs
+    blocks = list(zip((0, -1, 1, -2, 2), bias_refs))
+    states = attend_blocks(own_ref, swapped_ref, kva_ref, kvb_ref, blocks, extra_scr)
+    for a in range(2):
+        for i in range(3):
+            out_ref[a, i] = states[a][i]
+
+
+def finish_kernel(own_ref, swapped_ref, kva_ref, kvb_ref, *refs):
+    *bias_refs, state_ref, x0_ref, x1_ref, out_ref, extra_scr = refs
+    c, x = lax.axis_index("c"), lax.axis_index("x")
+    for q in range(8):
+        out_ref[q, x, 16:48, :] = x0_ref[x]
+        out_ref[q, 1 - x, 16:48, :] = x1_ref[x]
+    inner = lax.broadcasted_iota(jnp.int32, (128, 128), 1) % 32
+    blocks = list(zip((-3, 3, -4), bias_refs))
+    states = attend_blocks(own_ref, swapped_ref, kva_ref, kvb_ref, blocks, extra_scr)
+    for a in range(2):
+        mixed, top, total = states[a]
+        other_mixed, other_top, other_total = (state_ref[a, i] for i in range(3))
+        best = jnp.maximum(top, other_top)
+        weight, other_weight = jnp.exp(top - best), jnp.exp(other_top - best)
+        total = total * weight + other_total * other_weight
+        mixed = (mixed * weight + other_mixed * other_weight) / total
+        stats = jnp.zeros((128, 128), F32)
+        for t, piece in enumerate(split3(best) + split3(total)):
+            stats = jnp.where(inner == t, piece, stats)
         joined = jnp.concatenate([mixed, stats], axis=1).astype(BF16)
         for q in range(8):
-            out_ref[q, half, 0:16, :] = joined[q * 16 : q * 16 + 16]
+            out_ref[q, c ^ a, 0:16, :] = joined[q * 16 : q * 16 + 16]
 
 
 def refresh_kernel(
@@ -224,19 +244,27 @@
         sides_ref[i * 16 : i * 16 + 16, :] = jnp.concatenate(parts, axis=1).astype(BF16)
 
 
-def pack_kernel(mine_ref, theirs_ref, map_ref, factors_ref, mapping_ref, scr):
+def pack_kernel(mine_ref, theirs_ref, factors_ref, factor_scr):
     swapped = lax.axis_index("c") == 1
-    rows = []
     for q in range(8):
         for c in range(2):
             for x in range(2):
                 mine = mine_ref[2 * q + x, 16:48, :].astype(F32)
                 theirs = theirs_ref[2 * q + x].astype(F32)
-                rows.append(jnp.where(swapped == (c == 1), mine, theirs))
-    for i in range(8):
-        factors_ref[:, i * 128 : (i + 1) * 128] = jnp.concatenate(
-            rows[i * 4 : i * 4 + 4], axis=0
-        ).T.astype(BF16)
+                piece = jnp.where(swapped == (c == 1), mine, theirs)
+                place = (x * 16 + 2 * q + c) * 32
+                for i in range(2):
+                    factor_scr[i, place : place + 32, :] = piece[:, i * 128 : i * 128 + 128]
+    for k in range(8):
+        rows = []
+        for d in range(k * 4, k * 4 + 4):
+            rows.append(
+                jnp.concatenate([factor_scr[i, pl.ds(d, 32, stride=32), :] for i in range(2)], axis=1)
+            )
+        factors_ref[:, k * 128 : (k + 1) * 128] = jnp.concatenate(rows, axis=0).T.astype(BF16)
+
+
+def line_kernel(map_ref, mapping_ref, scr):
     scr[...] = map_ref[...].astype(F32)
     for d in range(32):
         piece = scr[pl.ds(d, 32, stride=32), :].astype(BF16)
@@ -244,7 +272,7 @@
             mapping_ref[k * 32 : k * 32 + 32, d * 128 : (d + 1) * 128] = piece
 
 
-def map_kernel(sides_ref, mapping_ref, out_ref, side_scr, scr):
+def map_kernel(sides_ref, mapping_ref, out_ref, side_scr):
     step = pl.program_id(0)
 
     @pl.when(step == 0)
@@ -261,43 +289,58 @@
             lefts.append(jnp.where(block == group * 2 + s, lined, 0.0))
     left = jnp.concatenate(lefts, axis=0).astype(BF16)
     for d in range(0, 32, 2):
-        mapped = dot(left, mapping_ref[:, d * 128 : (d + 2) * 128], NN)
+        mapped = dot(left, mapping_ref[:, d * 128 : (d + 2) * 128], NN).astype(BF16)
         for e in range(2):
             for r in range(8):
-                for s in range(2):
-                    scr[r, pl.ds(s * 32 + d + e, 16, stride=64), :] = mapped[
-                        r * 32 + s * 16 : r * 32 + s * 16 + 16, e * 128 : e * 128 + 128
-                    ]
-    for r in range(8):
-        out_ref[r // 2, :, (r % 2) * 128 : (r % 2) * 128 + 128] = scr[r].astype(BF16)
-
-
-def outer_kernel(live_ref, flags_ref, factors_ref, band_ref, mapped_ref, pair_ref, out_ref, scr, full_scr):
-    step = pl.program_id(0)
-    rows = pair_ref.shape[0]
-
-    @pl.when(step == 0)
-    def _():
-        for i in range(8):
-            scr[...] = factors_ref[:, i * 128 : (i + 1) * 128].astype(F32)
-            pair = [band_ref[2 * i + n].astype(F32) for n in range(2)]
-            band = jnp.concatenate(
-                [jnp.concatenate([p[:, g * 64 : g * 64 + 64] for p in pair], axis=1) for g in range(2)], axis=0
-            )
-            scr[pl.ds(0, 32, stride=8), :] = band
-            full_scr[:, i * 128 : (i + 1) * 128] = scr[...].astype(BF16)
+                out_ref[r // 2, (d + e) * 32 : (d + e) * 32 + 32, (r % 2) * 128 : (r % 2) * 128 + 128] = (
+                    mapped[r * 32 : r * 32 + 32, e * 128 : e * 128 + 128]
+                )
+
+
+def outer_kernel(
+    live_ref,
+    flags_ref,
+    factors_ref,
+    band_ref,
+    mapped_ref,
+    pair_ref,
+    out_ref,
+    scr,
+    band_scr,
+    full_scr,
+    done_scr,
+    sems,
+):
+    turned = jnp.concatenate([band_ref[n].astype(F32) for n in range(16)], axis=0).T
+    empty = jnp.zeros((32, 96), F32)
+    for s in range(2):
+        for n in range(16):
+            parts = [
+                turned[g * 64 + s * 32 : g * 64 + s * 32 + 32, n * 16 : n * 16 + 16] for g in range(2)
+            ]
+            band_scr[pl.ds(s * 16 + n, 32, stride=32), :] = jnp.concatenate(parts + [empty], axis=1)
+    for i in range(8):
+        scr[i] = factors_ref[:, i * 128 : (i + 1) * 128].astype(F32)
+        scr[i, pl.ds(0, 32, stride=8), :] = band_scr[i * 128 : (i + 1) * 128, :].T[0:32]
+        full_scr[:, i * 128 : (i + 1) * 128] = scr[i].astype(BF16)
 
     nvalid = jnp.int32(0)
     for s in range(32):
         nvalid += live_ref[s]
-    for r in range(0, rows, 2):
-        projected = dot(full_scr[...], mapped_ref[r // 2], NN)
-        for i in range(2):
-            flag = flags_ref[(step * rows + r + i) * 8]
-            scale = 1.0 / jnp.maximum((nvalid * flag).astype(F32), 1.0)
-            out_ref[r + i] = (
-                pair_ref[r + i].astype(F32) + projected[:, i * 128 : (i + 1) * 128] * scale
-            ).astype(BF16)
+    copies = []
+    for k in range(8):
+        for r in range(k * 4, k * 4 + 4, 2):
+            projected = dot(full_scr[...], mapped_ref[r // 2], NN)
+            for i in range(2):
+                scale = 1.0 / jnp.maximum((nvalid * flags_ref[(r + i) * 8]).astype(F32), 1.0)
+                done_scr[r + i] = (
+                    pair_ref[r + i].astype(F32) + projected[:, i * 128 : (i + 1) * 128] * scale
+                ).astype(BF16)
+        part = pl.ds(k * 4, 4)
+        copies.append(pltpu.make_async_copy(done_scr.at[part], out_ref.at[part], sems.at[k]))
+        copies[-1].start()
+    for copy in copies:
+        copy.wait()
 
 
 def gather(value, axes, count):
@@ -318,10 +361,11 @@
 
 
 MIRROR = [(w * 16 + n, n * 16 + w) for w in range(16) for n in range(16)]
-MIRROR_NEXT = [(w * 16 + n, n * 16 + (w ^ 1)) for w in range(16) for n in range(16)]
 ACROSS = [(a * 2 + b, b * 2 + a) for a in range(2) for b in range(2)]
 ACROSS_NEXT = [(a * 2 + b, (1 - b) * 2 + a) for a in range(2) for b in range(2)]
 SWAP = [(0, 1), (1, 0)]
+UP = [(i, (i + 1) % 8) for i in range(8)]
+DOWN = [(i, (i + 7) % 8) for i in range(8)]
 
 
 def local(
@@ -342,7 +386,6 @@
     other_factor_matrix,
     product_mapping_matrix,
 ):
-    c = lax.axis_index("c")
     g2 = product_scale_vector.reshape(1, 256)
     flags = position_valid_flags.reshape(2, 128)
     first, other = first_factor_matrix.T, other_factor_matrix.T
@@ -393,26 +436,49 @@
     )
 
     heads = lax.all_to_all(message, "q", 0, 0, tiled=True)
+    x0 = lax.ppermute(right, ALL, MIRROR)
+    mapping = pl.pallas_call(
+        line_kernel,
+        in_specs=[ARRAY],
+        out_specs=ARRAY,
+        out_shape=jax.ShapeDtypeStruct((128, 4096), BF16),
+        scratch_shapes=[pltpu.VMEM((1024, 128), F32)],
+        compiler_params=params(),
+    )(product_mapping_matrix)
+    heads, x0, mapping = lax.optimization_barrier((heads, x0, mapping))
     kv = heads[:, 32:176, :]
     own = heads[:, 160:176, 0:128]
     kva = lax.ppermute(kv, ("c", "x"), ACROSS)
     kvb = lax.ppermute(kv, ("c", "x"), ACROSS_NEXT)
     swapped = lax.ppermute(own, "x", SWAP)
-    x0 = lax.ppermute(jnp.where(c == 0, right[0], right[1]), ALL, MIRROR)
-    x1 = lax.ppermute(jnp.where(c == 0, right[1], right[0]), ALL, MIRROR_NEXT)
-    bias = gather(heads[:, 0:32, :], "z", 8)
-
+    x1 = lax.ppermute(x0, "x", SWAP)
+    below, above = [heads[:, 0:32, :]], [heads[:, 0:32, :]]
+    for step in range(4):
+        below.append(lax.ppermute(below[-1], "z", UP))
+        if step < 3:
+            above.append(lax.ppermute(above[-1], "z", DOWN))
+        if step == 1:
+            below[2], swapped = lax.optimization_barrier((below[2], swapped))
+
+
+    state = pl.pallas_call(
+        attend_kernel,
+        in_specs=[ARRAY] * 9,
+        out_specs=ARRAY,
+        out_shape=jax.ShapeDtypeStruct((2, 3, 128, 128), F32),
+        scratch_shapes=[pltpu.VMEM((2, 128, 5 * 256), F32)],
+        compiler_params=params(),
+    )(own, swapped, kva, kvb, below[0], below[1], above[1], below[2], above[2])
     parts = pl.pallas_call(
-        attend_kernel,
-        in_specs=[ARRAY] * 7,
+        finish_kernel,
+        in_specs=[ARRAY] * 10,
         out_specs=ARRAY,
         out_shape=jax.ShapeDtypeStruct((8, 2, 48, 256), BF16),
-        scratch_shapes=[pltpu.VMEM((2, 128, 2048), F32)],
-        compiler_params=params(),
-    )(own, swapped, kva, kvb, bias, x0, x1)
+        scratch_shapes=[pltpu.VMEM((2, 128, 3 * 256), F32)],
+        compiler_params=params(),
+    )(own, swapped, kva, kvb, below[3], above[3], below[4], state, x0, x1)
 
     parts = lax.all_to_all(parts.reshape(16, 48, 256), ("q", "x"), 0, 0, tiled=True)
-    theirs = lax.ppermute(parts[:, 16:48, :], "c", SWAP)
 
     fresh, sides = pl.pallas_call(
         refresh_kernel,
@@ -424,40 +490,39 @@
 
     sides = gather(sides, ("z", "x"), 16)
     band = lax.ppermute(sides[:, 16:32, :], ALL, MIRROR)
-
-    factors, mapping = pl.pallas_call(
+    parts, sides = lax.optimization_barrier((parts, sides))
+    theirs = lax.ppermute(parts[:, 16:48, :], "c", SWAP)
+    factors = pl.pallas_call(
         pack_kernel,
-        in_specs=[ARRAY] * 3,
-        out_specs=[ARRAY] * 2,
-        out_shape=[jax.ShapeDtypeStruct((256, 1024), BF16), jax.ShapeDtypeStruct((128, 4096), BF16)],
-        scratch_shapes=[pltpu.VMEM((1024, 128), F32)],
-        cost_estimate=pl.CostEstimate(flops=0, bytes_accessed=12 << 20, transcendentals=0),
-        compiler_params=params(),
-    )(parts, theirs, product_mapping_matrix)
+        in_specs=[ARRAY] * 2,
+        out_specs=ARRAY,
+        out_shape=jax.ShapeDtypeStruct((256, 1024), BF16),
+        scratch_shapes=[pltpu.VMEM((2, 1024, 128), F32)],
+        cost_estimate=pl.CostEstimate(flops=0, bytes_accessed=4 << 20, transcendentals=0),
+        compiler_params=params(),
+    )(parts, theirs)
     mapped = pl.pallas_call(
         map_kernel,
         grid=(4,),
         in_specs=[whole((16, 32, 128)), whole((128, 4096))],
         out_specs=pl.BlockSpec((4, 1024, 256), lambda i: (i, 0, 0)),
         out_shape=jax.ShapeDtypeStruct((16, 1024, 256), BF16),
-        scratch_shapes=[pltpu.VMEM((256, 128), F32), pltpu.VMEM((8, 1024, 128), F32)],
+        scratch_shapes=[pltpu.VMEM((256, 128), F32)],
         cost_estimate=pl.CostEstimate(flops=4 << 30, bytes_accessed=20 << 20, transcendentals=0),
         compiler_params=params(),
     )(sides, mapping)
     pair_out = pl.pallas_call(
         outer_kernel,
-        grid=(4,),
-        in_specs=[
-            SCALARS,
-            SCALARS,
-            whole((256, 1024)),
-            whole((16, 16, 128)),
-            pl.BlockSpec((4, 1024, 256), lambda i: (i, 0, 0)),
-            pl.BlockSpec((8, 256, 128), lambda i: (i, 0, 0)),
+        in_specs=[SCALARS] * 2 + [ARRAY] * 4,
+        out_specs=pl.BlockSpec(memory_space=pl.ANY),
+        out_shape=jax.ShapeDtypeStruct((32, 256, 128), BF16),
+        scratch_shapes=[
+            pltpu.VMEM((8, 256, 128), F32),
+            pltpu.VMEM((1024, 128), F32),
+            pltpu.VMEM((256, 1024), BF16),
+            pltpu.VMEM((32, 256, 128), BF16),
+            pltpu.SemaphoreType.DMA((8,)),
         ],
-        out_specs=pl.BlockSpec((8, 256, 128), lambda i: (i, 0, 0)),
-        out_shape=jax.ShapeDtypeStruct((32, 256, 128), BF16),
-        scratch_shapes=[pltpu.VMEM((256, 128), F32), pltpu.VMEM((256, 1024), BF16)],
         compiler_params=params(),
     )(sequence_valid_flags, position_valid_flags, factors, band, mapped, couple_activity)
     return fresh.reshape(2, 32, 256), pair_out

time: 124 us -> 111 us (0.90)
  the two profiles are of different devices: /device:TPU:1 before, /device:TPU:48 now
where the time goes in v3:
time: 111 us; the launch traced here: 109 us
  starting transfers between devices  35.6 us (32%)
  blocking collectives  30 us (27%)
  waiting for transfers between devices  21.5 us (19%)
  Pallas kernels  21.1 us (19%)
    all_to_all x1, blocking collectives, gather(): return lax.all_to_all(tiled, axes, 0, 0, tiled=True)  16.1 us
    all_to_all x1, blocking collectives, local(): lax.all_to_all(parts.reshape(16, 48, 256), ('q', 'x'), 0, 0, tiled=True)  13.8 us
    ppermute x1, starting transfers between devices, local(): x0 = lax.ppermute(right, ALL, MIRROR)  10.1 us
    all_to_all x1, starting transfers between devices, local(): heads = lax.all_to_all(message, 'q', 0, 0, tiled=True)  7.26 us
    ppermute x4, waiting for transfers between devices, local(): below.append(lax.ppermute(below[-1], 'z', UP))  6.83 us
    pallas_call x1, Pallas kernels, local(): pl.pallas_call(front_kernel, grid=(4,), in_specs=[SCALARS, pl.BlockSpec((...  6.45 us
    ppermute x1, waiting for transfers between devices, local(): band = lax.ppermute(sides[:, 16:32, :], ALL, MIRROR)  5.52 us
    ppermute x3, starting transfers between devices, local(): above.append(lax.ppermute(above[-1], 'z', DOWN))  5.09 us
  transfers between devices with their start and end apart: 15, of which 8 were waited for; matrix products, arithmetic and copies ran while one was open for 0% of the time, Pallas kernels for 6%

profile of v3, /device:TPU:48, one launch (start us, length us, event | category | flops | bytes accessed | tf_op | source)
XLA Modules:
  0.0 109.4 jit_solution(15073314170050552520)
XLA Ops:
  0.6 6.4 %shard_map.167 = (bf16[8,176,256]{2,1,0:T(8,128)(2,1)}, f32[64,256]{1,0:T(8,128)}, f32[64,256]{1,0:T(8,128)}, bf16[2,32,256]{2,1,0:T(8,128)(2,1)}) custom-call(s32[32]{0:T(128)} %live_ref.5, bf16[32,256,128]{2,1,0:T(8,128)(2,1)} %pair_ref.3, bf16[512,256]{1,0:T(8,128)(2,1)} %bitcast.18, s32[2,128]{1,0:T(2,128)} %bitcast.14, f32[1,256]{1,0:T(1,128)} %bitcast.20, ...), custom_call_target="tpu_custom_call" | custom-call | tf_op jit(solution)/shard_map/pallas_call | solution.py:393
  7.1 7.3 %all-to-all-start = ((bf16[8,176,256]{2,1,0:T(8,128)(2,1)}), bf16[8,176,256]{2,1,0:T(8,128)(2,1)S(1)}, u32[]{:S(2)}, u32[]{:S(2)}) async-start(bf16[8,176,256]{2,1,0:T(8,128)(2,1)} %get-tuple-element.15), calls=%async_computation | async-start | bytes 1441792 | tf_op jit(solution)/shard_map/all_to_all | solution.py:438
  14.4 10.1 %collective-permute-start = (bf16[2,32,256]{2,1,0:T(8,128)(2,1)}, bf16[2,32,256]{2,1,0:T(8,128)(2,1)S(1)}, u32[]{:S(2)}, u32[]{:S(2)}) collective-permute-start(bf16[2,32,256]{2,1,0:T(8,128)(2,1)} %get-tuple-element.16), channel_id=1, source_target_pairs={{0,0},{1,16},{2,32},{3,48},{4,64},{5,80},{6,96},{7,112},{8,128},{9... | collective-permute-start | bytes 98312 | tf_op jit(solution)/shard_map/ppermute | solution.py:439
  25.0 3.5 %collective-permute-done.refs_4_ = bf16[2,32,256]{2,1,0:T(8,128)(2,1)S(1)} collective-permute-done((bf16[2,32,256]{2,1,0:T(8,128)(2,1)}, bf16[2,32,256]{2,1,0:T(8,128)(2,1)S(1)}, u32[]{:S(2)}, u32[]{:S(2)}) %collective-permute-start) | collective-permute-done | bytes 32800 | tf_op jit(solution)/shard_map/ppermute | solution.py:439
  29.5 2.0 %collective-permute-start.7 = (bf16[8,32,256]{2,1,0:T(8,128)(2,1)S(1)}, bf16[8,32,256]{2,1,0:T(8,128)(2,1)S(1)}, u32[]{:S(2)}, u32[]{:S(2)}) collective-permute-start(bf16[8,32,256]{2,1,0:T(8,128)(2,1)S(1)} %slice.17.refs_0_), channel_id=1, source_target_pairs={{0,14},{2,0},{4,2},{6,4},{8,6},{10,8},{12,10},{14,12},{1,15},{3,1}... | collective-permute-start | bytes 393224 | tf_op jit(solution)/shard_map/ppermute | solution.py:459
  31.5 2.9 %collective-permute-done.1.refs_1_ = bf16[8,32,256]{2,1,0:T(8,128)(2,1)S(1)} collective-permute-done((bf16[8,32,256]{2,1,0:T(8,128)(2,1)S(1)}, bf16[8,32,256]{2,1,0:T(8,128)(2,1)S(1)}, u32[]{:S(2)}, u32[]{:S(2)}) %collective-permute-start.1) | collective-permute-done | bytes 131104 | tf_op jit(solution)/shard_map/ppermute | solution.py:457
  34.4 1.7 %collective-permute-start.2 = (bf16[8,32,256]{2,1,0:T(8,128)(2,1)S(1)}, bf16[8,32,256]{2,1,0:T(8,128)(2,1)S(1)}, u32[]{:S(2)}, u32[]{:S(2)}) collective-permute-start(bf16[8,32,256]{2,1,0:T(8,128)(2,1)S(1)} %collective-permute-done.1.refs_1_), channel_id=1, source_target_pairs={{0,2},{2,4},{4,6},{6,8},{8,10},{10,12},{12,14},{14,0},{1,3},{3,5},... | collective-permute-start | bytes 393224 | tf_op jit(solution)/shard_map/ppermute | solution.py:457
  36.1 4.1 %collective-permute-start.3 = (bf16[8,16,128]{2,1,0:T(8,128)(2,1)S(1)}, bf16[8,16,128]{2,1,0:T(8,128)(2,1)S(1)}, u32[]{:S(2)}, u32[]{:S(2)}) collective-permute-start(bf16[8,16,128]{2,1,0:T(8,128)(2,1)S(1)} %slice.16.own_ref), channel_id=1, source_target_pairs={{0,1},{1,0},{2,3},{3,2},{4,5},{5,4},{6,7},{7,6},{8,9},{9,8},{10,11... | collective-permute-start | bytes 98312 | tf_op jit(solution)/shard_map/ppermute | solution.py:453
  40.2 1.2 %collective-permute-start.8 = (bf16[8,32,256]{2,1,0:T(8,128)(2,1)S(1)}, bf16[8,32,256]{2,1,0:T(8,128)(2,1)S(1)}, u32[]{:S(2)}, u32[]{:S(2)}) collective-permute-start(bf16[8,32,256]{2,1,0:T(8,128)(2,1)S(1)} %collective-permute-done.7.refs_2_), channel_id=1, source_target_pairs={{0,14},{2,0},{4,2},{6,4},{8,6},{10,8},{12,10},{14,12},{1,15},{3,1}... | collective-permute-start | bytes 393224 | tf_op jit(solution)/shard_map/ppermute | solution.py:459
  41.4 4.1 %collective-permute-done.3.swapped_ref = bf16[8,16,128]{2,1,0:T(8,128)(2,1)S(1)} collective-permute-done((bf16[8,16,128]{2,1,0:T(8,128)(2,1)S(1)}, bf16[8,16,128]{2,1,0:T(8,128)(2,1)S(1)}, u32[]{:S(2)}, u32[]{:S(2)}) %collective-permute-start.3) | collective-permute-done | bytes 32800 | tf_op jit(solution)/shard_map/ppermute | solution.py:453
  45.7 1.9 %collective-permute-start.9 = (bf16[8,32,256]{2,1,0:T(8,128)(2,1)S(1)}, bf16[8,32,256]{2,1,0:T(8,128)(2,1)S(1)}, u32[]{:S(2)}, u32[]{:S(2)}) collective-permute-start(bf16[8,32,256]{2,1,0:T(8,128)(2,1)S(1)} %collective-permute-done.8.refs_4_), channel_id=1, source_target_pairs={{0,14},{2,0},{4,2},{6,4},{8,6},{10,8},{12,10},{14,12},{1,15},{3,1}... | collective-permute-start | bytes 393224 | tf_op jit(solution)/shard_map/ppermute | solution.py:459
  47.6 2.9 %collective-permute-done.6.refs_0_ = bf16[8,32,256]{2,1,0:T(8,128)(2,1)S(1)} collective-permute-done((bf16[8,32,256]{2,1,0:T(8,128)(2,1)S(1)}, bf16[8,32,256]{2,1,0:T(8,128)(2,1)S(1)}, u32[]{:S(2)}, u32[]{:S(2)}) %collective-permute-start.6) | collective-permute-done | bytes 131104 | tf_op jit(solution)/shard_map/ppermute | solution.py:457
  50.5 1.7 %collective-permute-start.10 = (bf16[8,32,256]{2,1,0:T(8,128)(2,1)S(1)}, bf16[8,32,256]{2,1,0:T(8,128)(2,1)S(1)}, u32[]{:S(2)}, u32[]{:S(2)}) collective-permute-start(bf16[8,32,256]{2,1,0:T(8,128)(2,1)S(1)} %collective-permute-done.6.refs_0_), channel_id=1, source_target_pairs={{0,2},{2,4},{4,6},{6,8},{8,10},{10,12},{12,14},{14,0},{1,3},{3,5},... | collective-permute-start | bytes 393224 | tf_op jit(solution)/shard_map/ppermute | solution.py:457
  52.2 2.5 %shard_map.169.refs_3_ = f32[2,3,128,128]{3,2,1,0:T(8,128)S(1)} custom-call(bf16[8,16,128]{2,1,0:T(8,128)(2,1)S(1)} %slice.16.own_ref, bf16[8,16,128]{2,1,0:T(8,128)(2,1)S(1)} %collective-permute-done.3.swapped_ref, bf16[8,144,256]{2,1,0:T(8,128)(2,1)S(1)} %collective-permute-done.4.kva_ref, bf16[8,144,256]{2,1,0:T(8,128)(2,1)S(1)} %collective-permute-done.5.kvb_ref, ...), custom_call_target="tpu_custom_call" | custom-call | tf_op jit(solution)/shard_map/pallas_call | solution.py:464
  54.8 1.4 %collective-permute-done.11.refs_5_ = bf16[2,32,256]{2,1,0:T(8,128)(2,1)S(1)} collective-permute-done((bf16[2,32,256]{2,1,0:T(8,128)(2,1)S(1)}, bf16[2,32,256]{2,1,0:T(8,128)(2,1)S(1)}, u32[]{:S(2)}, u32[]{:S(2)}) %collective-permute-start.11) | collective-permute-done | bytes 32800 | tf_op jit(solution)/shard_map/ppermute | solution.py:454
  56.1 0.9 collective-permute-done.10.refs_2_
  57.1 1.6 %shard_map.170 = bf16[8,2,48,256]{3,2,1,0:T(8,128)(2,1)S(1)} custom-call(bf16[8,16,128]{2,1,0:T(8,128)(2,1)S(1)} %slice.16.own_ref, bf16[8,16,128]{2,1,0:T(8,128)(2,1)S(1)} %collective-permute-done.3.swapped_ref, bf16[8,144,256]{2,1,0:T(8,128)(2,1)S(1)} %collective-permute-done.4.kva_ref, bf16[8,144,256]{2,1,0:T(8,128)(2,1)S(1)} %collective-permute-done.5.kvb_ref, ...), custom_call_target="tpu_custom_call" | custom-call | tf_op jit(solution)/shard_map/pallas_call | solution.py:472
  58.7 13.8 %all_to_all.15.parts_ref.mine_ref = bf16[16,48,256]{2,1,0:T(8,128)(2,1)S(1)} all-to-all(bf16[16,48,256]{2,1,0:T(8,128)(2,1)S(1)} %bitcast.10), channel_id=1, replica_groups=mesh['q'=8,'c'=2,'z'=8,'x'=2] {'q','x'}, dimensions={0} | all-to-all | bytes 786432 | tf_op jit(solution)/shard_map/all_to_all | solution.py:481
  72.6 2.0 %shard_map.171 = (bf16[64,256]{1,0:T(8,128)(2,1)}, bf16[32,128]{1,0:T(8,128)(2,1)S(1)}) custom-call(s32[32]{0:T(128)S(1)} %copy-done.8, bf16[16,48,256]{2,1,0:T(8,128)(2,1)S(1)} %all_to_all.15.parts_ref.mine_ref, f32[64,256]{1,0:T(8,128)S(1)} %copy-done.4, f32[64,256]{1,0:T(8,128)S(1)} %copy-done.5, s32[2,128]{1,0:T(2,128)S(1)} %bitcast.15, ...), custom_call_target="tpu_custom_call" | custom-call | tf_op jit(solution)/shard_map/pallas_call | solution.py:483
  74.6 16.1 %all_to_all.16.sides_ref = bf16[16,32,128]{2,1,0:T(8,128)(2,1)S(1)} all-to-all(bf16[16,32,128]{2,1,0:T(8,128)(2,1)S(1)} %broadcast_in_dim.2), channel_id=1, replica_groups=mesh['q'=8,'c'=2,'z'=8,'x'=2] {'z','x'}, dimensions={0} | all-to-all | bytes 262144 | tf_op jit(solution)/shard_map/all_to_all | solution.py:348
  90.8 4.6 %collective-permute-start.13 = (bf16[16,16,128]{2,1,0:T(8,128)(2,1)S(1)}, bf16[16,16,128]{2,1,0:T(8,128)(2,1)S(1)}, u32[]{:S(2)}, u32[]{:S(2)}) collective-permute-start(bf16[16,16,128]{2,1,0:T(8,128)(2,1)S(1)} %slice.21), channel_id=1, source_target_pairs={{0,0},{1,16},{2,32},{3,48},{4,64},{5,80},{6,96},{7,112},{8,128},{9... | collective-permute-start | bytes 196616 | tf_op jit(solution)/shard_map/ppermute | solution.py:492
  95.5 2.8 %shard_map.173.mapped_ref = bf16[16,1024,256]{2,1,0:T(8,128)(2,1)S(1)} custom-call(bf16[16,32,128]{2,1,0:T(8,128)(2,1)S(1)} %all_to_all.16.sides_ref, bf16[128,4096]{1,0:T(8,128)(2,1)S(1)} %shard_map.168.mapping_ref), custom_call_target="tpu_custom_call" | custom-call | flops 4294967296 | bytes 20971520 | tf_op jit(solution)/shard_map/pallas_call | solution.py:504
  99.2 5.5 %collective-permute-done.13.band_ref = bf16[16,16,128]{2,1,0:T(8,128)(2,1)S(1)} collective-permute-done((bf16[16,16,128]{2,1,0:T(8,128)(2,1)S(1)}, bf16[16,16,128]{2,1,0:T(8,128)(2,1)S(1)}, u32[]{:S(2)}, u32[]{:S(2)}) %collective-permute-start.13) | collective-permute-done | bytes 65568 | tf_op jit(solution)/shard_map/ppermute | solution.py:492
  104.7 4.5 %shard_map.174 = bf16[32,256,128]{2,1,0:T(8,128)(2,1)} custom-call(s32[32]{0:T(128)S(1)} %copy-done.8, s32[256]{0:T(256)S(1)} %copy-done.7, bf16[256,1024]{1,0:T(8,128)(2,1)S(1)} %shard_map.172.factors_ref, bf16[16,16,128]{2,1,0:T(8,128)(2,1)S(1)} %collective-permute-done.13.band_ref, bf16[16,1024,256]{2,1,0:T(8,128)(2,1)S(1)} %shard_map.173.mapped_ref, ...), custom_call_target="tpu_custom_call" | custom-call | tf_op jit(solution)/shard_map/pallas_call | solution.py:514
  (42 shorter events, 2.5 us)
Async XLA Ops:
  0.6 23.9 %copy-start.1 = (bf16[1024,128]{1,0:T(8,128)(2,1)S(1)}, bf16[1024,128]{1,0:T(8,128)(2,1)}, u32[]{:S(2)}) copy-start(bf16[1024,128]{1,0:T(8,128)(2,1)} %map_ref.1) | copy-start | bytes 786436
  7.1 21.4 %all-to-all-start = ((bf16[8,176,256]{2,1,0:T(8,128)(2,1)}), bf16[8,176,256]{2,1,0:T(8,128)(2,1)S(1)}, u32[]{:S(2)}, u32[]{:S(2)}) async-start(bf16[8,176,256]{2,1,0:T(8,128)(2,1)} %get-tuple-element.15), calls=%async_computation | async-start | bytes 1441792 | tf_op jit(solution)/shard_map/all_to_all | solution.py:438
  14.4 14.1 %collective-permute-start = (bf16[2,32,256]{2,1,0:T(8,128)(2,1)}, bf16[2,32,256]{2,1,0:T(8,128)(2,1)S(1)}, u32[]{:S(2)}, u32[]{:S(2)}) collective-permute-start(bf16[2,32,256]{2,1,0:T(8,128)(2,1)} %get-tuple-element.16), channel_id=1, source_target_pairs={{0,0},{1,16},{2,32},{3,48},{4,64},{5,80},{6,96},{7,112},{8,128},{9... | collective-permute-start | bytes 98312 | tf_op jit(solution)/shard_map/ppermute | solution.py:439
  28.5 23.7 %collective-permute-start.5 = (bf16[8,144,256]{2,1,0:T(8,128)(2,1)S(1)}, bf16[8,144,256]{2,1,0:T(8,128)(2,1)S(1)}, u32[]{:S(2)}, u32[]{:S(2)}) collective-permute-start(bf16[8,144,256]{2,1,0:T(8,128)(2,1)S(1)} %slice.18), channel_id=1, source_target_pairs={{0,16},{1,0},{16,17},{17,1},{2,18},{3,2},{18,19},{19,3},{4,20},{5,... | collective-permute-start | bytes 1769480 | tf_op jit(solution)/shard_map/ppermute | solution.py:452
  28.6 23.6 %collective-permute-start.4 = (bf16[8,144,256]{2,1,0:T(8,128)(2,1)S(1)}, bf16[8,144,256]{2,1,0:T(8,128)(2,1)S(1)}, u32[]{:S(2)}, u32[]{:S(2)}) collective-permute-start(bf16[8,144,256]{2,1,0:T(8,128)(2,1)S(1)} %slice.18), channel_id=1, source_target_pairs={{0,0},{1,16},{16,1},{17,17},{2,2},{3,18},{18,3},{19,19},{4,4},{5,2... | collective-permute-start | bytes 1769480 | tf_op jit(solution)/shard_map/ppermute | solution.py:451
  29.4 5.0 %collective-permute-start.1 = (bf16[8,32,256]{2,1,0:T(8,128)(2,1)S(1)}, bf16[8,32,256]{2,1,0:T(8,128)(2,1)S(1)}, u32[]{:S(2)}, u32[]{:S(2)}) collective-permute-start(bf16[8,32,256]{2,1,0:T(8,128)(2,1)S(1)} %slice.17.refs_0_), channel_id=1, source_target_pairs={{0,2},{2,4},{4,6},{6,8},{8,10},{10,12},{12,14},{14,0},{1,3},{3,5},... | collective-permute-start | bytes 393224 | tf_op jit(solution)/shard_map/ppermute | solution.py:457
  29.5 10.8 %collective-permute-start.7 = (bf16[8,32,256]{2,1,0:T(8,128)(2,1)S(1)}, bf16[8,32,256]{2,1,0:T(8,128)(2,1)S(1)}, u32[]{:S(2)}, u32[]{:S(2)}) collective-permute-start(bf16[8,32,256]{2,1,0:T(8,128)(2,1)S(1)} %slice.17.refs_0_), channel_id=1, source_target_pairs={{0,14},{2,0},{4,2},{6,4},{8,6},{10,8},{12,10},{14,12},{1,15},{3,1}... | collective-permute-start | bytes 393224 | tf_op jit(solution)/shard_map/ppermute | solution.py:459
  34.4 11.1 %collective-permute-start.2 = (bf16[8,32,256]{2,1,0:T(8,128)(2,1)S(1)}, bf16[8,32,256]{2,1,0:T(8,128)(2,1)S(1)}, u32[]{:S(2)}, u32[]{:S(2)}) collective-permute-start(bf16[8,32,256]{2,1,0:T(8,128)(2,1)S(1)} %collective-permute-done.1.refs_1_), channel_id=1, source_target_pairs={{0,2},{2,4},{4,6},{6,8},{8,10},{10,12},{12,14},{14,0},{1,3},{3,5},... | collective-permute-start | bytes 393224 | tf_op jit(solution)/shard_map/ppermute | solution.py:457
  36.1 9.4 %collective-permute-start.3 = (bf16[8,16,128]{2,1,0:T(8,128)(2,1)S(1)}, bf16[8,16,128]{2,1,0:T(8,128)(2,1)S(1)}, u32[]{:S(2)}, u32[]{:S(2)}) collective-permute-start(bf16[8,16,128]{2,1,0:T(8,128)(2,1)S(1)} %slice.16.own_ref), channel_id=1, source_target_pairs={{0,1},{1,0},{2,3},{3,2},{4,5},{5,4},{6,7},{7,6},{8,9},{9,8},{10,11... | collective-permute-start | bytes 98312 | tf_op jit(solution)/shard_map/ppermute | solution.py:453
  40.2 5.4 %collective-permute-start.8 = (bf16[8,32,256]{2,1,0:T(8,128)(2,1)S(1)}, bf16[8,32,256]{2,1,0:T(8,128)(2,1)S(1)}, u32[]{:S(2)}, u32[]{:S(2)}) collective-permute-start(bf16[8,32,256]{2,1,0:T(8,128)(2,1)S(1)} %collective-permute-done.7.refs_2_), channel_id=1, source_target_pairs={{0,14},{2,0},{4,2},{6,4},{8,6},{10,8},{12,10},{14,12},{1,15},{3,1}... | collective-permute-start | bytes 393224 | tf_op jit(solution)/shard_map/ppermute | solution.py:459
  45.5 5.0 %collective-permute-start.6 = (bf16[8,32,256]{2,1,0:T(8,128)(2,1)S(1)}, bf16[8,32,256]{2,1,0:T(8,128)(2,1)S(1)}, u32[]{:S(2)}, u32[]{:S(2)}) collective-permute-start(bf16[8,32,256]{2,1,0:T(8,128)(2,1)S(1)} %collective-permute-done.2.refs_3_), channel_id=1, source_target_pairs={{0,2},{2,4},{4,6},{6,8},{8,10},{10,12},{12,14},{14,0},{1,3},{3,5},... | collective-permute-start | bytes 393224 | tf_op jit(solution)/shard_map/ppermute | solution.py:457
  45.7 10.5 %collective-permute-start.9 = (bf16[8,32,256]{2,1,0:T(8,128)(2,1)S(1)}, bf16[8,32,256]{2,1,0:T(8,128)(2,1)S(1)}, u32[]{:S(2)}, u32[]{:S(2)}) collective-permute-start(bf16[8,32,256]{2,1,0:T(8,128)(2,1)S(1)} %collective-permute-done.8.refs_4_), channel_id=1, source_target_pairs={{0,14},{2,0},{4,2},{6,4},{8,6},{10,8},{12,10},{14,12},{1,15},{3,1}... | collective-permute-start | bytes 393224 | tf_op jit(solution)/shard_map/ppermute | solution.py:459
  50.5 6.6 %collective-permute-start.10 = (bf16[8,32,256]{2,1,0:T(8,128)(2,1)S(1)}, bf16[8,32,256]{2,1,0:T(8,128)(2,1)S(1)}, u32[]{:S(2)}, u32[]{:S(2)}) collective-permute-start(bf16[8,32,256]{2,1,0:T(8,128)(2,1)S(1)} %collective-permute-done.6.refs_0_), channel_id=1, source_target_pairs={{0,2},{2,4},{4,6},{6,8},{8,10},{10,12},{12,14},{14,0},{1,3},{3,5},... | collective-permute-start | bytes 393224 | tf_op jit(solution)/shard_map/ppermute | solution.py:457
  52.2 3.9 %collective-permute-start.11 = (bf16[2,32,256]{2,1,0:T(8,128)(2,1)S(1)}, bf16[2,32,256]{2,1,0:T(8,128)(2,1)S(1)}, u32[]{:S(2)}, u32[]{:S(2)}) collective-permute-start(bf16[2,32,256]{2,1,0:T(8,128)(2,1)S(1)} %collective-permute-done.refs_4_), channel_id=1, source_target_pairs={{0,1},{1,0},{2,3},{3,2},{4,5},{5,4},{6,7},{7,6},{8,9},{9,8},{10,11... | collective-permute-start | bytes 98312 | tf_op jit(solution)/shard_map/ppermute | solution.py:454
  54.7 17.8 %copy-start.2 = (bf16[256,256]{1,0:T(8,128)(2,1)S(1)}, bf16[256,256]{1,0:T(8,128)(2,1)}, u32[]{:S(2)}) copy-start(bf16[256,256]{1,0:T(8,128)(2,1)} %final_ref.1) | copy-start | bytes 393220
  54.7 17.8 %copy-start.3 = (bf16[256,32]{0,1:T(8,128)(2,1)S(1)}, bf16[256,32]{0,1:T(8,128)(2,1)}, u32[]{:S(2)}) copy-start(bf16[256,32]{0,1:T(8,128)(2,1)} %param.30) | copy-start | bytes 49156
  54.7 17.8 %copy-start.4 = (f32[64,256]{1,0:T(8,128)S(1)}, f32[64,256]{1,0:T(8,128)}, u32[]{:S(2)}) copy-start(f32[64,256]{1,0:T(8,128)} %get-tuple-element.21.gate_ref) | copy-start | bytes 196612
  54.7 17.8 %copy-start.5 = (f32[64,256]{1,0:T(8,128)S(1)}, f32[64,256]{1,0:T(8,128)}, u32[]{:S(2)}) copy-start(f32[64,256]{1,0:T(8,128)} %get-tuple-element.22.prior_ref) | copy-start | bytes 196612
  54.7 17.8 %copy-start.6 = (bf16[256,32]{0,1:T(8,128)(2,1)S(1)}, bf16[256,32]{0,1:T(8,128)(2,1)}, u32[]{:S(2)}) copy-start(bf16[256,32]{0,1:T(8,128)(2,1)} %param.29) | copy-start | bytes 49156
  54.8 17.8 %copy-start.7 = (s32[256]{0:T(256)S(1)}, s32[256]{0:T(256)}, u32[]{:S(2)}) copy-start(s32[256]{0:T(256)} %flags_ref.1) | copy-start | bytes 3076
  54.8 17.8 %copy-start.8 = (s32[32]{0:T(128)S(1)}, s32[32]{0:T(128)}, u32[]{:S(2)}) copy-start(s32[32]{0:T(128)} %live_ref.5) | copy-start | bytes 388
  54.8 17.8 %copy-start.9 = (f32[256]{0:T(256)S(1)}, f32[256]{0:T(256)}, u32[]{:S(2)}) copy-start(f32[256]{0:T(256)} %param.28) | copy-start | bytes 3076
  90.8 14.0 %collective-permute-start.13 = (bf16[16,16,128]{2,1,0:T(8,128)(2,1)S(1)}, bf16[16,16,128]{2,1,0:T(8,128)(2,1)S(1)}, u32[]{:S(2)}, u32[]{:S(2)}) collective-permute-start(bf16[16,16,128]{2,1,0:T(8,128)(2,1)S(1)} %slice.21), channel_id=1, source_target_pairs={{0,0},{1,16},{2,32},{3,48},{4,64},{5,80},{6,96},{7,112},{8,128},{9... | collective-permute-start | bytes 196616 | tf_op jit(solution)/shard_map/ppermute | solution.py:492
  95.4 3.0 %collective-permute-start.12 = (bf16[16,32,256]{2,1,0:T(8,128)(2,1)S(1)}, bf16[16,32,256]{2,1,0:T(8,128)(2,1)S(1)}, u32[]{:S(2)}, u32[]{:S(2)}) collective-permute-start(bf16[16,32,256]{2,1,0:T(8,128)(2,1)S(1)} %slice.19), channel_id=1, source_target_pairs={{0,16},{16,0},{1,17},{17,1},{2,18},{18,2},{3,19},{19,3},{4,20},{20... | collective-permute-start | bytes 786440 | tf_op jit(solution)/shard_map/ppermute | solution.py:494
  (1 other events, 9.2 us)

commit v4 on v3

--- a/solution.py
+++ b/solution.py
@@ -126,7 +126,7 @@
 
 def attend_blocks(own_ref, swapped_ref, kva_ref, kvb_ref, blocks, extra_scr):
     c, x, z = lax.axis_index("c"), lax.axis_index("x"), lax.axis_index("z")
-    places = [lax.rem(z + offset + 8, 8) for offset, _ in blocks]
+    places = [lax.rem(z + offset * (1 - 2 * c) + 8, 8) for offset, _ in blocks]
     block = lax.broadcasted_iota(jnp.int32, (128, 128), 1) // 32
     for k, (place, (_, bias_ref)) in enumerate(zip(places, blocks)):
         mask = jnp.concatenate(
@@ -161,7 +161,7 @@
 
 def attend_kernel(own_ref, swapped_ref, kva_ref, kvb_ref, *refs):
     *bias_refs, out_ref, extra_scr = refs
-    blocks = list(zip((0, -1, 1, -2, 2), bias_refs))
+    blocks = list(zip((0, -1, 1, -2, 2, -3, 3), bias_refs))
     states = attend_blocks(own_ref, swapped_ref, kva_ref, kvb_ref, blocks, extra_scr)
     for a in range(2):
         for i in range(3):
@@ -175,7 +175,7 @@
         out_ref[q, x, 16:48, :] = x0_ref[x]
         out_ref[q, 1 - x, 16:48, :] = x1_ref[x]
     inner = lax.broadcasted_iota(jnp.int32, (128, 128), 1) % 32
-    blocks = list(zip((-3, 3, -4), bias_refs))
+    blocks = list(zip((-4,), bias_refs))
     states = attend_blocks(own_ref, swapped_ref, kva_ref, kvb_ref, blocks, extra_scr)
     for a in range(2):
         mixed, top, total = states[a]
@@ -246,15 +246,16 @@
 
 def pack_kernel(mine_ref, theirs_ref, factors_ref, factor_scr):
     swapped = lax.axis_index("c") == 1
+    turn = lax.axis_index("z") * 2 + lax.axis_index("x")
     for q in range(8):
         for c in range(2):
             for x in range(2):
                 mine = mine_ref[2 * q + x, 16:48, :].astype(F32)
                 theirs = theirs_ref[2 * q + x].astype(F32)
                 piece = jnp.where(swapped == (c == 1), mine, theirs)
-                place = (x * 16 + 2 * q + c) * 32
+                place = pl.multiple_of((x * 16 + (turn ^ (2 * q + c))) * 32, 32)
                 for i in range(2):
-                    factor_scr[i, place : place + 32, :] = piece[:, i * 128 : i * 128 + 128]
+                    factor_scr[i, pl.ds(place, 32), :] = piece[:, i * 128 : i * 128 + 128]
     for k in range(8):
         rows = []
         for d in range(k * 4, k * 4 + 4):
@@ -305,7 +306,6 @@
     mapped_ref,
     pair_ref,
     out_ref,
-    scr,
     band_scr,
     full_scr,
     done_scr,
@@ -319,10 +319,12 @@
                 turned[g * 64 + s * 32 : g * 64 + s * 32 + 32, n * 16 : n * 16 + 16] for g in range(2)
             ]
             band_scr[pl.ds(s * 16 + n, 32, stride=32), :] = jnp.concatenate(parts + [empty], axis=1)
+    slot = lax.broadcasted_iota(jnp.int32, (256, 128), 0) % 8
     for i in range(8):
-        scr[i] = factors_ref[:, i * 128 : (i + 1) * 128].astype(F32)
-        scr[i, pl.ds(0, 32, stride=8), :] = band_scr[i * 128 : (i + 1) * 128, :].T[0:32]
-        full_scr[:, i * 128 : (i + 1) * 128] = scr[i].astype(BF16)
+        band = band_scr[i * 128 : (i + 1) * 128, :].T[0:32]
+        band = jnp.broadcast_to(band[:, None, :], (32, 8, 128)).reshape(256, 128)
+        piece = factors_ref[:, i * 128 : (i + 1) * 128].astype(F32)
+        full_scr[:, i * 128 : (i + 1) * 128] = jnp.where(slot == 0, band, piece).astype(BF16)
 
     nvalid = jnp.int32(0)
     for s in range(32):
@@ -360,12 +362,12 @@
     return pltpu.CompilerParams(vmem_limit_bytes=VMEM)
 
 
-MIRROR = [(w * 16 + n, n * 16 + w) for w in range(16) for n in range(16)]
+MIRROR = [(w * 16 + n, (n ^ w) * 16 + w) for w in range(16) for n in range(16)]
 ACROSS = [(a * 2 + b, b * 2 + a) for a in range(2) for b in range(2)]
 ACROSS_NEXT = [(a * 2 + b, (1 - b) * 2 + a) for a in range(2) for b in range(2)]
 SWAP = [(0, 1), (1, 0)]
-UP = [(i, (i + 1) % 8) for i in range(8)]
-DOWN = [(i, (i + 7) % 8) for i in range(8)]
+AHEAD = [(c * 8 + i, c * 8 + (i + 1 - 2 * c) % 8) for c in range(2) for i in range(8)]
+BEHIND = [(c * 8 + i, c * 8 + (i - 1 + 2 * c) % 8) for c in range(2) for i in range(8)]
 
 
 def local(
@@ -392,8 +394,8 @@
 
     message, gate, prior, right = pl.pallas_call(
         front_kernel,
-        grid=(4,),
-        in_specs=[SCALARS, pl.BlockSpec((8, 256, 128), lambda i: (i, 0, 0))]
+        grid=(2,),
+        in_specs=[SCALARS, pl.BlockSpec((16, 256, 128), lambda i: (i, 0, 0))]
         + [
             whole(s)
             for s in (
@@ -454,29 +456,29 @@
     x1 = lax.ppermute(x0, "x", SWAP)
     below, above = [heads[:, 0:32, :]], [heads[:, 0:32, :]]
     for step in range(4):
-        below.append(lax.ppermute(below[-1], "z", UP))
+        below.append(lax.ppermute(below[-1], ("c", "z"), AHEAD))
         if step < 3:
-            above.append(lax.ppermute(above[-1], "z", DOWN))
+            above.append(lax.ppermute(above[-1], ("c", "z"), BEHIND))
         if step == 1:
             below[2], swapped = lax.optimization_barrier((below[2], swapped))
 
 
     state = pl.pallas_call(
         attend_kernel,
-        in_specs=[ARRAY] * 9,
+        in_specs=[ARRAY] * 11,
         out_specs=ARRAY,
         out_shape=jax.ShapeDtypeStruct((2, 3, 128, 128), F32),
-        scratch_shapes=[pltpu.VMEM((2, 128, 5 * 256), F32)],
-        compiler_params=params(),
-    )(own, swapped, kva, kvb, below[0], below[1], above[1], below[2], above[2])
+        scratch_shapes=[pltpu.VMEM((2, 128, 7 * 256), F32)],
+        compiler_params=params(),
+    )(own, swapped, kva, kvb, below[0], below[1], above[1], below[2], above[2], below[3], above[3])
     parts = pl.pallas_call(
         finish_kernel,
-        in_specs=[ARRAY] * 10,
+        in_specs=[ARRAY] * 8,
         out_specs=ARRAY,
         out_shape=jax.ShapeDtypeStruct((8, 2, 48, 256), BF16),
-        scratch_shapes=[pltpu.VMEM((2, 128, 3 * 256), F32)],
-        compiler_params=params(),
-    )(own, swapped, kva, kvb, below[3], above[3], below[4], state, x0, x1)
+        scratch_shapes=[pltpu.VMEM((2, 128, 256), F32)],
+        compiler_params=params(),
+    )(own, swapped, kva, kvb, below[4], state, x0, x1)
 
     parts = lax.all_to_all(parts.reshape(16, 48, 256), ("q", "x"), 0, 0, tiled=True)
 
@@ -517,7 +519,6 @@
         out_specs=pl.BlockSpec(memory_space=pl.ANY),
         out_shape=jax.ShapeDtypeStruct((32, 256, 128), BF16),
         scratch_shapes=[
-            pltpu.VMEM((8, 256, 128), F32),
             pltpu.VMEM((1024, 128), F32),
             pltpu.VMEM((256, 1024), BF16),
             pltpu.VMEM((32, 256, 128), BF16),

time: 111 us -> 108 us (0.973); the launches traced: 109 us -> 108 us
  waiting for transfers between devices: 21.5 us -> 23.9 us
  blocking collectives: 30 us -> 28 us
  starting transfers between devices: 35.6 us -> 34.2 us
    ppermute x7, waiting for transfers between devices: 6.95 us -> 8.9 us  [the longest x4 8.73 us: local(): below.append(lax.ppermute(below[-1], ('c', 'z'), AHEAD))]
    all_to_all x1, blocking collectives: 13.8 us -> 12.6 us  [local(): lax.all_to_all(parts.reshape(16, 48, 256), ('q', 'x'), 0, 0, tiled=True)]
    ppermute x1, waiting for transfers between devices: 5.52 us -> 6.69 us  [local(): band = lax.ppermute(sides[:, 16:32, :], ALL, MIRROR)]
    ppermute x1, waiting for transfers between devices: 1.35 us -> 0.23 us  [local(): x1 = lax.ppermute(x0, 'x', SWAP)]
  transfers between devices with their start and end apart: 15 -> 15, of which waited for: 8 -> 8; matrix products, arithmetic and copies ran while one was open for 0% -> 0% of each run, Pallas kernels for 6% -> 7%
where the time goes in v4:
time: 108 us
  starting transfers between devices  34.2 us (32%)
  blocking collectives  28 us (26%)
  waiting for transfers between devices  23.9 us (22%)
  Pallas kernels  20.5 us (19%)
    all_to_all x1, blocking collectives, gather(): return lax.all_to_all(tiled, axes, 0, 0, tiled=True)  15.4 us
    all_to_all x1, blocking collectives, local(): lax.all_to_all(parts.reshape(16, 48, 256), ('q', 'x'), 0, 0, tiled=True)  12.6 us
    ppermute x1, starting transfers between devices, local(): x0 = lax.ppermute(right, ALL, MIRROR)  10.1 us
    ppermute x4, waiting for transfers between devices, local(): below.append(lax.ppermute(below[-1], ('c', 'z'), AHEAD))  8.73 us
    all_to_all x1, starting transfers between devices, local(): heads = lax.all_to_all(message, 'q', 0, 0, tiled=True)  7.26 us
    ppermute x3, starting transfers between devices, local(): above.append(lax.ppermute(above[-1], ('c', 'z'), BEHIND))  6.99 us
    ppermute x1, waiting for transfers between devices, local(): band = lax.ppermute(sides[:, 16:32, :], ALL, MIRROR)  6.69 us
    pallas_call x1, Pallas kernels, local(): pl.pallas_call(front_kernel, grid=(2,), in_specs=[SCALARS, pl.BlockSpec((...  5.94 us
  transfers between devices with their start and end apart: 15, of which 8 were waited for; matrix products, arithmetic and copies ran while one was open for 0% of the time, Pallas kernels for 7%

profile of v4, /device:TPU:48, one launch (start us, length us, event | category | flops | bytes accessed | tf_op | source)
XLA Modules:
  0.0 107.8 jit_solution(12808717241561909485)
XLA Ops:
  0.6 5.9 %shard_map.167 = (bf16[8,176,256]{2,1,0:T(8,128)(2,1)}, f32[64,256]{1,0:T(8,128)}, f32[64,256]{1,0:T(8,128)}, bf16[2,32,256]{2,1,0:T(8,128)(2,1)}) custom-call(s32[32]{0:T(128)} %live_ref.5, bf16[32,256,128]{2,1,0:T(8,128)(2,1)} %pair_ref.3, bf16[512,256]{1,0:T(8,128)(2,1)} %bitcast.18, s32[2,128]{1,0:T(2,128)} %bitcast.14, f32[1,256]{1,0:T(1,128)} %bitcast.20, ...), custom_call_target="tpu_custom_call" | custom-call | tf_op jit(solution)/shard_map/pallas_call | solution.py:395
  6.6 7.3 %all-to-all-start = ((bf16[8,176,256]{2,1,0:T(8,128)(2,1)}), bf16[8,176,256]{2,1,0:T(8,128)(2,1)S(1)}, u32[]{:S(2)}, u32[]{:S(2)}) async-start(bf16[8,176,256]{2,1,0:T(8,128)(2,1)} %get-tuple-element.15), calls=%async_computation | async-start | bytes 1441792 | tf_op jit(solution)/shard_map/all_to_all | solution.py:440
  13.8 10.1 %collective-permute-start = (bf16[2,32,256]{2,1,0:T(8,128)(2,1)}, bf16[2,32,256]{2,1,0:T(8,128)(2,1)S(1)}, u32[]{:S(2)}, u32[]{:S(2)}) collective-permute-start(bf16[2,32,256]{2,1,0:T(8,128)(2,1)} %get-tuple-element.16), channel_id=1, source_target_pairs={{0,0},{1,16},{2,32},{3,48},{4,64},{5,80},{6,96},{7,112},{8,128},{9... | collective-permute-start | bytes 98312 | tf_op jit(solution)/shard_map/ppermute | solution.py:441
  24.4 4.2 %collective-permute-done.refs_2_ = bf16[2,32,256]{2,1,0:T(8,128)(2,1)S(1)} collective-permute-done((bf16[2,32,256]{2,1,0:T(8,128)(2,1)}, bf16[2,32,256]{2,1,0:T(8,128)(2,1)S(1)}, u32[]{:S(2)}, u32[]{:S(2)}) %collective-permute-start) | collective-permute-done | bytes 32800 | tf_op jit(solution)/shard_map/ppermute | solution.py:441
  28.8 0.7 collective-permute-start.4
  29.6 2.0 %collective-permute-start.8 = (bf16[8,32,256]{2,1,0:T(8,128)(2,1)S(1)}, bf16[8,32,256]{2,1,0:T(8,128)(2,1)S(1)}, u32[]{:S(2)}, u32[]{:S(2)}) collective-permute-start(bf16[8,32,256]{2,1,0:T(8,128)(2,1)S(1)} %slice.17.refs_0_), channel_id=1, source_target_pairs={{0,14},{2,0},{4,2},{6,4},{8,6},{10,8},{12,10},{14,12},{16,18},{18,... | collective-permute-start | bytes 393224 | tf_op jit(solution)/shard_map/ppermute | solution.py:461
  31.6 2.9 %collective-permute-done.1.refs_1_ = bf16[8,32,256]{2,1,0:T(8,128)(2,1)S(1)} collective-permute-done((bf16[8,32,256]{2,1,0:T(8,128)(2,1)S(1)}, bf16[8,32,256]{2,1,0:T(8,128)(2,1)S(1)}, u32[]{:S(2)}, u32[]{:S(2)}) %collective-permute-start.1) | collective-permute-done | bytes 131104 | tf_op jit(solution)/shard_map/ppermute | solution.py:459
  34.6 0.5 collective-permute-start.2
  35.1 3.8 %collective-permute-start.3 = (bf16[8,16,128]{2,1,0:T(8,128)(2,1)S(1)}, bf16[8,16,128]{2,1,0:T(8,128)(2,1)S(1)}, u32[]{:S(2)}, u32[]{:S(2)}) collective-permute-start(bf16[8,16,128]{2,1,0:T(8,128)(2,1)S(1)} %slice.16.own_ref), channel_id=1, source_target_pairs={{0,1},{1,0},{2,3},{3,2},{4,5},{5,4},{6,7},{7,6},{8,9},{9,8},{10,11... | collective-permute-start | bytes 98312 | tf_op jit(solution)/shard_map/ppermute | solution.py:455
  38.9 3.0 %collective-permute-start.9 = (bf16[8,32,256]{2,1,0:T(8,128)(2,1)S(1)}, bf16[8,32,256]{2,1,0:T(8,128)(2,1)S(1)}, u32[]{:S(2)}, u32[]{:S(2)}) collective-permute-start(bf16[8,32,256]{2,1,0:T(8,128)(2,1)S(1)} %collective-permute-done.8.refs_2_), channel_id=1, source_target_pairs={{0,14},{2,0},{4,2},{6,4},{8,6},{10,8},{12,10},{14,12},{16,18},{18,... | collective-permute-start | bytes 393224 | tf_op jit(solution)/shard_map/ppermute | solution.py:461
  41.9 3.9 %collective-permute-done.3.swapped_ref = bf16[8,16,128]{2,1,0:T(8,128)(2,1)S(1)} collective-permute-done((bf16[8,16,128]{2,1,0:T(8,128)(2,1)S(1)}, bf16[8,16,128]{2,1,0:T(8,128)(2,1)S(1)}, u32[]{:S(2)}, u32[]{:S(2)}) %collective-permute-start.3) | collective-permute-done | bytes 32800 | tf_op jit(solution)/shard_map/ppermute | solution.py:455
  45.7 2.0 %collective-permute-start.10 = (bf16[8,32,256]{2,1,0:T(8,128)(2,1)S(1)}, bf16[8,32,256]{2,1,0:T(8,128)(2,1)S(1)}, u32[]{:S(2)}, u32[]{:S(2)}) collective-permute-start(bf16[8,32,256]{2,1,0:T(8,128)(2,1)S(1)} %collective-permute-done.9.refs_4_), channel_id=1, source_target_pairs={{0,14},{2,0},{4,2},{6,4},{8,6},{10,8},{12,10},{14,12},{16,18},{18,... | collective-permute-start | bytes 393224 | tf_op jit(solution)/shard_map/ppermute | solution.py:461
  47.7 4.1 %collective-permute-done.6.refs_5_ = bf16[8,32,256]{2,1,0:T(8,128)(2,1)S(1)} collective-permute-done((bf16[8,32,256]{2,1,0:T(8,128)(2,1)S(1)}, bf16[8,32,256]{2,1,0:T(8,128)(2,1)S(1)}, u32[]{:S(2)}, u32[]{:S(2)}) %collective-permute-start.6) | collective-permute-done | bytes 131104 | tf_op jit(solution)/shard_map/ppermute | solution.py:459
  52.1 3.3 %shard_map.169.refs_1_ = f32[2,3,128,128]{3,2,1,0:T(8,128)S(1)} custom-call(bf16[8,16,128]{2,1,0:T(8,128)(2,1)S(1)} %slice.16.own_ref, bf16[8,16,128]{2,1,0:T(8,128)(2,1)S(1)} %collective-permute-done.3.swapped_ref, bf16[8,144,256]{2,1,0:T(8,128)(2,1)S(1)} %collective-permute-done.4.kva_ref, bf16[8,144,256]{2,1,0:T(8,128)(2,1)S(1)} %collective-permute-done.5.kvb_ref, ...), custom_call_target="tpu_custom_call" | custom-call | tf_op jit(solution)/shard_map/pallas_call | solution.py:466
  55.7 1.7 %collective-permute-done.7.refs_0_ = bf16[8,32,256]{2,1,0:T(8,128)(2,1)S(1)} collective-permute-done((bf16[8,32,256]{2,1,0:T(8,128)(2,1)S(1)}, bf16[8,32,256]{2,1,0:T(8,128)(2,1)S(1)}, u32[]{:S(2)}, u32[]{:S(2)}) %collective-permute-start.7) | collective-permute-done | bytes 131104 | tf_op jit(solution)/shard_map/ppermute | solution.py:459
  57.5 0.7 shard_map.170
  58.1 12.6 %all_to_all.15.parts_ref.mine_ref = bf16[16,48,256]{2,1,0:T(8,128)(2,1)S(1)} all-to-all(bf16[16,48,256]{2,1,0:T(8,128)(2,1)S(1)} %bitcast.10), channel_id=1, replica_groups=mesh['q'=8,'c'=2,'z'=8,'x'=2] {'q','x'}, dimensions={0} | all-to-all | bytes 786432 | tf_op jit(solution)/shard_map/all_to_all | solution.py:483
  70.8 2.0 %shard_map.171 = (bf16[64,256]{1,0:T(8,128)(2,1)}, bf16[32,128]{1,0:T(8,128)(2,1)S(1)}) custom-call(s32[32]{0:T(128)S(1)} %copy-done.8, bf16[16,48,256]{2,1,0:T(8,128)(2,1)S(1)} %all_to_all.15.parts_ref.mine_ref, f32[64,256]{1,0:T(8,128)S(1)} %copy-done.4, f32[64,256]{1,0:T(8,128)S(1)} %copy-done.5, s32[2,128]{1,0:T(2,128)S(1)} %bitcast.15, ...), custom_call_target="tpu_custom_call" | custom-call | tf_op jit(solution)/shard_map/pallas_call | solution.py:485
  72.8 15.4 %all_to_all.16.sides_ref = bf16[16,32,128]{2,1,0:T(8,128)(2,1)S(1)} all-to-all(bf16[16,32,128]{2,1,0:T(8,128)(2,1)S(1)} %broadcast_in_dim.2), channel_id=1, replica_groups=mesh['q'=8,'c'=2,'z'=8,'x'=2] {'z','x'}, dimensions={0} | all-to-all | bytes 262144 | tf_op jit(solution)/shard_map/all_to_all | solution.py:350
  88.2 4.4 %collective-permute-start.13 = (bf16[16,16,128]{2,1,0:T(8,128)(2,1)S(1)}, bf16[16,16,128]{2,1,0:T(8,128)(2,1)S(1)}, u32[]{:S(2)}, u32[]{:S(2)}) collective-permute-start(bf16[16,16,128]{2,1,0:T(8,128)(2,1)S(1)} %slice.21), channel_id=1, source_target_pairs={{0,0},{1,16},{2,32},{3,48},{4,64},{5,80},{6,96},{7,112},{8,128},{9... | collective-permute-start | bytes 196616 | tf_op jit(solution)/shard_map/ppermute | solution.py:494
  92.7 2.8 %shard_map.173.mapped_ref = bf16[16,1024,256]{2,1,0:T(8,128)(2,1)S(1)} custom-call(bf16[16,32,128]{2,1,0:T(8,128)(2,1)S(1)} %all_to_all.16.sides_ref, bf16[128,4096]{1,0:T(8,128)(2,1)S(1)} %shard_map.168.mapping_ref), custom_call_target="tpu_custom_call" | custom-call | flops 4294967296 | bytes 20971520 | tf_op jit(solution)/shard_map/pallas_call | solution.py:506
  95.6 0.8 shard_map.172.factors_ref
  96.4 6.7 %collective-permute-done.13.band_ref = bf16[16,16,128]{2,1,0:T(8,128)(2,1)S(1)} collective-permute-done((bf16[16,16,128]{2,1,0:T(8,128)(2,1)S(1)}, bf16[16,16,128]{2,1,0:T(8,128)(2,1)S(1)}, u32[]{:S(2)}, u32[]{:S(2)}) %collective-permute-start.13) | collective-permute-done | bytes 65568 | tf_op jit(solution)/shard_map/ppermute | solution.py:494
  103.1 4.5 %shard_map.174 = bf16[32,256,128]{2,1,0:T(8,128)(2,1)} custom-call(s32[32]{0:T(128)S(1)} %copy-done.8, s32[256]{0:T(256)S(1)} %copy-done.7, bf16[256,1024]{1,0:T(8,128)(2,1)S(1)} %shard_map.172.factors_ref, bf16[16,16,128]{2,1,0:T(8,128)(2,1)S(1)} %collective-permute-done.13.band_ref, bf16[16,1024,256]{2,1,0:T(8,128)(2,1)S(1)} %shard_map.173.mapped_ref, ...), custom_call_target="tpu_custom_call" | custom-call | tf_op jit(solution)/shard_map/pallas_call | solution.py:516
  (42 shorter events, 1.4 us)
Async XLA Ops:
  0.6 23.4 %copy-start.1 = (bf16[1024,128]{1,0:T(8,128)(2,1)S(1)}, bf16[1024,128]{1,0:T(8,128)(2,1)}, u32[]{:S(2)}) copy-start(bf16[1024,128]{1,0:T(8,128)(2,1)} %map_ref.1) | copy-start | bytes 786436
  6.6 22.1 %all-to-all-start = ((bf16[8,176,256]{2,1,0:T(8,128)(2,1)}), bf16[8,176,256]{2,1,0:T(8,128)(2,1)S(1)}, u32[]{:S(2)}, u32[]{:S(2)}) async-start(bf16[8,176,256]{2,1,0:T(8,128)(2,1)} %get-tuple-element.15), calls=%async_computation | async-start | bytes 1441792 | tf_op jit(solution)/shard_map/all_to_all | solution.py:440
  13.8 14.8 %collective-permute-start = (bf16[2,32,256]{2,1,0:T(8,128)(2,1)}, bf16[2,32,256]{2,1,0:T(8,128)(2,1)S(1)}, u32[]{:S(2)}, u32[]{:S(2)}) collective-permute-start(bf16[2,32,256]{2,1,0:T(8,128)(2,1)} %get-tuple-element.16), channel_id=1, source_target_pairs={{0,0},{1,16},{2,32},{3,48},{4,64},{5,80},{6,96},{7,112},{8,128},{9... | collective-permute-start | bytes 98312 | tf_op jit(solution)/shard_map/ppermute | solution.py:441
  28.7 23.4 %collective-permute-start.5 = (bf16[8,144,256]{2,1,0:T(8,128)(2,1)S(1)}, bf16[8,144,256]{2,1,0:T(8,128)(2,1)S(1)}, u32[]{:S(2)}, u32[]{:S(2)}) collective-permute-start(bf16[8,144,256]{2,1,0:T(8,128)(2,1)S(1)} %slice.18), channel_id=1, source_target_pairs={{0,16},{1,0},{16,17},{17,1},{2,18},{3,2},{18,19},{19,3},{4,20},{5,... | collective-permute-start | bytes 1769480 | tf_op jit(solution)/shard_map/ppermute | solution.py:454
  28.8 23.3 %collective-permute-start.4 = (bf16[8,144,256]{2,1,0:T(8,128)(2,1)S(1)}, bf16[8,144,256]{2,1,0:T(8,128)(2,1)S(1)}, u32[]{:S(2)}, u32[]{:S(2)}) collective-permute-start(bf16[8,144,256]{2,1,0:T(8,128)(2,1)S(1)} %slice.18), channel_id=1, source_target_pairs={{0,0},{1,16},{16,1},{17,17},{2,2},{3,18},{18,3},{19,19},{4,4},{5,2... | collective-permute-start | bytes 1769480 | tf_op jit(solution)/shard_map/ppermute | solution.py:453
  29.5 5.0 %collective-permute-start.1 = (bf16[8,32,256]{2,1,0:T(8,128)(2,1)S(1)}, bf16[8,32,256]{2,1,0:T(8,128)(2,1)S(1)}, u32[]{:S(2)}, u32[]{:S(2)}) collective-permute-start(bf16[8,32,256]{2,1,0:T(8,128)(2,1)S(1)} %slice.17.refs_0_), channel_id=1, source_target_pairs={{0,2},{2,4},{4,6},{6,8},{8,10},{10,12},{12,14},{14,0},{16,30},{18,... | collective-permute-start | bytes 393224 | tf_op jit(solution)/shard_map/ppermute | solution.py:459
  29.6 9.3 %collective-permute-start.8 = (bf16[8,32,256]{2,1,0:T(8,128)(2,1)S(1)}, bf16[8,32,256]{2,1,0:T(8,128)(2,1)S(1)}, u32[]{:S(2)}, u32[]{:S(2)}) collective-permute-start(bf16[8,32,256]{2,1,0:T(8,128)(2,1)S(1)} %slice.17.refs_0_), channel_id=1, source_target_pairs={{0,14},{2,0},{4,2},{6,4},{8,6},{10,8},{12,10},{14,12},{16,18},{18,... | collective-permute-start | bytes 393224 | tf_op jit(solution)/shard_map/ppermute | solution.py:461
  34.6 11.1 %collective-permute-start.2 = (bf16[8,32,256]{2,1,0:T(8,128)(2,1)S(1)}, bf16[8,32,256]{2,1,0:T(8,128)(2,1)S(1)}, u32[]{:S(2)}, u32[]{:S(2)}) collective-permute-start(bf16[8,32,256]{2,1,0:T(8,128)(2,1)S(1)} %collective-permute-done.1.refs_1_), channel_id=1, source_target_pairs={{0,2},{2,4},{4,6},{6,8},{8,10},{10,12},{12,14},{14,0},{16,30},{18,... | collective-permute-start | bytes 393224 | tf_op jit(solution)/shard_map/ppermute | solution.py:459
  35.1 10.6 %collective-permute-start.3 = (bf16[8,16,128]{2,1,0:T(8,128)(2,1)S(1)}, bf16[8,16,128]{2,1,0:T(8,128)(2,1)S(1)}, u32[]{:S(2)}, u32[]{:S(2)}) collective-permute-start(bf16[8,16,128]{2,1,0:T(8,128)(2,1)S(1)} %slice.16.own_ref), channel_id=1, source_target_pairs={{0,1},{1,0},{2,3},{3,2},{4,5},{5,4},{6,7},{7,6},{8,9},{9,8},{10,11... | collective-permute-start | bytes 98312 | tf_op jit(solution)/shard_map/ppermute | solution.py:455
  38.9 6.8 %collective-permute-start.9 = (bf16[8,32,256]{2,1,0:T(8,128)(2,1)S(1)}, bf16[8,32,256]{2,1,0:T(8,128)(2,1)S(1)}, u32[]{:S(2)}, u32[]{:S(2)}) collective-permute-start(bf16[8,32,256]{2,1,0:T(8,128)(2,1)S(1)} %collective-permute-done.8.refs_2_), channel_id=1, source_target_pairs={{0,14},{2,0},{4,2},{6,4},{8,6},{10,8},{12,10},{14,12},{16,18},{18,... | collective-permute-start | bytes 393224 | tf_op jit(solution)/shard_map/ppermute | solution.py:461
  45.7 6.1 %collective-permute-start.6 = (bf16[8,32,256]{2,1,0:T(8,128)(2,1)S(1)}, bf16[8,32,256]{2,1,0:T(8,128)(2,1)S(1)}, u32[]{:S(2)}, u32[]{:S(2)}) collective-permute-start(bf16[8,32,256]{2,1,0:T(8,128)(2,1)S(1)} %collective-permute-done.2.refs_3_), channel_id=1, source_target_pairs={{0,2},{2,4},{4,6},{6,8},{8,10},{10,12},{12,14},{14,0},{16,30},{18,... | collective-permute-start | bytes 393224 | tf_op jit(solution)/shard_map/ppermute | solution.py:459
  45.7 6.4 %collective-permute-start.10 = (bf16[8,32,256]{2,1,0:T(8,128)(2,1)S(1)}, bf16[8,32,256]{2,1,0:T(8,128)(2,1)S(1)}, u32[]{:S(2)}, u32[]{:S(2)}) collective-permute-start(bf16[8,32,256]{2,1,0:T(8,128)(2,1)S(1)} %collective-permute-done.9.refs_4_), channel_id=1, source_target_pairs={{0,14},{2,0},{4,2},{6,4},{8,6},{10,8},{12,10},{14,12},{16,18},{18,... | collective-permute-start | bytes 393224 | tf_op jit(solution)/shard_map/ppermute | solution.py:461
  51.8 5.7 %collective-permute-start.7 = (bf16[8,32,256]{2,1,0:T(8,128)(2,1)S(1)}, bf16[8,32,256]{2,1,0:T(8,128)(2,1)S(1)}, u32[]{:S(2)}, u32[]{:S(2)}) collective-permute-start(bf16[8,32,256]{2,1,0:T(8,128)(2,1)S(1)} %collective-permute-done.6.refs_5_), channel_id=1, source_target_pairs={{0,2},{2,4},{4,6},{6,8},{8,10},{10,12},{12,14},{14,0},{16,30},{18,... | collective-permute-start | bytes 393224 | tf_op jit(solution)/shard_map/ppermute | solution.py:459
  51.8 3.9 %collective-permute-start.11 = (bf16[2,32,256]{2,1,0:T(8,128)(2,1)S(1)}, bf16[2,32,256]{2,1,0:T(8,128)(2,1)S(1)}, u32[]{:S(2)}, u32[]{:S(2)}) collective-permute-start(bf16[2,32,256]{2,1,0:T(8,128)(2,1)S(1)} %collective-permute-done.refs_2_), channel_id=1, source_target_pairs={{0,1},{1,0},{2,3},{3,2},{4,5},{5,4},{6,7},{7,6},{8,9},{9,8},{10,11... | collective-permute-start | bytes 98312 | tf_op jit(solution)/shard_map/ppermute | solution.py:456
  55.4 15.3 %copy-start.2 = (bf16[256,256]{1,0:T(8,128)(2,1)S(1)}, bf16[256,256]{1,0:T(8,128)(2,1)}, u32[]{:S(2)}) copy-start(bf16[256,256]{1,0:T(8,128)(2,1)} %final_ref.1) | copy-start | bytes 393220
  55.4 15.3 %copy-start.3 = (bf16[256,32]{0,1:T(8,128)(2,1)S(1)}, bf16[256,32]{0,1:T(8,128)(2,1)}, u32[]{:S(2)}) copy-start(bf16[256,32]{0,1:T(8,128)(2,1)} %param.30) | copy-start | bytes 49156
  55.4 15.3 %copy-start.4 = (f32[64,256]{1,0:T(8,128)S(1)}, f32[64,256]{1,0:T(8,128)}, u32[]{:S(2)}) copy-start(f32[64,256]{1,0:T(8,128)} %get-tuple-element.21.gate_ref) | copy-start | bytes 196612
  55.4 15.3 %copy-start.5 = (f32[64,256]{1,0:T(8,128)S(1)}, f32[64,256]{1,0:T(8,128)}, u32[]{:S(2)}) copy-start(f32[64,256]{1,0:T(8,128)} %get-tuple-element.22.prior_ref) | copy-start | bytes 196612
  55.4 15.3 %copy-start.6 = (bf16[256,32]{0,1:T(8,128)(2,1)S(1)}, bf16[256,32]{0,1:T(8,128)(2,1)}, u32[]{:S(2)}) copy-start(bf16[256,32]{0,1:T(8,128)(2,1)} %param.29) | copy-start | bytes 49156
  55.5 15.3 %copy-start.7 = (s32[256]{0:T(256)S(1)}, s32[256]{0:T(256)}, u32[]{:S(2)}) copy-start(s32[256]{0:T(256)} %flags_ref.1) | copy-start | bytes 3076
  55.5 15.3 %copy-start.8 = (s32[32]{0:T(128)S(1)}, s32[32]{0:T(128)}, u32[]{:S(2)}) copy-start(s32[32]{0:T(128)} %live_ref.5) | copy-start | bytes 388
  55.5 15.3 %copy-start.9 = (f32[256]{0:T(256)S(1)}, f32[256]{0:T(256)}, u32[]{:S(2)}) copy-start(f32[256]{0:T(256)} %param.28) | copy-start | bytes 3076
  88.2 14.9 %collective-permute-start.13 = (bf16[16,16,128]{2,1,0:T(8,128)(2,1)S(1)}, bf16[16,16,128]{2,1,0:T(8,128)(2,1)S(1)}, u32[]{:S(2)}, u32[]{:S(2)}) collective-permute-start(bf16[16,16,128]{2,1,0:T(8,128)(2,1)S(1)} %slice.21), channel_id=1, source_target_pairs={{0,0},{1,16},{2,32},{3,48},{4,64},{5,80},{6,96},{7,112},{8,128},{9... | collective-permute-start | bytes 196616 | tf_op jit(solution)/shard_map/ppermute | solution.py:494
  92.6 3.0 %collective-permute-start.12 = (bf16[16,32,256]{2,1,0:T(8,128)(2,1)S(1)}, bf16[16,32,256]{2,1,0:T(8,128)(2,1)S(1)}, u32[]{:S(2)}, u32[]{:S(2)}) collective-permute-start(bf16[16,32,256]{2,1,0:T(8,128)(2,1)S(1)} %slice.19), channel_id=1, source_target_pairs={{0,16},{16,0},{1,17},{17,1},{2,18},{18,2},{3,19},{19,3},{4,20},{20... | collective-permute-start | bytes 786440 | tf_op jit(solution)/shard_map/ppermute | solution.py:496
  (1 other events, 10.3 us)

commit v5 on v4

--- a/solution.py
+++ b/solution.py
@@ -211,14 +211,17 @@
     live = jnp.concatenate([band * live_ref[first_row + s].astype(F32) for s in range(2)], axis=0)
     rows = lax.broadcasted_iota(jnp.int32, (128, 128), 0)
     lanes = lax.broadcasted_iota(jnp.int32, (128, 128), 1)
-    spread = [jnp.where(rows == (lanes // 32) * 32 + t, 1.0, 0.0).astype(BF16) for t in range(6)]
+    spread = jnp.concatenate(
+        [jnp.where(rows == (lanes // 32) * 32 + t, 1.0, 0.0).astype(BF16) for t in range(6)], axis=1
+    )
     tops, totals, mixes = [], [], []
     for x in range(2):
         mixes.append(
             jnp.concatenate([parts_ref[2 * h + x, 0:16, 0:128] for h in range(8)], axis=0).astype(F32)
         )
         stats = jnp.concatenate([parts_ref[2 * h + x, 0:16, 128:256] for h in range(8)], axis=0)
-        wide = [dot(stats, spread[t], NN) for t in range(6)]
+        wide = dot(stats, spread, NN)
+        wide = [wide[:, t * 128 : (t + 1) * 128] for t in range(6)]
         tops.append(wide[0] + wide[1] + wide[2])
         totals.append(wide[3] + wide[4] + wide[5])
     top = jnp.maximum(tops[0], tops[1])
@@ -459,8 +462,8 @@
         below.append(lax.ppermute(below[-1], ("c", "z"), AHEAD))
         if step < 3:
             above.append(lax.ppermute(above[-1], ("c", "z"), BEHIND))
-        if step == 1:
-            below[2], swapped = lax.optimization_barrier((below[2], swapped))
+        if step == 2:
+            below[3], swapped = lax.optimization_barrier((below[3], swapped))
 
 
     state = pl.pallas_call(

time: 108 us -> 107 us (level)
  waiting for transfers between devices: 23.9 us -> 17.7 us
  starting transfers between devices: 34.2 us -> 38.9 us
    ppermute x1, starting transfers between devices: 0.14 us -> 4.05 us  [local(): x1 = lax.ppermute(x0, 'x', SWAP)]
    ppermute x1, waiting for transfers between devices: 3.86 us -> 0.01 us  [local(): swapped = lax.ppermute(own, 'x', SWAP)]
    ppermute x4, waiting for transfers between devices: 8.73 us -> 6.38 us  [local(): below.append(lax.ppermute(below[-1], ('c', 'z'), AHEAD))]
    all_to_all x1, blocking collectives: 12.6 us -> 13.7 us  [local(): lax.all_to_all(parts.reshape(16, 48, 256), ('q', 'x'), 0, 0, tiled=True)]
  transfers between devices with their start and end apart: 15 -> 15, of which waited for: 8 -> 5; matrix products, arithmetic and copies ran while one was open for 0% -> 0% of each run, Pallas kernels for 7% -> 7%
where the time goes in v5:
time: 107 us
  starting transfers between devices  38.9 us (36%)
  blocking collectives  28.6 us (27%)
  Pallas kernels  20.4 us (19%)
  waiting for transfers between devices  17.7 us (17%)
  between operations  1.07 us (1%)
    all_to_all x1, blocking collectives, gather(): return lax.all_to_all(tiled, axes, 0, 0, tiled=True)  14.8 us
    all_to_all x1, blocking collectives, local(): lax.all_to_all(parts.reshape(16, 48, 256), ('q', 'x'), 0, 0, tiled=True)  13.7 us
    ppermute x1, starting transfers between devices, local(): x0 = lax.ppermute(right, ALL, MIRROR)  10.1 us
    all_to_all x1, starting transfers between devices, local(): heads = lax.all_to_all(message, 'q', 0, 0, tiled=True)  7.26 us
    ppermute x3, starting transfers between devices, local(): above.append(lax.ppermute(above[-1], ('c', 'z'), BEHIND))  6.92 us
    ppermute x1, waiting for transfers between devices, local(): band = lax.ppermute(sides[:, 16:32, :], ALL, MIRROR)  6.68 us
    ppermute x4, waiting for transfers between devices, local(): below.append(lax.ppermute(below[-1], ('c', 'z'), AHEAD))  6.38 us
    pallas_call x1, Pallas kernels, local(): pl.pallas_call(front_kernel, grid=(2,), in_specs=[SCALARS, pl.BlockSpec((...  5.94 us
  transfers between devices with their start and end apart: 15, of which 5 were waited for; matrix products, arithmetic and copies ran while one was open for 0% of the time, Pallas kernels for 7%

profile of v5, /device:TPU:48, one launch (start us, length us, event | category | flops | bytes accessed | tf_op | source)
XLA Modules:
  0.0 106.9 jit_solution(4059167312704382046)
XLA Ops:
  0.6 5.9 %shard_map.167 = (bf16[8,176,256]{2,1,0:T(8,128)(2,1)}, f32[64,256]{1,0:T(8,128)}, f32[64,256]{1,0:T(8,128)}, bf16[2,32,256]{2,1,0:T(8,128)(2,1)}) custom-call(s32[32]{0:T(128)} %live_ref.5, bf16[32,256,128]{2,1,0:T(8,128)(2,1)} %pair_ref.3, bf16[512,256]{1,0:T(8,128)(2,1)} %bitcast.18, s32[2,128]{1,0:T(2,128)} %bitcast.14, f32[1,256]{1,0:T(1,128)} %bitcast.20, ...), custom_call_target="tpu_custom_call" | custom-call | tf_op jit(solution)/shard_map/pallas_call | solution.py:398
  6.6 7.3 %all-to-all-start = ((bf16[8,176,256]{2,1,0:T(8,128)(2,1)}), bf16[8,176,256]{2,1,0:T(8,128)(2,1)S(1)}, u32[]{:S(2)}, u32[]{:S(2)}) async-start(bf16[8,176,256]{2,1,0:T(8,128)(2,1)} %get-tuple-element.15), calls=%async_computation | async-start | bytes 1441792 | tf_op jit(solution)/shard_map/all_to_all | solution.py:443
  13.8 10.1 %collective-permute-start = (bf16[2,32,256]{2,1,0:T(8,128)(2,1)}, bf16[2,32,256]{2,1,0:T(8,128)(2,1)S(1)}, u32[]{:S(2)}, u32[]{:S(2)}) collective-permute-start(bf16[2,32,256]{2,1,0:T(8,128)(2,1)} %get-tuple-element.16), channel_id=1, source_target_pairs={{0,0},{1,16},{2,32},{3,48},{4,64},{5,80},{6,96},{7,112},{8,128},{9... | collective-permute-start | bytes 98312 | tf_op jit(solution)/shard_map/ppermute | solution.py:444
  24.0 0.4 shard_map.168.mapping_ref
  24.4 4.2 %collective-permute-done.refs_2_ = bf16[2,32,256]{2,1,0:T(8,128)(2,1)S(1)} collective-permute-done((bf16[2,32,256]{2,1,0:T(8,128)(2,1)}, bf16[2,32,256]{2,1,0:T(8,128)(2,1)S(1)}, u32[]{:S(2)}, u32[]{:S(2)}) %collective-permute-start) | collective-permute-done | bytes 32800 | tf_op jit(solution)/shard_map/ppermute | solution.py:444
  28.8 0.7 collective-permute-start.5
  29.6 2.0 %collective-permute-start.8 = (bf16[8,32,256]{2,1,0:T(8,128)(2,1)S(1)}, bf16[8,32,256]{2,1,0:T(8,128)(2,1)S(1)}, u32[]{:S(2)}, u32[]{:S(2)}) collective-permute-start(bf16[8,32,256]{2,1,0:T(8,128)(2,1)S(1)} %slice.17.refs_0_), channel_id=1, source_target_pairs={{0,14},{2,0},{4,2},{6,4},{8,6},{10,8},{12,10},{14,12},{16,18},{18,... | collective-permute-start | bytes 393224 | tf_op jit(solution)/shard_map/ppermute | solution.py:464
  31.6 2.9 %collective-permute-done.1.refs_1_ = bf16[8,32,256]{2,1,0:T(8,128)(2,1)S(1)} collective-permute-done((bf16[8,32,256]{2,1,0:T(8,128)(2,1)S(1)}, bf16[8,32,256]{2,1,0:T(8,128)(2,1)S(1)}, u32[]{:S(2)}, u32[]{:S(2)}) %collective-permute-start.1) | collective-permute-done | bytes 131104 | tf_op jit(solution)/shard_map/ppermute | solution.py:462
  34.6 0.5 collective-permute-start.2
  35.5 2.0 %collective-permute-start.9 = (bf16[8,32,256]{2,1,0:T(8,128)(2,1)S(1)}, bf16[8,32,256]{2,1,0:T(8,128)(2,1)S(1)}, u32[]{:S(2)}, u32[]{:S(2)}) collective-permute-start(bf16[8,32,256]{2,1,0:T(8,128)(2,1)S(1)} %collective-permute-done.8.refs_2_), channel_id=1, source_target_pairs={{0,14},{2,0},{4,2},{6,4},{8,6},{10,8},{12,10},{14,12},{16,18},{18,... | collective-permute-start | bytes 393224 | tf_op jit(solution)/shard_map/ppermute | solution.py:464
  37.5 3.4 %collective-permute-done.2.refs_3_ = bf16[8,32,256]{2,1,0:T(8,128)(2,1)S(1)} collective-permute-done((bf16[8,32,256]{2,1,0:T(8,128)(2,1)S(1)}, bf16[8,32,256]{2,1,0:T(8,128)(2,1)S(1)}, u32[]{:S(2)}, u32[]{:S(2)}) %collective-permute-start.2) | collective-permute-done | bytes 131104 | tf_op jit(solution)/shard_map/ppermute | solution.py:462
  40.9 4.7 %collective-permute-start.4 = (bf16[8,16,128]{2,1,0:T(8,128)(2,1)S(1)}, bf16[8,16,128]{2,1,0:T(8,128)(2,1)S(1)}, u32[]{:S(2)}, u32[]{:S(2)}) collective-permute-start(bf16[8,16,128]{2,1,0:T(8,128)(2,1)S(1)} %slice.16.own_ref), channel_id=1, source_target_pairs={{0,1},{1,0},{2,3},{3,2},{4,5},{5,4},{6,7},{7,6},{8,9},{9,8},{10,11... | collective-permute-start | bytes 98312 | tf_op jit(solution)/shard_map/ppermute | solution.py:458
  45.6 3.0 %collective-permute-start.10 = (bf16[8,32,256]{2,1,0:T(8,128)(2,1)S(1)}, bf16[8,32,256]{2,1,0:T(8,128)(2,1)S(1)}, u32[]{:S(2)}, u32[]{:S(2)}) collective-permute-start(bf16[8,32,256]{2,1,0:T(8,128)(2,1)S(1)} %collective-permute-done.9.refs_4_), channel_id=1, source_target_pairs={{0,14},{2,0},{4,2},{6,4},{8,6},{10,8},{12,10},{14,12},{16,18},{18,... | collective-permute-start | bytes 393224 | tf_op jit(solution)/shard_map/ppermute | solution.py:464
  48.6 4.0 %collective-permute-start.11 = (bf16[2,32,256]{2,1,0:T(8,128)(2,1)S(1)}, bf16[2,32,256]{2,1,0:T(8,128)(2,1)S(1)}, u32[]{:S(2)}, u32[]{:S(2)}) collective-permute-start(bf16[2,32,256]{2,1,0:T(8,128)(2,1)S(1)} %collective-permute-done.refs_2_), channel_id=1, source_target_pairs={{0,1},{1,0},{2,3},{3,2},{4,5},{5,4},{6,7},{7,6},{8,9},{9,8},{10,11... | collective-permute-start | bytes 98312 | tf_op jit(solution)/shard_map/ppermute | solution.py:459
  52.6 3.3 %shard_map.169.refs_1_ = f32[2,3,128,128]{3,2,1,0:T(8,128)S(1)} custom-call(bf16[8,16,128]{2,1,0:T(8,128)(2,1)S(1)} %slice.16.own_ref, bf16[8,16,128]{2,1,0:T(8,128)(2,1)S(1)} %collective-permute-done.4.swapped_ref, bf16[8,144,256]{2,1,0:T(8,128)(2,1)S(1)} %collective-permute-done.5.kva_ref, bf16[8,144,256]{2,1,0:T(8,128)(2,1)S(1)} %collective-permute-done.6.kvb_ref, ...), custom_call_target="tpu_custom_call" | custom-call | tf_op jit(solution)/shard_map/pallas_call | solution.py:469
  56.0 0.7 shard_map.170
  56.7 13.7 %all_to_all.15.parts_ref.mine_ref = bf16[16,48,256]{2,1,0:T(8,128)(2,1)S(1)} all-to-all(bf16[16,48,256]{2,1,0:T(8,128)(2,1)S(1)} %bitcast.10), channel_id=1, replica_groups=mesh['q'=8,'c'=2,'z'=8,'x'=2] {'q','x'}, dimensions={0} | all-to-all | bytes 786432 | tf_op jit(solution)/shard_map/all_to_all | solution.py:486
  70.5 1.9 %shard_map.171 = (bf16[64,256]{1,0:T(8,128)(2,1)}, bf16[32,128]{1,0:T(8,128)(2,1)S(1)}) custom-call(s32[32]{0:T(128)S(1)} %copy-done.8, bf16[16,48,256]{2,1,0:T(8,128)(2,1)S(1)} %all_to_all.15.parts_ref.mine_ref, f32[64,256]{1,0:T(8,128)S(1)} %copy-done.4, f32[64,256]{1,0:T(8,128)S(1)} %copy-done.5, s32[2,128]{1,0:T(2,128)S(1)} %bitcast.15, ...), custom_call_target="tpu_custom_call" | custom-call | tf_op jit(solution)/shard_map/pallas_call | solution.py:488
  72.5 14.8 %all_to_all.16.sides_ref = bf16[16,32,128]{2,1,0:T(8,128)(2,1)S(1)} all-to-all(bf16[16,32,128]{2,1,0:T(8,128)(2,1)S(1)} %broadcast_in_dim.2), channel_id=1, replica_groups=mesh['q'=8,'c'=2,'z'=8,'x'=2] {'z','x'}, dimensions={0} | all-to-all | bytes 262144 | tf_op jit(solution)/shard_map/all_to_all | solution.py:353
  87.3 4.4 %collective-permute-start.13 = (bf16[16,16,128]{2,1,0:T(8,128)(2,1)S(1)}, bf16[16,16,128]{2,1,0:T(8,128)(2,1)S(1)}, u32[]{:S(2)}, u32[]{:S(2)}) collective-permute-start(bf16[16,16,128]{2,1,0:T(8,128)(2,1)S(1)} %slice.21), channel_id=1, source_target_pairs={{0,0},{1,16},{2,32},{3,48},{4,64},{5,80},{6,96},{7,112},{8,128},{9... | collective-permute-start | bytes 196616 | tf_op jit(solution)/shard_map/ppermute | solution.py:497
  91.9 2.8 %shard_map.173.mapped_ref = bf16[16,1024,256]{2,1,0:T(8,128)(2,1)S(1)} custom-call(bf16[16,32,128]{2,1,0:T(8,128)(2,1)S(1)} %all_to_all.16.sides_ref, bf16[128,4096]{1,0:T(8,128)(2,1)S(1)} %shard_map.168.mapping_ref), custom_call_target="tpu_custom_call" | custom-call | flops 4294967296 | bytes 20971520 | tf_op jit(solution)/shard_map/pallas_call | solution.py:509
  94.7 0.8 shard_map.172.factors_ref
  95.5 6.7 %collective-permute-done.13.band_ref = bf16[16,16,128]{2,1,0:T(8,128)(2,1)S(1)} collective-permute-done((bf16[16,16,128]{2,1,0:T(8,128)(2,1)S(1)}, bf16[16,16,128]{2,1,0:T(8,128)(2,1)S(1)}, u32[]{:S(2)}, u32[]{:S(2)}) %collective-permute-start.13) | collective-permute-done | bytes 65568 | tf_op jit(solution)/shard_map/ppermute | solution.py:497
  102.2 4.5 %shard_map.174 = bf16[32,256,128]{2,1,0:T(8,128)(2,1)} custom-call(s32[32]{0:T(128)S(1)} %copy-done.8, s32[256]{0:T(256)S(1)} %copy-done.7, bf16[256,1024]{1,0:T(8,128)(2,1)S(1)} %shard_map.172.factors_ref, bf16[16,16,128]{2,1,0:T(8,128)(2,1)S(1)} %collective-permute-done.13.band_ref, bf16[16,1024,256]{2,1,0:T(8,128)(2,1)S(1)} %shard_map.173.mapped_ref, ...), custom_call_target="tpu_custom_call" | custom-call | tf_op jit(solution)/shard_map/pallas_call | solution.py:519
  (42 shorter events, 0.9 us)
Async XLA Ops:
  0.6 23.4 %copy-start.1 = (bf16[1024,128]{1,0:T(8,128)(2,1)S(1)}, bf16[1024,128]{1,0:T(8,128)(2,1)}, u32[]{:S(2)}) copy-start(bf16[1024,128]{1,0:T(8,128)(2,1)} %map_ref.1) | copy-start | bytes 786436
  6.6 22.1 %all-to-all-start = ((bf16[8,176,256]{2,1,0:T(8,128)(2,1)}), bf16[8,176,256]{2,1,0:T(8,128)(2,1)S(1)}, u32[]{:S(2)}, u32[]{:S(2)}) async-start(bf16[8,176,256]{2,1,0:T(8,128)(2,1)} %get-tuple-element.15), calls=%async_computation | async-start | bytes 1441792 | tf_op jit(solution)/shard_map/all_to_all | solution.py:443
  13.8 14.8 %collective-permute-start = (bf16[2,32,256]{2,1,0:T(8,128)(2,1)}, bf16[2,32,256]{2,1,0:T(8,128)(2,1)S(1)}, u32[]{:S(2)}, u32[]{:S(2)}) collective-permute-start(bf16[2,32,256]{2,1,0:T(8,128)(2,1)} %get-tuple-element.16), channel_id=1, source_target_pairs={{0,0},{1,16},{2,32},{3,48},{4,64},{5,80},{6,96},{7,112},{8,128},{9... | collective-permute-start | bytes 98312 | tf_op jit(solution)/shard_map/ppermute | solution.py:444
  28.7 23.9 %collective-permute-start.6 = (bf16[8,144,256]{2,1,0:T(8,128)(2,1)S(1)}, bf16[8,144,256]{2,1,0:T(8,128)(2,1)S(1)}, u32[]{:S(2)}, u32[]{:S(2)}) collective-permute-start(bf16[8,144,256]{2,1,0:T(8,128)(2,1)S(1)} %slice.18), channel_id=1, source_target_pairs={{0,16},{1,0},{16,17},{17,1},{2,18},{3,2},{18,19},{19,3},{4,20},{5,... | collective-permute-start | bytes 1769480 | tf_op jit(solution)/shard_map/ppermute | solution.py:457
  28.8 23.8 %collective-permute-start.5 = (bf16[8,144,256]{2,1,0:T(8,128)(2,1)S(1)}, bf16[8,144,256]{2,1,0:T(8,128)(2,1)S(1)}, u32[]{:S(2)}, u32[]{:S(2)}) collective-permute-start(bf16[8,144,256]{2,1,0:T(8,128)(2,1)S(1)} %slice.18), channel_id=1, source_target_pairs={{0,0},{1,16},{16,1},{17,17},{2,2},{3,18},{18,3},{19,19},{4,4},{5,2... | collective-permute-start | bytes 1769480 | tf_op jit(solution)/shard_map/ppermute | solution.py:456
  29.5 5.0 %collective-permute-start.1 = (bf16[8,32,256]{2,1,0:T(8,128)(2,1)S(1)}, bf16[8,32,256]{2,1,0:T(8,128)(2,1)S(1)}, u32[]{:S(2)}, u32[]{:S(2)}) collective-permute-start(bf16[8,32,256]{2,1,0:T(8,128)(2,1)S(1)} %slice.17.refs_0_), channel_id=1, source_target_pairs={{0,2},{2,4},{4,6},{6,8},{8,10},{10,12},{12,14},{14,0},{16,30},{18,... | collective-permute-start | bytes 393224 | tf_op jit(solution)/shard_map/ppermute | solution.py:462
  29.6 5.9 %collective-permute-start.8 = (bf16[8,32,256]{2,1,0:T(8,128)(2,1)S(1)}, bf16[8,32,256]{2,1,0:T(8,128)(2,1)S(1)}, u32[]{:S(2)}, u32[]{:S(2)}) collective-permute-start(bf16[8,32,256]{2,1,0:T(8,128)(2,1)S(1)} %slice.17.refs_0_), channel_id=1, source_target_pairs={{0,14},{2,0},{4,2},{6,4},{8,6},{10,8},{12,10},{14,12},{16,18},{18,... | collective-permute-start | bytes 393224 | tf_op jit(solution)/shard_map/ppermute | solution.py:464
  34.6 6.3 %collective-permute-start.2 = (bf16[8,32,256]{2,1,0:T(8,128)(2,1)S(1)}, bf16[8,32,256]{2,1,0:T(8,128)(2,1)S(1)}, u32[]{:S(2)}, u32[]{:S(2)}) collective-permute-start(bf16[8,32,256]{2,1,0:T(8,128)(2,1)S(1)} %collective-permute-done.1.refs_1_), channel_id=1, source_target_pairs={{0,2},{2,4},{4,6},{6,8},{8,10},{10,12},{12,14},{14,0},{16,30},{18,... | collective-permute-start | bytes 393224 | tf_op jit(solution)/shard_map/ppermute | solution.py:462
  35.5 10.1 %collective-permute-start.9 = (bf16[8,32,256]{2,1,0:T(8,128)(2,1)S(1)}, bf16[8,32,256]{2,1,0:T(8,128)(2,1)S(1)}, u32[]{:S(2)}, u32[]{:S(2)}) collective-permute-start(bf16[8,32,256]{2,1,0:T(8,128)(2,1)S(1)} %collective-permute-done.8.refs_2_), channel_id=1, source_target_pairs={{0,14},{2,0},{4,2},{6,4},{8,6},{10,8},{12,10},{14,12},{16,18},{18,... | collective-permute-start | bytes 393224 | tf_op jit(solution)/shard_map/ppermute | solution.py:464
  40.9 7.7 %collective-permute-start.3 = (bf16[8,32,256]{2,1,0:T(8,128)(2,1)S(1)}, bf16[8,32,256]{2,1,0:T(8,128)(2,1)S(1)}, u32[]{:S(2)}, u32[]{:S(2)}) collective-permute-start(bf16[8,32,256]{2,1,0:T(8,128)(2,1)S(1)} %collective-permute-done.2.refs_3_), channel_id=1, source_target_pairs={{0,2},{2,4},{4,6},{6,8},{8,10},{10,12},{12,14},{14,0},{16,30},{18,... | collective-permute-start | bytes 393224 | tf_op jit(solution)/shard_map/ppermute | solution.py:462
  40.9 7.7 %collective-permute-start.4 = (bf16[8,16,128]{2,1,0:T(8,128)(2,1)S(1)}, bf16[8,16,128]{2,1,0:T(8,128)(2,1)S(1)}, u32[]{:S(2)}, u32[]{:S(2)}) collective-permute-start(bf16[8,16,128]{2,1,0:T(8,128)(2,1)S(1)} %slice.16.own_ref), channel_id=1, source_target_pairs={{0,1},{1,0},{2,3},{3,2},{4,5},{5,4},{6,7},{7,6},{8,9},{9,8},{10,11... | collective-permute-start | bytes 98312 | tf_op jit(solution)/shard_map/ppermute | solution.py:458
  45.6 7.0 %collective-permute-start.10 = (bf16[8,32,256]{2,1,0:T(8,128)(2,1)S(1)}, bf16[8,32,256]{2,1,0:T(8,128)(2,1)S(1)}, u32[]{:S(2)}, u32[]{:S(2)}) collective-permute-start(bf16[8,32,256]{2,1,0:T(8,128)(2,1)S(1)} %collective-permute-done.9.refs_4_), channel_id=1, source_target_pairs={{0,14},{2,0},{4,2},{6,4},{8,6},{10,8},{12,10},{14,12},{16,18},{18,... | collective-permute-start | bytes 393224 | tf_op jit(solution)/shard_map/ppermute | solution.py:464
  48.6 7.5 %collective-permute-start.7 = (bf16[8,32,256]{2,1,0:T(8,128)(2,1)S(1)}, bf16[8,32,256]{2,1,0:T(8,128)(2,1)S(1)}, u32[]{:S(2)}, u32[]{:S(2)}) collective-permute-start(bf16[8,32,256]{2,1,0:T(8,128)(2,1)S(1)} %collective-permute-done.3.refs_5_), channel_id=1, source_target_pairs={{0,2},{2,4},{4,6},{6,8},{8,10},{10,12},{12,14},{14,0},{16,30},{18,... | collective-permute-start | bytes 393224 | tf_op jit(solution)/shard_map/ppermute | solution.py:462
  48.6 7.4 %collective-permute-start.11 = (bf16[2,32,256]{2,1,0:T(8,128)(2,1)S(1)}, bf16[2,32,256]{2,1,0:T(8,128)(2,1)S(1)}, u32[]{:S(2)}, u32[]{:S(2)}) collective-permute-start(bf16[2,32,256]{2,1,0:T(8,128)(2,1)S(1)} %collective-permute-done.refs_2_), channel_id=1, source_target_pairs={{0,1},{1,0},{2,3},{3,2},{4,5},{5,4},{6,7},{7,6},{8,9},{9,8},{10,11... | collective-permute-start | bytes 98312 | tf_op jit(solution)/shard_map/ppermute | solution.py:459
  55.9 14.5 %copy-start.2 = (bf16[256,256]{1,0:T(8,128)(2,1)S(1)}, bf16[256,256]{1,0:T(8,128)(2,1)}, u32[]{:S(2)}) copy-start(bf16[256,256]{1,0:T(8,128)(2,1)} %final_ref.1) | copy-start | bytes 393220
  55.9 14.5 %copy-start.3 = (bf16[256,32]{0,1:T(8,128)(2,1)S(1)}, bf16[256,32]{0,1:T(8,128)(2,1)}, u32[]{:S(2)}) copy-start(bf16[256,32]{0,1:T(8,128)(2,1)} %param.30) | copy-start | bytes 49156
  55.9 14.5 %copy-start.4 = (f32[64,256]{1,0:T(8,128)S(1)}, f32[64,256]{1,0:T(8,128)}, u32[]{:S(2)}) copy-start(f32[64,256]{1,0:T(8,128)} %get-tuple-element.21.gate_ref) | copy-start | bytes 196612
  56.0 14.5 %copy-start.5 = (f32[64,256]{1,0:T(8,128)S(1)}, f32[64,256]{1,0:T(8,128)}, u32[]{:S(2)}) copy-start(f32[64,256]{1,0:T(8,128)} %get-tuple-element.22.prior_ref) | copy-start | bytes 196612
  56.0 14.5 %copy-start.6 = (bf16[256,32]{0,1:T(8,128)(2,1)S(1)}, bf16[256,32]{0,1:T(8,128)(2,1)}, u32[]{:S(2)}) copy-start(bf16[256,32]{0,1:T(8,128)(2,1)} %param.29) | copy-start | bytes 49156
  56.0 14.5 %copy-start.7 = (s32[256]{0:T(256)S(1)}, s32[256]{0:T(256)}, u32[]{:S(2)}) copy-start(s32[256]{0:T(256)} %flags_ref.1) | copy-start | bytes 3076
  56.0 14.5 %copy-start.8 = (s32[32]{0:T(128)S(1)}, s32[32]{0:T(128)}, u32[]{:S(2)}) copy-start(s32[32]{0:T(128)} %live_ref.5) | copy-start | bytes 388
  56.0 14.5 %copy-start.9 = (f32[256]{0:T(256)S(1)}, f32[256]{0:T(256)}, u32[]{:S(2)}) copy-start(f32[256]{0:T(256)} %param.28) | copy-start | bytes 3076
  87.3 14.9 %collective-permute-start.13 = (bf16[16,16,128]{2,1,0:T(8,128)(2,1)S(1)}, bf16[16,16,128]{2,1,0:T(8,128)(2,1)S(1)}, u32[]{:S(2)}, u32[]{:S(2)}) collective-permute-start(bf16[16,16,128]{2,1,0:T(8,128)(2,1)S(1)} %slice.21), channel_id=1, source_target_pairs={{0,0},{1,16},{2,32},{3,48},{4,64},{5,80},{6,96},{7,112},{8,128},{9... | collective-permute-start | bytes 196616 | tf_op jit(solution)/shard_map/ppermute | solution.py:497
  91.8 3.0 %collective-permute-start.12 = (bf16[16,32,256]{2,1,0:T(8,128)(2,1)S(1)}, bf16[16,32,256]{2,1,0:T(8,128)(2,1)S(1)}, u32[]{:S(2)}, u32[]{:S(2)}) collective-permute-start(bf16[16,32,256]{2,1,0:T(8,128)(2,1)S(1)} %slice.19), channel_id=1, source_target_pairs={{0,16},{16,0},{1,17},{17,1},{2,18},{18,2},{3,19},{19,3},{4,20},{20... | collective-permute-start | bytes 786440 | tf_op jit(solution)/shard_map/ppermute | solution.py:499
  (1 other events, 10.3 us)

commit v6 on v5

--- a/solution.py
+++ b/solution.py
@@ -45,14 +45,11 @@
     ask_ref,
     look_ref,
     cont_ref,
-    sig_ref,
     gp_ref,
     head_ref,
     g2_ref,
     other_ref,
     msg_ref,
-    gate_ref,
-    prior_ref,
     right_ref,
     bias_scr,
     norm_scr,
@@ -72,8 +69,7 @@
 
     @pl.when(step == 0)
     def _():
-        raw = seq_ref[...].astype(F32)
-        base = center_and_scale(raw)
+        base = center_and_scale(seq_ref[...].astype(F32))
         normed = (base * g1_ref[...]).astype(BF16)
         keys = dot(look_ref[...], normed, TT).astype(BF16)
         values = dot(cont_ref[...], normed, TT).astype(BF16)
@@ -85,11 +81,9 @@
         wide = normed.astype(F32)
         for i in range(2):
             norm_scr[i] = wide[:, i * 128 : (i + 1) * 128]
-            norm_scr[2 + i] = raw[:, i * 128 : (i + 1) * 128]
-        cuts = [norm_scr[i, pl.ds(0, 64, stride=8), :] for i in range(4)]
-        band = jnp.concatenate(cuts[:2], axis=1).astype(BF16)
-        prior_ref[...] = jnp.concatenate(cuts[2:], axis=1)
-        gate_ref[...] = jax.nn.sigmoid(dot(band, sig_ref[...], NN))
+        band = jnp.concatenate(
+            [norm_scr[i, pl.ds(0, 64, stride=8), :] for i in range(2)], axis=1
+        ).astype(BF16)
         query = (dot(band, ask_ref[...], NN) * 32 ** (-0.5)).astype(BF16).astype(F32)
         flags = flags_ref[...].astype(F32)
         row = lax.broadcasted_iota(jnp.int32, (16, 128), 0)
@@ -129,9 +123,8 @@
     places = [lax.rem(z + offset * (1 - 2 * c) + 8, 8) for offset, _ in blocks]
     block = lax.broadcasted_iota(jnp.int32, (128, 128), 1) // 32
     for k, (place, (_, bias_ref)) in enumerate(zip(places, blocks)):
-        mask = jnp.concatenate(
-            [kva_ref[place, 128 + i : 129 + i, 128:256].astype(F32) for i in range(2)], axis=1
-        )
+        tile = kva_ref[place, 128:144, 128:256].astype(F32)
+        mask = jnp.concatenate([tile[0:1], tile[1:2]], axis=1)
         for g in range(2):
             piece = bias_ref[:, g * 16 : g * 16 + 16, :].reshape(128, 256).astype(F32)
             extra_scr[g, :, k * 256 : (k + 1) * 256] = piece + BIG * (mask - 1.0)
@@ -193,11 +186,10 @@
 
 
 def refresh_kernel(
-    live_ref,
     parts_ref,
     gate_ref,
     prior_ref,
-    flags_ref,
+    alive_ref,
     final_ref,
     g2_ref,
     first_ref,
@@ -205,10 +197,6 @@
     fresh_ref,
     sides_ref,
 ):
-    first_row = (lax.axis_index("z") * 2 + lax.axis_index("x")) * 2
-    flags = flags_ref[...].astype(F32)
-    band = row_of(jnp.concatenate([flags[0:1], flags[1:2]], axis=1), 32)
-    live = jnp.concatenate([band * live_ref[first_row + s].astype(F32) for s in range(2)], axis=0)
     rows = lax.broadcasted_iota(jnp.int32, (128, 128), 0)
     lanes = lax.broadcasted_iota(jnp.int32, (128, 128), 1)
     spread = jnp.concatenate(
@@ -242,7 +230,7 @@
     fresh_ref[...] = fresh
     again = (center_and_scale(fresh.astype(F32)) * g2_ref[...]).astype(BF16)
     for i, factor in enumerate((first_ref, other_ref)):
-        side = dot(again, factor[...], NT) * live
+        side = dot(again, factor[...], NT) * alive_ref[...]
         parts = [side[s * 32 + g * 16 : s * 32 + g * 16 + 16] for g in range(2) for s in range(2)]
         sides_ref[i * 16 : i * 16 + 16, :] = jnp.concatenate(parts, axis=1).astype(BF16)
 
@@ -268,7 +256,20 @@
         factors_ref[:, k * 128 : (k + 1) * 128] = jnp.concatenate(rows, axis=0).T.astype(BF16)
 
 
-def line_kernel(map_ref, mapping_ref, scr):
+def side_kernel(
+    live_ref, seq_ref, flags_ref, g1_ref, sig_ref, map_ref, gate_ref, prior_ref, alive_ref, mapping_ref, seq_scr, scr
+):
+    for i in range(2):
+        seq_scr[i] = seq_ref[:, i * 128 : (i + 1) * 128].astype(F32)
+    prior = jnp.concatenate([seq_scr[i, pl.ds(0, 64, stride=8), :] for i in range(2)], axis=1)
+    prior_ref[...] = prior
+    band = (center_and_scale(prior) * g1_ref[...]).astype(BF16)
+    gate_ref[...] = jax.nn.sigmoid(dot(band, sig_ref[...], NN))
+    first_row = (lax.axis_index("z") * 2 + lax.axis_index("x")) * 2
+    flags = flags_ref[...].astype(F32)
+    column = row_of(jnp.concatenate([flags[0:1], flags[1:2]], axis=1), 32)
+    live = jnp.concatenate([column * live_ref[first_row + s].astype(F32) for s in range(2)], axis=0)
+    alive_ref[...] = jnp.broadcast_to(live, (64, 32))
     scr[...] = map_ref[...].astype(F32)
     for d in range(32):
         piece = scr[pl.ds(d, 32, stride=32), :].astype(BF16)
@@ -395,7 +396,9 @@
     flags = position_valid_flags.reshape(2, 128)
     first, other = first_factor_matrix.T, other_factor_matrix.T
 
-    message, gate, prior, right = pl.pallas_call(
+    seq = sequence_activity.reshape(512, 256)
+    g1 = attend_scale_vector.reshape(1, 256)
+    message, right = pl.pallas_call(
         front_kernel,
         grid=(2,),
         in_specs=[SCALARS, pl.BlockSpec((16, 256, 128), lambda i: (i, 0, 0))]
@@ -408,32 +411,28 @@
                 (256, 256),
                 (256, 256),
                 (256, 256),
-                (256, 256),
                 (1, 128),
                 (8, 128),
                 (1, 256),
                 (32, 256),
             )
         ],
-        out_specs=[whole((8, 176, 256)), whole((64, 256)), whole((64, 256)), whole((2, 32, 256))],
+        out_specs=[whole((8, 176, 256)), whole((2, 32, 256))],
         out_shape=[
             jax.ShapeDtypeStruct((8, 176, 256), BF16),
-            jax.ShapeDtypeStruct((64, 256), F32),
-            jax.ShapeDtypeStruct((64, 256), F32),
             jax.ShapeDtypeStruct((2, 32, 256), BF16),
         ],
-        scratch_shapes=[pltpu.VMEM((2, 256, 128), F32), pltpu.VMEM((4, 512, 128), F32)],
+        scratch_shapes=[pltpu.VMEM((2, 256, 128), F32), pltpu.VMEM((2, 512, 128), F32)],
         compiler_params=pltpu.CompilerParams(vmem_limit_bytes=FULL),
     )(
         sequence_valid_flags,
         couple_activity,
-        sequence_activity.reshape(512, 256),
+        seq,
         flags,
-        attend_scale_vector.reshape(1, 256),
+        g1,
         asking_matrix,
         lookup_matrix,
         content_matrix,
-        sigmoid_matrix,
         couple_scale_vector.reshape(1, 128),
         headwise_additive_matrix.T,
         g2,
@@ -442,14 +441,19 @@
 
     heads = lax.all_to_all(message, "q", 0, 0, tiled=True)
     x0 = lax.ppermute(right, ALL, MIRROR)
-    mapping = pl.pallas_call(
-        line_kernel,
-        in_specs=[ARRAY],
-        out_specs=ARRAY,
-        out_shape=jax.ShapeDtypeStruct((128, 4096), BF16),
-        scratch_shapes=[pltpu.VMEM((1024, 128), F32)],
-        compiler_params=params(),
-    )(product_mapping_matrix)
+    gate, prior, alive, mapping = pl.pallas_call(
+        side_kernel,
+        in_specs=[SCALARS] + [ARRAY] * 5,
+        out_specs=[ARRAY] * 4,
+        out_shape=[
+            jax.ShapeDtypeStruct((64, 256), F32),
+            jax.ShapeDtypeStruct((64, 256), F32),
+            jax.ShapeDtypeStruct((64, 32), F32),
+            jax.ShapeDtypeStruct((128, 4096), BF16),
+        ],
+        scratch_shapes=[pltpu.VMEM((2, 512, 128), F32), pltpu.VMEM((1024, 128), F32)],
+        compiler_params=params(),
+    )(sequence_valid_flags, seq, flags, g1, sigmoid_matrix, product_mapping_matrix)
     heads, x0, mapping = lax.optimization_barrier((heads, x0, mapping))
     kv = heads[:, 32:176, :]
     own = heads[:, 160:176, 0:128]
@@ -487,11 +491,11 @@
 
     fresh, sides = pl.pallas_call(
         refresh_kernel,
-        in_specs=[SCALARS] + [ARRAY] * 8,
+        in_specs=[ARRAY] * 8,
         out_specs=[ARRAY] * 2,
         out_shape=[jax.ShapeDtypeStruct((64, 256), BF16), jax.ShapeDtypeStruct((32, 128), BF16)],
         compiler_params=params(),
-    )(sequence_valid_flags, parts, gate, prior, flags, attend_final_matrix, g2, first, other)
+    )(parts, gate, prior, alive, attend_final_matrix, g2, first, other)
 
     sides = gather(sides, ("z", "x"), 16)
     band = lax.ppermute(sides[:, 16:32, :], ALL, MIRROR)

time: 107 us -> 107 us (level)
  transfers between devices with their start and end apart: 15 -> 15, of which waited for: 5 -> 5; matrix products, arithmetic and copies ran while one was open for 0% -> 0% of each run, Pallas kernels for 7% -> 8%
where the time goes in v6:
time: 107 us; the launch traced here: 106 us
  starting transfers between devices  38.9 us (36%)
  blocking collectives  28.6 us (27%)
  Pallas kernels  20.7 us (19%)
  waiting for transfers between devices  16.9 us (16%)
  between operations  1.09 us (1%)
    all_to_all x1, blocking collectives, gather(): return lax.all_to_all(tiled, axes, 0, 0, tiled=True)  14.8 us
    all_to_all x1, blocking collectives, local(): lax.all_to_all(parts.reshape(16, 48, 256), ('q', 'x'), 0, 0, tiled=True)  13.7 us
    ppermute x1, starting transfers between devices, local(): x0 = lax.ppermute(right, ALL, MIRROR)  10.1 us
    all_to_all x1, starting transfers between devices, local(): heads = lax.all_to_all(message, 'q', 0, 0, tiled=True)  7.26 us
    ppermute x3, starting transfers between devices, local(): above.append(lax.ppermute(above[-1], ('c', 'z'), BEHIND))  6.92 us
    ppermute x1, waiting for transfers between devices, local(): band = lax.ppermute(sides[:, 16:32, :], ALL, MIRROR)  6.69 us
    ppermute x4, waiting for transfers between devices, local(): below.append(lax.ppermute(below[-1], ('c', 'z'), AHEAD))  6.38 us
    pallas_call x1, Pallas kernels, local(): pl.pallas_call(front_kernel, grid=(2,), in_specs=[SCALARS, pl.BlockSpec((...  5.96 us
  transfers between devices with their start and end apart: 15, of which 5 were waited for; matrix products, arithmetic and copies ran while one was open for 0% of the time, Pallas kernels for 8%

profile of v6, /device:TPU:48, one launch (start us, length us, event | category | flops | bytes accessed | tf_op | source)
XLA Modules:
  0.0 106.4 jit_solution(14249959758636734821)
XLA Ops:
  0.7 6.0 %shard_map.167 = (bf16[8,176,256]{2,1,0:T(8,128)(2,1)}, bf16[2,32,256]{2,1,0:T(8,128)(2,1)}) custom-call(s32[32]{0:T(128)} %live_ref.5, bf16[32,256,128]{2,1,0:T(8,128)(2,1)} %pair_ref.3, bf16[512,256]{1,0:T(8,128)(2,1)} %bitcast.11, s32[2,128]{1,0:T(2,128)} %bitcast.16, f32[1,256]{1,0:T(1,128)} %bitcast.18, bf16[256,256]{1,0:T(8,128)(2,1)} %ask_ref.1, ...), custom_call_target="tpu_custom_call" | custom-call | tf_op jit(solution)/shard_map/pallas_call | solution.py:401
  6.7 7.3 %all-to-all-start = ((bf16[8,176,256]{2,1,0:T(8,128)(2,1)}), bf16[8,176,256]{2,1,0:T(8,128)(2,1)S(1)}, u32[]{:S(2)}, u32[]{:S(2)}) async-start(bf16[8,176,256]{2,1,0:T(8,128)(2,1)} %get-tuple-element.17), calls=%async_computation | async-start | bytes 1441792 | tf_op jit(solution)/shard_map/all_to_all | solution.py:442
  13.9 10.1 %collective-permute-start = (bf16[2,32,256]{2,1,0:T(8,128)(2,1)}, bf16[2,32,256]{2,1,0:T(8,128)(2,1)S(1)}, u32[]{:S(2)}, u32[]{:S(2)}) collective-permute-start(bf16[2,32,256]{2,1,0:T(8,128)(2,1)} %get-tuple-element.18), channel_id=1, source_target_pairs={{0,0},{1,16},{2,32},{3,48},{4,64},{5,80},{6,96},{7,112},{8,128},{9... | collective-permute-start | bytes 98312 | tf_op jit(solution)/shard_map/ppermute | solution.py:443
  24.1 1.2 %shard_map.168 = (f32[64,256]{1,0:T(8,128)S(1)}, f32[64,256]{1,0:T(8,128)S(1)}, f32[64,32]{1,0:T(8,128)S(1)}, bf16[128,4096]{1,0:T(8,128)(2,1)S(1)}) custom-call(s32[32]{0:T(128)S(1)} %copy-done.8, bf16[512,256]{1,0:T(8,128)(2,1)S(1)} %bitcast.12, s32[2,128]{1,0:T(2,128)S(1)} %bitcast.17, f32[1,256]{1,0:T(1,128)S(1)} %bitcast.19, ...), custom_call_target="tpu_custom_call" | custom-call | tf_op jit(solution)/shard_map/pallas_call | solution.py:444
  25.3 3.4 %collective-permute-done.refs_2_ = bf16[2,32,256]{2,1,0:T(8,128)(2,1)S(1)} collective-permute-done((bf16[2,32,256]{2,1,0:T(8,128)(2,1)}, bf16[2,32,256]{2,1,0:T(8,128)(2,1)S(1)}, u32[]{:S(2)}, u32[]{:S(2)}) %collective-permute-start) | collective-permute-done | bytes 32800 | tf_op jit(solution)/shard_map/ppermute | solution.py:443
  28.9 0.7 collective-permute-start.5
  29.7 2.0 %collective-permute-start.8 = (bf16[8,32,256]{2,1,0:T(8,128)(2,1)S(1)}, bf16[8,32,256]{2,1,0:T(8,128)(2,1)S(1)}, u32[]{:S(2)}, u32[]{:S(2)}) collective-permute-start(bf16[8,32,256]{2,1,0:T(8,128)(2,1)S(1)} %slice.17.refs_0_), channel_id=1, source_target_pairs={{0,14},{2,0},{4,2},{6,4},{8,6},{10,8},{12,10},{14,12},{16,18},{18,... | collective-permute-start | bytes 393224 | tf_op jit(solution)/shard_map/ppermute | solution.py:468
  31.7 2.9 %collective-permute-done.1.refs_1_ = bf16[8,32,256]{2,1,0:T(8,128)(2,1)S(1)} collective-permute-done((bf16[8,32,256]{2,1,0:T(8,128)(2,1)S(1)}, bf16[8,32,256]{2,1,0:T(8,128)(2,1)S(1)}, u32[]{:S(2)}, u32[]{:S(2)}) %collective-permute-start.1) | collective-permute-done | bytes 131104 | tf_op jit(solution)/shard_map/ppermute | solution.py:466
  34.7 0.5 collective-permute-start.2
  35.6 2.0 %collective-permute-start.9 = (bf16[8,32,256]{2,1,0:T(8,128)(2,1)S(1)}, bf16[8,32,256]{2,1,0:T(8,128)(2,1)S(1)}, u32[]{:S(2)}, u32[]{:S(2)}) collective-permute-start(bf16[8,32,256]{2,1,0:T(8,128)(2,1)S(1)} %collective-permute-done.8.refs_2_), channel_id=1, source_target_pairs={{0,14},{2,0},{4,2},{6,4},{8,6},{10,8},{12,10},{14,12},{16,18},{18,... | collective-permute-start | bytes 393224 | tf_op jit(solution)/shard_map/ppermute | solution.py:468
  37.5 3.4 %collective-permute-done.2.refs_3_ = bf16[8,32,256]{2,1,0:T(8,128)(2,1)S(1)} collective-permute-done((bf16[8,32,256]{2,1,0:T(8,128)(2,1)S(1)}, bf16[8,32,256]{2,1,0:T(8,128)(2,1)S(1)}, u32[]{:S(2)}, u32[]{:S(2)}) %collective-permute-start.2) | collective-permute-done | bytes 131104 | tf_op jit(solution)/shard_map/ppermute | solution.py:466
  41.0 4.7 %collective-permute-start.4 = (bf16[8,16,128]{2,1,0:T(8,128)(2,1)S(1)}, bf16[8,16,128]{2,1,0:T(8,128)(2,1)S(1)}, u32[]{:S(2)}, u32[]{:S(2)}) collective-permute-start(bf16[8,16,128]{2,1,0:T(8,128)(2,1)S(1)} %slice.16.own_ref), channel_id=1, source_target_pairs={{0,1},{1,0},{2,3},{3,2},{4,5},{5,4},{6,7},{7,6},{8,9},{9,8},{10,11... | collective-permute-start | bytes 98312 | tf_op jit(solution)/shard_map/ppermute | solution.py:462
  45.7 3.0 %collective-permute-start.10 = (bf16[8,32,256]{2,1,0:T(8,128)(2,1)S(1)}, bf16[8,32,256]{2,1,0:T(8,128)(2,1)S(1)}, u32[]{:S(2)}, u32[]{:S(2)}) collective-permute-start(bf16[8,32,256]{2,1,0:T(8,128)(2,1)S(1)} %collective-permute-done.9.refs_4_), channel_id=1, source_target_pairs={{0,14},{2,0},{4,2},{6,4},{8,6},{10,8},{12,10},{14,12},{16,18},{18,... | collective-permute-start | bytes 393224 | tf_op jit(solution)/shard_map/ppermute | solution.py:468
  48.7 4.0 %collective-permute-start.11 = (bf16[2,32,256]{2,1,0:T(8,128)(2,1)S(1)}, bf16[2,32,256]{2,1,0:T(8,128)(2,1)S(1)}, u32[]{:S(2)}, u32[]{:S(2)}) collective-permute-start(bf16[2,32,256]{2,1,0:T(8,128)(2,1)S(1)} %collective-permute-done.refs_2_), channel_id=1, source_target_pairs={{0,1},{1,0},{2,3},{3,2},{4,5},{5,4},{6,7},{7,6},{8,9},{9,8},{10,11... | collective-permute-start | bytes 98312 | tf_op jit(solution)/shard_map/ppermute | solution.py:463
  52.7 3.3 %shard_map.169.refs_1_ = f32[2,3,128,128]{3,2,1,0:T(8,128)S(1)} custom-call(bf16[8,16,128]{2,1,0:T(8,128)(2,1)S(1)} %slice.16.own_ref, bf16[8,16,128]{2,1,0:T(8,128)(2,1)S(1)} %collective-permute-done.4.swapped_ref, bf16[8,144,256]{2,1,0:T(8,128)(2,1)S(1)} %collective-permute-done.5.kva_ref, bf16[8,144,256]{2,1,0:T(8,128)(2,1)S(1)} %collective-permute-done.6.kvb_ref, ...), custom_call_target="tpu_custom_call" | custom-call | tf_op jit(solution)/shard_map/pallas_call | solution.py:473
  56.1 0.7 shard_map.170
  56.8 13.7 %all_to_all.15.parts_ref.mine_ref = bf16[16,48,256]{2,1,0:T(8,128)(2,1)S(1)} all-to-all(bf16[16,48,256]{2,1,0:T(8,128)(2,1)S(1)} %bitcast.10), channel_id=1, replica_groups=mesh['q'=8,'c'=2,'z'=8,'x'=2] {'q','x'}, dimensions={0} | all-to-all | bytes 786432 | tf_op jit(solution)/shard_map/all_to_all | solution.py:490
  70.5 1.4 %shard_map.171 = (bf16[64,256]{1,0:T(8,128)(2,1)}, bf16[32,128]{1,0:T(8,128)(2,1)S(1)}) custom-call(bf16[16,48,256]{2,1,0:T(8,128)(2,1)S(1)} %all_to_all.15.parts_ref.mine_ref, f32[64,256]{1,0:T(8,128)S(1)} %get-tuple-element.24.gate_ref, f32[64,256]{1,0:T(8,128)S(1)} %get-tuple-element.25.prior_ref, f32[64,32]{1,0:T(8,128)S(1)} %get-tuple-element.26.alive_ref, ...), custom_call_target="tpu_custom_call" | custom-call | tf_op jit(solution)/shard_map/pallas_call | solution.py:492
  72.0 14.8 %all_to_all.16.sides_ref = bf16[16,32,128]{2,1,0:T(8,128)(2,1)S(1)} all-to-all(bf16[16,32,128]{2,1,0:T(8,128)(2,1)S(1)} %broadcast_in_dim.2), channel_id=1, replica_groups=mesh['q'=8,'c'=2,'z'=8,'x'=2] {'z','x'}, dimensions={0} | all-to-all | bytes 262144 | tf_op jit(solution)/shard_map/all_to_all | solution.py:354
  86.8 4.4 %collective-permute-start.13 = (bf16[16,16,128]{2,1,0:T(8,128)(2,1)S(1)}, bf16[16,16,128]{2,1,0:T(8,128)(2,1)S(1)}, u32[]{:S(2)}, u32[]{:S(2)}) collective-permute-start(bf16[16,16,128]{2,1,0:T(8,128)(2,1)S(1)} %slice.21), channel_id=1, source_target_pairs={{0,0},{1,16},{2,32},{3,48},{4,64},{5,80},{6,96},{7,112},{8,128},{9... | collective-permute-start | bytes 196616 | tf_op jit(solution)/shard_map/ppermute | solution.py:501
  91.4 2.8 %shard_map.173.mapped_ref = bf16[16,1024,256]{2,1,0:T(8,128)(2,1)S(1)} custom-call(bf16[16,32,128]{2,1,0:T(8,128)(2,1)S(1)} %all_to_all.16.sides_ref, bf16[128,4096]{1,0:T(8,128)(2,1)S(1)} %get-tuple-element.31.mapping_ref), custom_call_target="tpu_custom_call" | custom-call | flops 4294967296 | bytes 20971520 | tf_op jit(solution)/shard_map/pallas_call | solution.py:513
  94.2 0.8 shard_map.172.factors_ref
  95.0 6.7 %collective-permute-done.13.band_ref = bf16[16,16,128]{2,1,0:T(8,128)(2,1)S(1)} collective-permute-done((bf16[16,16,128]{2,1,0:T(8,128)(2,1)S(1)}, bf16[16,16,128]{2,1,0:T(8,128)(2,1)S(1)}, u32[]{:S(2)}, u32[]{:S(2)}) %collective-permute-start.13) | collective-permute-done | bytes 65568 | tf_op jit(solution)/shard_map/ppermute | solution.py:501
  101.7 4.5 %shard_map.174 = bf16[32,256,128]{2,1,0:T(8,128)(2,1)} custom-call(s32[32]{0:T(128)S(1)} %copy-done.8, s32[256]{0:T(256)S(1)} %copy-done.7, bf16[256,1024]{1,0:T(8,128)(2,1)S(1)} %shard_map.172.factors_ref, bf16[16,16,128]{2,1,0:T(8,128)(2,1)S(1)} %collective-permute-done.13.band_ref, bf16[16,1024,256]{2,1,0:T(8,128)(2,1)S(1)} %shard_map.173.mapped_ref, ...), custom_call_target="tpu_custom_call" | custom-call | tf_op jit(solution)/shard_map/pallas_call | solution.py:523
  (44 shorter events, 0.9 us)
Async XLA Ops:
  0.6 23.4 %copy-start.1 = (bf16[2,256,256]{2,1,0:T(8,128)(2,1)S(1)}, bf16[2,256,256]{2,1,0:T(8,128)(2,1)}, u32[]{:S(2)}) copy-start(bf16[2,256,256]{2,1,0:T(8,128)(2,1)} %param.16) | copy-start | bytes 786436
  0.6 23.4 %copy-start.2 = (bf16[1024,128]{1,0:T(8,128)(2,1)S(1)}, bf16[1024,128]{1,0:T(8,128)(2,1)}, u32[]{:S(2)}) copy-start(bf16[1024,128]{1,0:T(8,128)(2,1)} %map_ref.1) | copy-start | bytes 786436
  0.7 23.4 %copy-start.3 = (bf16[256,256]{1,0:T(8,128)(2,1)S(1)}, bf16[256,256]{1,0:T(8,128)(2,1)}, u32[]{:S(2)}) copy-start(bf16[256,256]{1,0:T(8,128)(2,1)} %sig_ref.1) | copy-start | bytes 393220
  0.7 23.4 %copy-start.7 = (s32[256]{0:T(256)S(1)}, s32[256]{0:T(256)}, u32[]{:S(2)}) copy-start(s32[256]{0:T(256)} %flags_ref.1) | copy-start | bytes 3076
  0.7 23.4 %copy-start.8 = (s32[32]{0:T(128)S(1)}, s32[32]{0:T(128)}, u32[]{:S(2)}) copy-start(s32[32]{0:T(128)} %live_ref.5) | copy-start | bytes 388
  0.7 23.4 %copy-start.9 = (f32[256]{0:T(256)S(1)}, f32[256]{0:T(256)}, u32[]{:S(2)}) copy-start(f32[256]{0:T(256)} %param.20) | copy-start | bytes 3076
  6.7 22.1 %all-to-all-start = ((bf16[8,176,256]{2,1,0:T(8,128)(2,1)}), bf16[8,176,256]{2,1,0:T(8,128)(2,1)S(1)}, u32[]{:S(2)}, u32[]{:S(2)}) async-start(bf16[8,176,256]{2,1,0:T(8,128)(2,1)} %get-tuple-element.17), calls=%async_computation | async-start | bytes 1441792 | tf_op jit(solution)/shard_map/all_to_all | solution.py:442
  13.9 14.8 %collective-permute-start = (bf16[2,32,256]{2,1,0:T(8,128)(2,1)}, bf16[2,32,256]{2,1,0:T(8,128)(2,1)S(1)}, u32[]{:S(2)}, u32[]{:S(2)}) collective-permute-start(bf16[2,32,256]{2,1,0:T(8,128)(2,1)} %get-tuple-element.18), channel_id=1, source_target_pairs={{0,0},{1,16},{2,32},{3,48},{4,64},{5,80},{6,96},{7,112},{8,128},{9... | collective-permute-start | bytes 98312 | tf_op jit(solution)/shard_map/ppermute | solution.py:443
  28.8 23.9 %collective-permute-start.6 = (bf16[8,144,256]{2,1,0:T(8,128)(2,1)S(1)}, bf16[8,144,256]{2,1,0:T(8,128)(2,1)S(1)}, u32[]{:S(2)}, u32[]{:S(2)}) collective-permute-start(bf16[8,144,256]{2,1,0:T(8,128)(2,1)S(1)} %slice.18), channel_id=1, source_target_pairs={{0,16},{1,0},{16,17},{17,1},{2,18},{3,2},{18,19},{19,3},{4,20},{5,... | collective-permute-start | bytes 1769480 | tf_op jit(solution)/shard_map/ppermute | solution.py:461
  28.9 23.8 %collective-permute-start.5 = (bf16[8,144,256]{2,1,0:T(8,128)(2,1)S(1)}, bf16[8,144,256]{2,1,0:T(8,128)(2,1)S(1)}, u32[]{:S(2)}, u32[]{:S(2)}) collective-permute-start(bf16[8,144,256]{2,1,0:T(8,128)(2,1)S(1)} %slice.18), channel_id=1, source_target_pairs={{0,0},{1,16},{16,1},{17,17},{2,2},{3,18},{18,3},{19,19},{4,4},{5,2... | collective-permute-start | bytes 1769480 | tf_op jit(solution)/shard_map/ppermute | solution.py:460
  29.6 5.0 %collective-permute-start.1 = (bf16[8,32,256]{2,1,0:T(8,128)(2,1)S(1)}, bf16[8,32,256]{2,1,0:T(8,128)(2,1)S(1)}, u32[]{:S(2)}, u32[]{:S(2)}) collective-permute-start(bf16[8,32,256]{2,1,0:T(8,128)(2,1)S(1)} %slice.17.refs_0_), channel_id=1, source_target_pairs={{0,2},{2,4},{4,6},{6,8},{8,10},{10,12},{12,14},{14,0},{16,30},{18,... | collective-permute-start | bytes 393224 | tf_op jit(solution)/shard_map/ppermute | solution.py:466
  29.7 5.9 %collective-permute-start.8 = (bf16[8,32,256]{2,1,0:T(8,128)(2,1)S(1)}, bf16[8,32,256]{2,1,0:T(8,128)(2,1)S(1)}, u32[]{:S(2)}, u32[]{:S(2)}) collective-permute-start(bf16[8,32,256]{2,1,0:T(8,128)(2,1)S(1)} %slice.17.refs_0_), channel_id=1, source_target_pairs={{0,14},{2,0},{4,2},{6,4},{8,6},{10,8},{12,10},{14,12},{16,18},{18,... | collective-permute-start | bytes 393224 | tf_op jit(solution)/shard_map/ppermute | solution.py:468
  34.7 6.3 %collective-permute-start.2 = (bf16[8,32,256]{2,1,0:T(8,128)(2,1)S(1)}, bf16[8,32,256]{2,1,0:T(8,128)(2,1)S(1)}, u32[]{:S(2)}, u32[]{:S(2)}) collective-permute-start(bf16[8,32,256]{2,1,0:T(8,128)(2,1)S(1)} %collective-permute-done.1.refs_1_), channel_id=1, source_target_pairs={{0,2},{2,4},{4,6},{6,8},{8,10},{10,12},{12,14},{14,0},{16,30},{18,... | collective-permute-start | bytes 393224 | tf_op jit(solution)/shard_map/ppermute | solution.py:466
  35.6 10.1 %collective-permute-start.9 = (bf16[8,32,256]{2,1,0:T(8,128)(2,1)S(1)}, bf16[8,32,256]{2,1,0:T(8,128)(2,1)S(1)}, u32[]{:S(2)}, u32[]{:S(2)}) collective-permute-start(bf16[8,32,256]{2,1,0:T(8,128)(2,1)S(1)} %collective-permute-done.8.refs_2_), channel_id=1, source_target_pairs={{0,14},{2,0},{4,2},{6,4},{8,6},{10,8},{12,10},{14,12},{16,18},{18,... | collective-permute-start | bytes 393224 | tf_op jit(solution)/shard_map/ppermute | solution.py:468
  41.0 7.7 %collective-permute-start.3 = (bf16[8,32,256]{2,1,0:T(8,128)(2,1)S(1)}, bf16[8,32,256]{2,1,0:T(8,128)(2,1)S(1)}, u32[]{:S(2)}, u32[]{:S(2)}) collective-permute-start(bf16[8,32,256]{2,1,0:T(8,128)(2,1)S(1)} %collective-permute-done.2.refs_3_), channel_id=1, source_target_pairs={{0,2},{2,4},{4,6},{6,8},{8,10},{10,12},{12,14},{14,0},{16,30},{18,... | collective-permute-start | bytes 393224 | tf_op jit(solution)/shard_map/ppermute | solution.py:466
  41.0 7.7 %collective-permute-start.4 = (bf16[8,16,128]{2,1,0:T(8,128)(2,1)S(1)}, bf16[8,16,128]{2,1,0:T(8,128)(2,1)S(1)}, u32[]{:S(2)}, u32[]{:S(2)}) collective-permute-start(bf16[8,16,128]{2,1,0:T(8,128)(2,1)S(1)} %slice.16.own_ref), channel_id=1, source_target_pairs={{0,1},{1,0},{2,3},{3,2},{4,5},{5,4},{6,7},{7,6},{8,9},{9,8},{10,11... | collective-permute-start | bytes 98312 | tf_op jit(solution)/shard_map/ppermute | solution.py:462
  45.7 7.0 %collective-permute-start.10 = (bf16[8,32,256]{2,1,0:T(8,128)(2,1)S(1)}, bf16[8,32,256]{2,1,0:T(8,128)(2,1)S(1)}, u32[]{:S(2)}, u32[]{:S(2)}) collective-permute-start(bf16[8,32,256]{2,1,0:T(8,128)(2,1)S(1)} %collective-permute-done.9.refs_4_), channel_id=1, source_target_pairs={{0,14},{2,0},{4,2},{6,4},{8,6},{10,8},{12,10},{14,12},{16,18},{18,... | collective-permute-start | bytes 393224 | tf_op jit(solution)/shard_map/ppermute | solution.py:468
  48.6 7.5 %collective-permute-start.7 = (bf16[8,32,256]{2,1,0:T(8,128)(2,1)S(1)}, bf16[8,32,256]{2,1,0:T(8,128)(2,1)S(1)}, u32[]{:S(2)}, u32[]{:S(2)}) collective-permute-start(bf16[8,32,256]{2,1,0:T(8,128)(2,1)S(1)} %collective-permute-done.3.refs_5_), channel_id=1, source_target_pairs={{0,2},{2,4},{4,6},{6,8},{8,10},{10,12},{12,14},{14,0},{16,30},{18,... | collective-permute-start | bytes 393224 | tf_op jit(solution)/shard_map/ppermute | solution.py:466
  48.7 7.4 %collective-permute-start.11 = (bf16[2,32,256]{2,1,0:T(8,128)(2,1)S(1)}, bf16[2,32,256]{2,1,0:T(8,128)(2,1)S(1)}, u32[]{:S(2)}, u32[]{:S(2)}) collective-permute-start(bf16[2,32,256]{2,1,0:T(8,128)(2,1)S(1)} %collective-permute-done.refs_2_), channel_id=1, source_target_pairs={{0,1},{1,0},{2,3},{3,2},{4,5},{5,4},{6,7},{7,6},{8,9},{9,8},{10,11... | collective-permute-start | bytes 98312 | tf_op jit(solution)/shard_map/ppermute | solution.py:463
  56.0 14.5 %copy-start.4 = (bf16[256,256]{1,0:T(8,128)(2,1)S(1)}, bf16[256,256]{1,0:T(8,128)(2,1)}, u32[]{:S(2)}) copy-start(bf16[256,256]{1,0:T(8,128)(2,1)} %final_ref.1) | copy-start | bytes 393220
  56.0 14.5 %copy-start.5 = (bf16[256,32]{0,1:T(8,128)(2,1)S(1)}, bf16[256,32]{0,1:T(8,128)(2,1)}, u32[]{:S(2)}) copy-start(bf16[256,32]{0,1:T(8,128)(2,1)} %param.30) | copy-start | bytes 49156
  56.1 14.5 %copy-start.6 = (bf16[256,32]{0,1:T(8,128)(2,1)S(1)}, bf16[256,32]{0,1:T(8,128)(2,1)}, u32[]{:S(2)}) copy-start(bf16[256,32]{0,1:T(8,128)(2,1)} %param.29) | copy-start | bytes 49156
  86.8 14.9 %collective-permute-start.13 = (bf16[16,16,128]{2,1,0:T(8,128)(2,1)S(1)}, bf16[16,16,128]{2,1,0:T(8,128)(2,1)S(1)}, u32[]{:S(2)}, u32[]{:S(2)}) collective-permute-start(bf16[16,16,128]{2,1,0:T(8,128)(2,1)S(1)} %slice.21), channel_id=1, source_target_pairs={{0,0},{1,16},{2,32},{3,48},{4,64},{5,80},{6,96},{7,112},{8,128},{9... | collective-permute-start | bytes 196616 | tf_op jit(solution)/shard_map/ppermute | solution.py:501
  91.3 3.0 %collective-permute-start.12 = (bf16[16,32,256]{2,1,0:T(8,128)(2,1)S(1)}, bf16[16,32,256]{2,1,0:T(8,128)(2,1)S(1)}, u32[]{:S(2)}, u32[]{:S(2)}) collective-permute-start(bf16[16,32,256]{2,1,0:T(8,128)(2,1)S(1)} %slice.19), channel_id=1, source_target_pairs={{0,16},{16,0},{1,17},{17,1},{2,18},{18,2},{3,19},{19,3},{4,20},{20... | collective-permute-start | bytes 786440 | tf_op jit(solution)/shard_map/ppermute | solution.py:503
  (2 other events, 24.8 us)
